TPU v7x, 32 devices: a whole 2x2x4 slice. The times are simulated.
32 devices in a mesh: section: 2 (over x), tensor: 2 (over y), dp: 8 (over z, core).
Axes of the slice: x: 2, y: 2, z: 4, core: 2. Of those that a mesh axis runs over, the one named last changes fastest.
Arguments:
- inputs: bfloat16 [2, 8, 128, 768], P(None, 'dp'), may hold values from -6 to 6
- cotangent: bfloat16 [2, 8, 128, 768], P(None, 'dp'), may hold values from -6 to 6
- ln1_gain: bfloat16 [2, 768], P('section'), may hold values from 0.25 to 1.75
- ln1_bias: bfloat16 [2, 768], P('section'), may hold values from -4 to 4
- ln2_gain: bfloat16 [2, 768], P('section'), may hold values from 0.25 to 1.75
- ln2_bias: bfloat16 [2, 768], P('section'), may hold values from -4 to 4
- w_qkv: bfloat16 [2, 768, 3, 768], P('section', None, None, 'tensor'), may hold values from -0.21875 to 0.21875
- b_qkv: bfloat16 [2, 3, 768], P('section', None, 'tensor'), may hold values from -4 to 4
- w_out: bfloat16 [2, 768, 768], P('section', 'tensor'), may hold values from -1.25 to 1.25
- b_out: bfloat16 [2, 768], P('section'), may hold values from -4 to 4
- w_up: bfloat16 [2, 768, 3072], P('section', None, 'tensor'), may hold values from -0.21875 to 0.21875
- b_up: bfloat16 [2, 3072], P('section', 'tensor'), may hold values from -4 to 4
- w_down: bfloat16 [2, 3072, 768], P('section', 'tensor'), may hold values from -0.15625 to 0.15625
- b_down: bfloat16 [2, 768], P('section'), may hold values from -4 to 4
Outputs:
- section_out: bfloat16 [2, 2, 8, 128, 768], P('section', None, 'dp')
- input_grad: float32 [2, 2, 8, 128, 768], P('section', None, 'dp')
- grad_ln1_gain: float32 [2, 768], P('section', ('tensor', 'dp'))
- grad_ln1_bias: float32 [2, 768], P('section', ('tensor', 'dp'))
- grad_ln2_gain: float32 [2, 768], P('section', ('tensor', 'dp'))
- grad_ln2_bias: float32 [2, 768], P('section', ('tensor', 'dp'))
- grad_w_qkv: float32 [2, 768, 3, 768], P('section', 'dp', None, 'tensor')
- grad_b_qkv: float32 [2, 3, 768], P('section', None, ('tensor', 'dp'))
- grad_w_out: float32 [2, 768, 768], P('section', ('tensor', 'dp'))
- grad_b_out: float32 [2, 768], P('section', ('tensor', 'dp'))
- grad_w_up: float32 [2, 768, 3072], P('section', 'dp', 'tensor')
- grad_b_up: float32 [2, 3072], P('section', ('tensor', 'dp'))
- grad_w_down: float32 [2, 3072, 768], P('section', ('tensor', 'dp'))
- grad_b_down: float32 [2, 768], P('section', ('tensor', 'dp'))
All inputs are finite; a program needn't handle non-finite values.
Results may differ from a plain program's by a relative error of at most 0.019.
Values may be sent and summed in bfloat16 or wider, within the bound.
No kernel may reach another device: no remote copies, remote signals or barrier semaphores. Data moves between devices by JAX's collectives and lax.ppermute only.
A program may use at most 128 MiB of HBM per device.

v0:
```python
import functools
import math

import jax
import jax.numpy as jnp
import numpy as np
from jax import lax
from jax.experimental import pallas as pl
from jax.experimental.pallas import tpu as pltpu
from jax.sharding import PartitionSpec as P

HEAD = 64
ROT = 16
LANES = 128
EPSILON = 1e-05
BF = jnp.bfloat16
F32 = jnp.float32
VMEM_LIMIT = 48 * 2**20


def rope_tables(length):
    half = ROT // 2
    inverse = np.exp(-math.log(10000.0) * np.arange(half, dtype=np.float32) * np.float32(2.0) / ROT)
    angle = np.arange(length, dtype=np.float32)[:, None] * inverse[None, :].astype(np.float32)
    cosine, sine = np.cos(angle), np.sin(angle)
    table = np.zeros((3, length, LANES), np.float32)
    table[0] = 1.0
    for head in range(LANES // HEAD):
        at = head * HEAD
        table[0, :, at : at + half] = cosine
        table[0, :, at + half : at + ROT] = cosine
        table[1, :, at : at + half] = -sine
        table[2, :, at + half : at + ROT] = sine
    return table


def dot(a, b):
    return jnp.dot(a, b, preferred_element_type=F32)


def dot_nt(a, b):
    return lax.dot_general(a, b, (((1,), (1,)), ((), ())), preferred_element_type=F32)


def dot_tn(a, b):
    return lax.dot_general(a, b, (((0,), (0,)), ((), ())), preferred_element_type=F32)


def roped(value, table, sign):
    half = ROT // 2
    ahead = pltpu.roll(value, LANES - half, 1) * table[1]
    behind = pltpu.roll(value, half, 1) * table[2]
    return value * table[0] + sign * (ahead + behind)


def head_pair(value):
    low = lax.broadcasted_iota(jnp.int32, value.shape, 1) < HEAD
    zero = jnp.zeros_like(value)
    return jnp.concatenate([jnp.where(low, value, zero), jnp.where(low, zero, value)], axis=0)


def pair_merge(value):
    rows = value.shape[0] // 2
    low = lax.broadcasted_iota(jnp.int32, (rows, LANES), 1) < HEAD
    return jnp.where(low, value[:rows], value[rows:])


def normal(block):
    width = block.shape[1]
    center = block - jnp.sum(block, axis=1, keepdims=True) * (1.0 / width)
    spread = jnp.sum(center * center, axis=1, keepdims=True) * (1.0 / width)
    scale = lax.rsqrt(spread + EPSILON)
    return center * scale, scale


def forward_part(x, vec, table, w, wait, put):
    rows, width = x.shape
    unit, unused = normal(x.astype(F32))
    first = (unit * vec["g1"] + vec["b1"]).astype(BF)
    second = (unit * vec["g2"] + vec["b2"]).astype(BF)
    put("a1", first)
    put("a2", second)
    wait("wqkv")
    bqkv = vec["bqkv"]
    raw = [dot(first, w["wqkv"][j]) + bqkv[j : j + 1] for j in range(3)]
    local = raw[0].shape[1]
    row = lax.broadcasted_iota(jnp.int32, (rows, rows), 0)
    keep = row >= lax.broadcasted_iota(jnp.int32, (rows, rows), 1)
    for p in range(local // LANES):
        sl = slice(p * LANES, (p + 1) * LANES)
        q = roped(raw[0][:, sl], table, 1.0).astype(BF)
        k = roped(raw[1][:, sl], table, 1.0).astype(BF)
        v = raw[2][:, sl].astype(BF)
        put("q", q, sl)
        put("k", k, sl)
        put("v", v, sl)
        scores = dot_nt(q, head_pair(k)) * HEAD**-0.5
        prob = []
        for h in range(2):
            part = jnp.where(keep, scores[:, h * rows : (h + 1) * rows], -1e30)
            expo = jnp.exp(part - jnp.max(part, axis=1, keepdims=True))
            prob.append(expo * (1.0 / jnp.sum(expo, axis=1, keepdims=True)))
        prob = jnp.concatenate(prob, axis=1)
        put("prob", prob, slice(p * 2 * rows, (p + 1) * 2 * rows))
        put("mixed", dot(prob.astype(BF), head_pair(v)).astype(BF), sl)
    wait("wup")
    hidden = w["wup"].shape[1]
    step = 256
    for c in range(0, hidden, step):
        sl = slice(c, c + step)
        u = dot(second, w["wup"][:, sl]) + vec["bup"][:, sl]
        phi = 0.5 + 0.5 * lax.erf(u * (2.0**-0.5))
        put("g", (u * phi).astype(BF), sl)
        put("gp", lambda: phi + u * (jnp.exp(-0.5 * u * u) * (2.0 * math.pi) ** -0.5), sl)


def output_part(mixed, active, vec, w, wait, owner):
    wait("wout")
    total = dot(mixed[...], w["wout"][...])
    wait("wdown")
    total = total + dot(active[...], w["wdown"][...])
    extra = vec["bout"] + vec["bdown"]
    return (total + jnp.where(owner == 0, extra, jnp.zeros_like(extra))).astype(BF)


def backward_part(x, dy, saved, vec, table, w, wait, put):
    rows, width = x.shape
    hidden = w["wdown"].shape[0]
    step = 256
    wait("wdown")
    for c in range(0, hidden, step):
        sl = slice(c, c + step)
        du = (dot_nt(dy, w["wdown"][sl, :]) * saved["gp"][:, sl].astype(F32)).astype(BF)
        put("du", du, sl)
    wait("wout")
    d_mixed = dot_nt(dy, w["wout"][...]).astype(BF)
    local = d_mixed.shape[1]
    for p in range(local // LANES):
        sl = slice(p * LANES, (p + 1) * LANES)
        q, k, v = saved["q"][:, sl], saved["k"][:, sl], saved["v"][:, sl]
        prob = saved["prob"][:, p * 2 * rows : (p + 1) * 2 * rows]
        d_tile = d_mixed[:, sl]
        d_prob = dot_nt(d_tile, head_pair(v))
        d_value = pair_merge(dot_tn(prob.astype(BF), d_tile))
        d_scores = []
        for h in range(2):
            part = prob[:, h * rows : (h + 1) * rows]
            d_part = d_prob[:, h * rows : (h + 1) * rows]
            both = part * d_part
            d_scores.append(both - part * jnp.sum(both, axis=1, keepdims=True))
        d_scores = jnp.concatenate(d_scores, axis=1).astype(BF)
        scale = HEAD**-0.5
        d_query = dot(d_scores, head_pair(k)) * scale
        d_keys = pair_merge(dot_tn(d_scores, q)) * scale
        put("dqkv", roped(d_query, table, -1.0).astype(BF), slice(p * LANES, (p + 1) * LANES))
        at = local + p * LANES
        put("dqkv", roped(d_keys, table, -1.0).astype(BF), slice(at, at + LANES))
        at = 2 * local + p * LANES
        put("dqkv", d_value.astype(BF), slice(at, at + LANES))
    return local


def norm_back(x, du, dqkv, local, vec, w, wait):
    wait("wup")
    d_second = dot_nt(du[...], w["wup"][...])
    wait("wqkv")
    d_first = dot_nt(dqkv[:, :local], w["wqkv"][0])
    for j in range(1, 3):
        d_first = d_first + dot_nt(dqkv[:, j * local : (j + 1) * local], w["wqkv"][j])
    unit, scale = normal(x.astype(F32))
    e = d_first * vec["g1"] + d_second * vec["g2"]
    width = x.shape[1]
    mean = jnp.sum(e, axis=1, keepdims=True) * (1.0 / width)
    along = jnp.sum(e * unit, axis=1, keepdims=True) * (1.0 / width)
    dx = (e - mean - unit * along) * scale
    return dx.astype(BF), d_first, d_second, unit


WEIGHTS = ("wqkv", "wout", "wup", "wdown")
VECTORS = ("g1", "b1", "g2", "b2", "bqkv", "bout", "bup", "bdown")


def start_weights(hbm, scratch, sems):
    waited = set()
    copies = {}
    order = {name: i for i, name in enumerate(WEIGHTS)}
    for name in hbm:
        copies[name] = pltpu.make_async_copy(hbm[name], scratch[name], sems.at[order[name]])

    def start(names):
        for name in names:
            copies[name].start()

    def wait(name):
        if name not in waited:
            waited.add(name)
            copies[name].wait()

    return start, wait


def f_kernel(*refs):
    x_ref, owner_ref, table_ref = refs[:3]
    vec = {n: r[...].astype(F32) for n, r in zip(VECTORS, refs[3:11])}
    hbm = dict(zip(WEIGHTS, refs[11:15]))
    out_ref = refs[15]
    w = dict(zip(WEIGHTS, refs[16:20]))
    mixed, active, sems = refs[20:]
    start, wait = start_weights(hbm, w, sems)
    start(("wqkv", "wup", "wout", "wdown"))

    def put(name, value, sl=slice(None)):
        if name == "mixed":
            mixed[:, sl] = value
        if name == "g":
            active[:, sl] = value

    forward_part(x_ref[...], vec, table_ref, w, wait, put)
    out_ref[...] = output_part(mixed, active, vec, w, wait, owner_ref[0])


SAVED = ("a1", "a2", "q", "k", "v", "prob", "mixed", "g", "gp")


def fb_kernel(*refs):
    x_ref, dy_ref, owner_ref, table_ref = refs[:4]
    vec = {n: r[...].astype(F32) for n, r in zip(VECTORS, refs[4:12])}
    hbm = dict(zip(WEIGHTS, refs[12:16]))
    out_ref, dx_ref = refs[16:18]
    saved = dict(zip(SAVED, refs[18:27]))
    w = dict(zip(WEIGHTS, refs[27:31]))
    du, dqkv, sems = refs[31:]
    start, wait = start_weights(hbm, w, sems)
    start(("wqkv", "wup", "wdown", "wout"))
    saved_too = dict(saved, du=du, dqkv=dqkv)

    def put(name, value, sl=slice(None)):
        ref = saved_too[name]
        value = value() if callable(value) else value
        ref[:, sl] = value.astype(ref.dtype)

    x = x_ref[...]
    forward_part(x, vec, table_ref, w, wait, put)
    local = backward_part(x, dy_ref[...], saved, vec, table_ref, w, wait, put)
    dx_ref[...] = norm_back(x, du, dqkv, local, vec, w, wait)[0]
    out_ref[...] = output_part(saved["mixed"], saved["g"], vec, w, wait, owner_ref[0])


def b_kernel(*refs):
    x_ref, dy_ref, table_ref = refs[:3]
    vec = {n: r[...].astype(F32) for n, r in zip(("g1", "g2"), refs[3:5])}
    hbm = dict(zip(WEIGHTS, refs[5:9]))
    saved = dict(zip(("q", "k", "v", "prob", "gp"), refs[9:14]))
    dx_ref, du, dqkv, sum_d, sum_up, sum_qkv = refs[14:20]
    w = dict(zip(WEIGHTS, refs[20:24]))
    sems = refs[24]
    start, wait = start_weights(hbm, w, sems)
    start(("wdown", "wout", "wup", "wqkv"))
    kept = {"du": du, "dqkv": dqkv}

    def put(name, value, sl=slice(None)):
        kept[name][:, sl] = value

    x = x_ref[...]
    dy = dy_ref[...]
    local = backward_part(x, dy, saved, vec, table_ref, w, wait, put)
    dx, d_first, d_second, unit = norm_back(x, du, dqkv, local, vec, w, wait)
    dx_ref[...] = dx

    def total(value):
        return jnp.sum(value, axis=0, keepdims=True)

    sum_d[0:1] = total(d_first * unit)
    sum_d[1:2] = total(d_first)
    sum_d[2:3] = total(d_second * unit)
    sum_d[3:4] = total(d_second)
    sum_d[4:5] = total(dy.astype(F32)) * 0.5
    sum_up[...] = total(du[...].astype(F32))
    sum_qkv[...] = total(dqkv[...].astype(F32))


VM = pl.BlockSpec(memory_space=pltpu.VMEM)
SM = pl.BlockSpec(memory_space=pltpu.SMEM)
ANY = pl.BlockSpec(memory_space=pl.ANY)


def weight_scratch(ws):
    return [pltpu.VMEM(a.shape, a.dtype) for a in ws]


def cost(ws, rows, passes):
    size = sum(math.prod(a.shape) for a in ws)
    return pl.CostEstimate(flops=2 * size * rows * passes, bytes_accessed=2 * size, transcendentals=0)


def call_f(x, owner, table, vecs, ws):
    rows, width = x.shape
    local, hidden = ws[1].shape[0], ws[3].shape[0]
    return pl.pallas_call(
        f_kernel,
        out_shape=jax.ShapeDtypeStruct((rows, width), BF),
        in_specs=[VM, SM, VM] + [VM] * 8 + [ANY] * 4,
        out_specs=VM,
        scratch_shapes=weight_scratch(ws)
        + [pltpu.VMEM((rows, local), BF), pltpu.VMEM((rows, hidden), BF), pltpu.SemaphoreType.DMA((4,))],
        compiler_params=pltpu.CompilerParams(vmem_limit_bytes=VMEM_LIMIT),
        cost_estimate=cost(ws, rows, 1),
    )(x, owner, table, *vecs, *ws)


def call_fb(x, dy, owner, table, vecs, ws):
    rows, width = x.shape
    local, hidden = ws[1].shape[0], ws[3].shape[0]
    shape = jax.ShapeDtypeStruct
    outs = [
        shape((rows, width), BF),
        shape((rows, width), BF),
        shape((rows, width), BF),
        shape((rows, width), BF),
        shape((rows, local), BF),
        shape((rows, local), BF),
        shape((rows, local), BF),
        shape((rows, 2 * rows * local // LANES), F32),
        shape((rows, local), BF),
        shape((rows, hidden), BF),
        shape((rows, hidden), F32),
    ]
    return pl.pallas_call(
        fb_kernel,
        out_shape=outs,
        in_specs=[VM, VM, SM, VM] + [VM] * 8 + [ANY] * 4,
        out_specs=[VM] * len(outs),
        scratch_shapes=weight_scratch(ws)
        + [pltpu.VMEM((rows, hidden), BF), pltpu.VMEM((rows, 3 * local), BF), pltpu.SemaphoreType.DMA((4,))],
        compiler_params=pltpu.CompilerParams(vmem_limit_bytes=VMEM_LIMIT),
        cost_estimate=cost(ws, rows, 2),
    )(x, dy, owner, table, *vecs, *ws)


def call_b(x, dy, table, gains, ws, saved):
    rows, width = x.shape
    local, hidden = ws[1].shape[0], ws[3].shape[0]
    shape = jax.ShapeDtypeStruct
    outs = [
        shape((rows, width), BF),
        shape((rows, hidden), BF),
        shape((rows, 3 * local), BF),
        shape((5, width), F32),
        shape((1, hidden), F32),
        shape((1, 3 * local), F32),
    ]
    return pl.pallas_call(
        b_kernel,
        out_shape=outs,
        in_specs=[VM] * 3 + [VM] * 2 + [ANY] * 4 + [VM] * 5,
        out_specs=[VM] * len(outs),
        scratch_shapes=weight_scratch(ws) + [pltpu.SemaphoreType.DMA((4,))],
        compiler_params=pltpu.CompilerParams(vmem_limit_bytes=VMEM_LIMIT),
        cost_estimate=cost(ws, rows, 1),
    )(x, dy, table, *gains, *ws, *saved)


def swap(value):
    return lax.ppermute(value, "tensor", [(0, 1), (1, 0)])


def per_device(inputs, cotangent, g1, b1, g2, b2, w_qkv, b_qkv, w_out, b_out, w_up, b_up, w_down, b_down):
    section = lax.axis_index("section")
    owner_at = lax.axis_index("tensor")
    dp_at = lax.axis_index("dp")
    parts = lax.axis_size("dp")
    tensors = lax.axis_size("tensor")
    micro, seqs, length, width = inputs.shape
    rows = seqs * length
    local, hidden = w_out.shape[1], w_up.shape[2]
    owner = owner_at.astype(jnp.int32).reshape(1)
    table = jnp.asarray(rope_tables(length))
    vecs = (g1, b1, g2, b2, b_qkv[0], b_out, b_up, b_down)
    ws = (w_qkv[0].transpose(1, 0, 2), w_out[0], w_up[0], w_down[0])
    xs = inputs.reshape(micro, rows, width)
    cots = cotangent.reshape(micro, rows, width)

    sources = []
    for m in range(micro):
        part = call_f(xs[m], owner, table, vecs, ws)
        other = swap(part)
        whole = (xs[m].astype(F32) + (part.astype(F32) + other.astype(F32))).astype(BF)
        arrived = lax.ppermute(whole, "section", [(0, 1)])
        sources.append(jnp.where(section == 0, xs[m], arrived))
    kept, ups, produced = [], [], []
    for m in range(micro):
        part, dx, *saved = call_fb(sources[m], cots[m], owner, table, vecs, ws)
        other = swap(dx)
        whole = (cots[m].astype(F32) + (dx.astype(F32) + other.astype(F32))).astype(BF)
        arrived = lax.ppermute(whole, "section", [(1, 0)])
        ups.append(jnp.where(section == 1, cots[m], arrived))
        kept.append(dict(zip(SAVED, saved)))
        produced.append(part)
    grads, dus, dqkvs, sums = [], [], [], []
    for m in range(micro):
        saved = [kept[m][n] for n in ("q", "k", "v", "prob", "gp")]
        dx, du, dqkv, sum_d, sum_up, sum_qkv = call_b(sources[m], ups[m], table, (g1, g2), ws, saved)
        grads.append(dx)
        dus.append(du)
        dqkvs.append(dqkv)
        sums.append((sum_d, sum_up, sum_qkv))
    input_grad = []
    section_out = []
    for m in range(micro):
        dx, part = grads[m], produced[m]
        input_grad.append(ups[m].astype(F32) + (dx.astype(F32) + swap(dx).astype(F32)))
        whole = sources[m].astype(F32) + (part.astype(F32) + swap(part).astype(F32))
        section_out.append(whole.astype(BF))
    input_grad = jnp.stack(input_grad).reshape(1, micro, seqs, length, width)
    section_out = jnp.stack(section_out).reshape(1, micro, seqs, length, width)

    def rowed(pieces):
        return jnp.concatenate(pieces, axis=0)

    all_up = rowed(ups)
    all_du, all_dqkv = rowed(dus), rowed(dqkvs)
    a1, a2, mixed, active = (rowed([kept[m][n] for m in range(micro)]) for n in ("a1", "a2", "mixed", "g"))

    def outer(a, b):
        return jnp.einsum("ta,tb->ab", a, b, preferred_element_type=F32).astype(BF)

    def scatter(value):
        return lax.psum_scatter(value, "dp", scatter_dimension=0, tiled=True).astype(F32)

    d_wdown = scatter(outer(active, all_up))
    d_wout = scatter(outer(mixed, all_up))
    d_wup = scatter(outer(a2, all_du))
    d_wqkv = scatter(outer(a1, all_dqkv)).reshape(-1, 3, local)
    sum_d = sum(s[0] for s in sums)
    sum_up = sum(s[1] for s in sums)
    sum_qkv = sum(s[2] for s in sums).reshape(3, local)
    mine = jnp.concatenate([sum_up.reshape(-1), sum_qkv.reshape(-1)])
    flat = jnp.zeros((tensors, mine.shape[0]), F32)
    flat = lax.dynamic_update_slice(flat, mine[None], (owner_at, 0)).reshape(-1)
    total = lax.psum(jnp.concatenate([sum_d.reshape(-1), flat]), ("tensor", "dp"))
    total_d = total[: 5 * width].reshape(5, width)
    mine = lax.dynamic_slice_in_dim(total[5 * width :].reshape(tensors, -1), owner_at, 1, 0).reshape(-1)
    share = width // (tensors * parts)
    d_vec = lax.dynamic_slice_in_dim(total_d, (owner_at * parts + dp_at) * share, share, 1)
    up_share, qkv_share = hidden // parts, local // parts
    d_bup = lax.dynamic_slice_in_dim(mine[:hidden], dp_at * up_share, up_share, 0)
    d_bqkv = lax.dynamic_slice_in_dim(mine[hidden:].reshape(3, local), dp_at * qkv_share, qkv_share, 1)
    return (
        section_out,
        input_grad,
        d_vec[0:1],
        d_vec[1:2],
        d_vec[2:3],
        d_vec[3:4],
        d_wqkv[None],
        d_bqkv[None],
        d_wout[None],
        d_vec[4:5],
        d_wup[None],
        d_bup[None],
        d_wdown[None],
        d_vec[4:5],
    )


def solution(mesh):
    return jax.shard_map(
        per_device,
        mesh=mesh,
        in_specs=(
            P(None, "dp", None, None),
            P(None, "dp", None, None),
            P("section", None),
            P("section", None),
            P("section", None),
            P("section", None),
            P("section", None, None, "tensor"),
            P("section", None, "tensor"),
            P("section", "tensor", None),
            P("section", None),
            P("section", None, "tensor"),
            P("section", "tensor"),
            P("section", "tensor", None),
            P("section", None),
        ),
        out_specs=(
            P("section", None, "dp", None, None),
            P("section", None, "dp", None, None),
            P("section", ("tensor", "dp")),
            P("section", ("tensor", "dp")),
            P("section", ("tensor", "dp")),
            P("section", ("tensor", "dp")),
            P("section", "dp", None, "tensor"),
            P("section", None, ("tensor", "dp")),
            P("section", ("tensor", "dp"), None),
            P("section", ("tensor", "dp")),
            P("section", "dp", "tensor"),
            P("section", ("tensor", "dp")),
            P("section", ("tensor", "dp"), None),
            P("section", ("tensor", "dp")),
        ),
        check_vma=False,
    )
```

profile of v0, /device:TPU:0, one launch (start us, length us, event | category | flops | bytes accessed | tf_op | source)
XLA Modules:
  0.0 240.3 jit_solution(976772216132376486)
XLA Ops:
  7.2 1.1 slice_bitcast_fusion.3
  8.3 1.7 copy-done
  10.0 1.5 copy-done.2
  11.4 1.1 copy-done.5
  12.5 0.9 copy-done.7
  14.8 0.7 copy-done.39
  18.9 3.4 %shard_map.254 = bf16[128,768]{1,0:T(8,128)(2,1)S(1)} custom-call(bf16[128,768]{1,0:T(8,128)(2,1)S(1)} %get-tuple-element.120.refs_0_, s32[1]{0:T(128)} %bitcast.1.refs_1_.refs_2_, f32[3,128,128]{2,1,0:T(8,128)S(1)} %copy-done.7, bf16[1,768]{1,0:T(2,128)(2,1)S(1)} %copy-done.23, bf16[1,768]{1,0:T(2,128)(2,1)S(1)} %copy-done.41, ...), custom_call_target="tpu_custom_call" | custom-call | flops 905969664 | bytes 7077888 | tf_op jit(solution)/shard_map/pallas_call | solution.py:299
  22.3 3.0 %collective-permute-start = (bf16[128,768]{1,0:T(8,128)(2,1)S(1)}, bf16[128,768]{1,0:T(8,128)(2,1)S(1)}, u32[]{:S(2)}, u32[]{:S(2)}) collective-permute-start(bf16[128,768]{1,0:T(8,128)(2,1)S(1)} %shard_map.254), channel_id=1, source_target_pairs={{0,8},{8,0},{1,9},{9,1},{2,10},{10,2},{3,11},{11,3},{4,12},{12,4},... | collective-permute-start | bytes 589832 | tf_op jit(solution)/shard_map/ppermute | solution.py:364
  25.3 3.3 %shard_map.256 = bf16[128,768]{1,0:T(8,128)(2,1)S(1)} custom-call(bf16[128,768]{1,0:T(8,128)(2,1)S(1)} %get-tuple-element.121.refs_0_, s32[1]{0:T(128)} %bitcast.1.refs_1_.refs_2_, f32[3,128,128]{2,1,0:T(8,128)S(1)} %copy-done.8, bf16[1,768]{1,0:T(2,128)(2,1)S(1)} %copy-done.23, bf16[1,768]{1,0:T(2,128)(2,1)S(1)} %copy-done.41, ...), custom_call_target="tpu_custom_call" | custom-call | flops 905969664 | bytes 7077888 | tf_op jit(solution)/shard_map/pallas_call | solution.py:299
  28.8 1.4 collective-permute-done
  30.2 4.8 %collective-permute-done.3 = bf16[128,768]{1,0:T(8,128)(2,1)S(1)} collective-permute-done((bf16[128,768]{1,0:T(8,128)(2,1)S(1)}, bf16[128,768]{1,0:T(8,128)(2,1)S(1)}, u32[]{:S(2)}, u32[]{:S(2)}) %collective-permute-start.3) | collective-permute-done | bytes 196640 | tf_op jit(solution)/shard_map/ppermute | solution.py:364
  35.1 1.2 add_convert_fusion.5
  36.2 3.4 %collective-permute-start.1 = (bf16[128,768]{1,0:T(8,128)(2,1)S(1)}, bf16[128,768]{1,0:T(8,128)(2,1)S(1)}, u32[]{:S(2)}, u32[]{:S(2)}) collective-permute-start(bf16[128,768]{1,0:T(8,128)(2,1)S(1)} %get-tuple-element.118), channel_id=1, source_target_pairs={{0,16},{1,17},{2,18},{3,19},{4,20},{5,21},{6,22},{7,23},{8,24},{9,... | collective-permute-start | bytes 589832 | tf_op jit(solution)/shard_map/ppermute | solution.py:388
  39.6 1.5 collective-permute-start.4
  41.1 1.1 slice_bitcast_fusion.2
  42.2 2.5 %collective-permute-done.1 = bf16[128,768]{1,0:T(8,128)(2,1)S(1)} collective-permute-done((bf16[128,768]{1,0:T(8,128)(2,1)S(1)}, bf16[128,768]{1,0:T(8,128)(2,1)S(1)}, u32[]{:S(2)}, u32[]{:S(2)}) %collective-permute-start.1) | collective-permute-done | bytes 196640 | tf_op jit(solution)/shard_map/ppermute | solution.py:388
  44.7 2.1 collective-permute-done.4
  46.8 1.1 broadcast_select_fusion.3
  48.0 6.6 %shard_map.255 = (bf16[128,768]{1,0:T(8,128)(2,1)S(1)}, bf16[128,768]{1,0:T(8,128)(2,1)S(1)}, bf16[128,768]{1,0:T(8,128)(2,1)S(1)}, bf16[128,768]{1,0:T(8,128)(2...) custom-call(bf16[128,768]{1,0:T(8,128)(2,1)S(1)} %get-tuple-element., ...), custom_call_target="tpu_custom_call" | custom-call | flops 1811939328 | bytes 7077888 | tf_op jit(solution)/shard_map/pallas_call | solution.py:328
  54.6 0.7 copy-done.13
  57.3 0.7 copy-done.61
  58.7 0.7 copy-done.71
  60.0 1.8 collective-permute-start.6
  61.8 6.6 %shard_map.257 = (bf16[128,768]{1,0:T(8,128)(2,1)S(1)}, bf16[128,768]{1,0:T(8,128)(2,1)S(1)}, bf16[128,768]{1,0:T(8,128)(2,1)S(1)}, bf16[128,768]{1,0:T(8,128)(2...) custom-call(bf16[128,768]{1,0:T(8,128)(2,1)S(1)} %get-tuple-element., ...), custom_call_target="tpu_custom_call" | custom-call | flops 1811939328 | bytes 7077888 | tf_op jit(solution)/shard_map/pallas_call | solution.py:328
  68.4 0.9 copy-done.11
  69.3 0.7 copy-done.15
  70.4 5.4 %collective-permute-done.9 = bf16[128,768]{1,0:T(8,128)(2,1)S(1)} collective-permute-done((bf16[128,768]{1,0:T(8,128)(2,1)S(1)}, bf16[128,768]{1,0:T(8,128)(2,1)S(1)}, u32[]{:S(2)}, u32[]{:S(2)}) %collective-permute-start.9) | collective-permute-done | bytes 196640 | tf_op jit(solution)/shard_map/ppermute | solution.py:364
  75.9 0.9 add_convert_fusion.1
  76.7 1.3 collective-permute-start.7
  78.1 1.3 collective-permute-start.10
  79.4 5.5 %collective-permute-done.7 = bf16[128,768]{1,0:T(8,128)(2,1)} collective-permute-done((bf16[128,768]{1,0:T(8,128)(2,1)}, bf16[128,768]{1,0:T(8,128)(2,1)}, u32[]{:S(2)}, u32[]{:S(2)}) %collective-permute-start.7) | collective-permute-done | bytes 196640 | tf_op jit(solution)/shard_map/ppermute | solution.py:395
  84.9 2.1 collective-permute-done.10
  87.0 1.3 broadcast_select_fusion.1
  88.3 2.1 convolution_convert_fusion.3
  90.7 1.1 copy-done.12
  91.8 1.0 copy-done.16
  92.8 0.9 copy-done.34
  93.7 0.9 copy-done.36
  94.6 0.9 copy-done.38
  95.5 6.7 %shard_map.259 = (bf16[128,768]{1,0:T(8,128)(2,1)S(1)}, bf16[128,1536]{1,0:T(8,128)(2,1)S(1)}, bf16[128,1152]{1,0:T(8,128)(2,1)S(1)}, f32[5,768]{1,0:T(8,128)S(1...) custom-call(bf16[128,768]{1,0:T(8,128)(2,1)S(1)} %get-tuple-element.117.refs_0_, ...), custom_call_target="tpu_custom_call" | custom-call | flops 905969664 | bytes 7077888 | tf_op jit(solution)/shard_map/pallas_call | solution.py:352
  103.4 0.7 copy-done.65
  104.2 6.7 %shard_map.258 = (bf16[128,768]{1,0:T(8,128)(2,1)S(1)}, bf16[128,1536]{1,0:T(8,128)(2,1)S(1)}, bf16[128,1152]{1,0:T(8,128)(2,1)S(1)}, f32[5,768]{1,0:T(8,128)S(1...) custom-call(bf16[128,768]{1,0:T(8,128)(2,1)S(1)} %get-tuple-element.116.refs_0_, ...), custom_call_target="tpu_custom_call" | custom-call | flops 905969664 | bytes 7077888 | tf_op jit(solution)/shard_map/pallas_call | solution.py:352
  110.9 0.7 copy-done.21
  113.4 0.7 copy-done.67
  114.2 1.9 convolution_convert_fusion.2
  116.2 2.2 convolution_convert_fusion.1
  118.5 0.9 copy-done.62
  119.5 2.2 convolution_convert_fusion
  121.9 0.8 copy-done.18
  123.0 1.7 collective-permute-start.2
  124.7 3.6 %collective-permute-done.5 = bf16[128,768]{1,0:T(8,128)(2,1)S(1)} collective-permute-done((bf16[128,768]{1,0:T(8,128)(2,1)S(1)}, bf16[128,768]{1,0:T(8,128)(2,1)S(1)}, u32[]{:S(2)}, u32[]{:S(2)}) %collective-permute-start.5) | collective-permute-done | bytes 196640 | tf_op jit(solution)/shard_map/ppermute | solution.py:364
  128.5 2.0 collective-permute-done.2
  130.6 0.8 maximum_bitcast_fusion.1
  131.7 58.6 %psum.7 = f32[9216]{0:T(1024)S(1)} all-reduce(f32[9216]{0:T(1024)S(1)} %pad_maximum_fusion.3), channel_id=1, replica_groups=mesh['section'=2,'tensor'=2,'dp'=8] {'tensor','dp'}, use_global_device_ids=true, to_apply=%region_0.1 | all-reduce | flops 9216 | bytes 73728 | tf_op jit(solution)/shard_map/psum | solution.py:440
  190.8 1.6 collective-permute-start.8
  194.4 1.6 collective-permute-done.11
  196.1 2.0 collective-permute-done.8
  198.2 0.9 maximum_bitcast_fusion
  199.2 1.6 bitcast_convert_fusion.2
  200.7 1.1 reshape.85
  201.9 0.8 copy.34
  202.7 1.8 bitcast_convert_fusion.1
  204.5 27.0 %reduce-scatter.11.cloned.1.call-done = bf16[192,768]{1,0:T(8,128)(2,1)} async-done(((bf16[1536,768]{1,0:T(8,128)(2,1)}), bf16[192,768]{1,0:T(8,128)(2,1)}) %reduce-scatter.11.cloned.1.call-update) | async-done | bytes 294928 | tf_op jit(solution)/shard_map/reduce_scatter | solution.py:428
  231.5 1.8 bitcast_convert_fusion
  (184 shorter events, 16.1 us)
Async XLA Ops:
  7.2 192.0 %reduce-scatter.7.cloned.1.call-start = ((), (), s32[]{:S(2)}) async-start(), calls=%async_computation.5 | async-start | bytes 663552 | tf_op jit(solution)/shard_map/reduce_scatter | solution.py:428
  8.3 1.7 copy-start
  10.0 1.5 copy-start.2
  11.4 1.1 copy-start.5
  18.9 6.4 %copy-start.1 = (bf16[1,768,1536]{2,1,0:T(8,128)(2,1)S(1)}, bf16[1,768,1536]{2,1,0:T(8,128)(2,1)}, u32[]{:S(2)}) copy-start(bf16[1,768,1536]{2,1,0:T(8,128)(2,1)} %param.25) | copy-start | bytes 7077892
  18.9 6.4 %copy-start.3 = (bf16[1,768,3,384]{3,1,2,0:T(8,128)(2,1)S(1)}, bf16[1,768,3,384]{3,1,2,0:T(8,128)(2,1)}, u32[]{:S(2)}) copy-start(bf16[1,768,3,384]{3,1,2,0:T(8,128)(2,1)} %param.21) | copy-start | bytes 5308420
  18.9 6.4 %copy-start.8 = (f32[3,128,128]{2,1,0:T(8,128)S(1)}, f32[3,128,128]{2,1,0:T(8,128)}, u32[]{:S(2)}) copy-start(f32[3,128,128]{2,1,0:T(8,128)} %constant.36.clone.refs_2_.refs_3_) | copy-start | bytes 589828
  22.3 7.9 %collective-permute-start = (bf16[128,768]{1,0:T(8,128)(2,1)S(1)}, bf16[128,768]{1,0:T(8,128)(2,1)S(1)}, u32[]{:S(2)}, u32[]{:S(2)}) collective-permute-start(bf16[128,768]{1,0:T(8,128)(2,1)S(1)} %shard_map.254), channel_id=1, source_target_pairs={{0,8},{8,0},{1,9},{9,1},{2,10},{10,2},{3,11},{11,3},{4,12},{12,4},... | collective-permute-start | bytes 589832 | tf_op jit(solution)/shard_map/ppermute | solution.py:364
  28.6 6.4 %collective-permute-start.3 = (bf16[128,768]{1,0:T(8,128)(2,1)S(1)}, bf16[128,768]{1,0:T(8,128)(2,1)S(1)}, u32[]{:S(2)}, u32[]{:S(2)}) collective-permute-start(bf16[128,768]{1,0:T(8,128)(2,1)S(1)} %shard_map.256), channel_id=1, source_target_pairs={{0,8},{8,0},{1,9},{9,1},{2,10},{10,2},{3,11},{11,3},{4,12},{12,4},... | collective-permute-start | bytes 589832 | tf_op jit(solution)/shard_map/ppermute | solution.py:364
  28.7 19.1 %copy-start.4 = (bf16[1,768,3,384]{3,1,2,0:T(8,128)(2,1)S(1)}, bf16[1,768,3,384]{3,1,2,0:T(8,128)(2,1)}, u32[]{:S(2)}) copy-start(bf16[1,768,3,384]{3,1,2,0:T(8,128)(2,1)} %param.21) | copy-start | bytes 5308420
  28.7 19.1 %copy-start.6 = (bf16[1,384,768]{2,1,0:T(8,128)(2,1)S(1)}, bf16[1,384,768]{2,1,0:T(8,128)(2,1)}, u32[]{:S(2)}) copy-start(bf16[1,384,768]{2,1,0:T(8,128)(2,1)} %param.23) | copy-start | bytes 1769476
  28.7 19.1 %copy-start.24 = (bf16[1,768]{1,0:T(2,128)(2,1)S(1)}, bf16[1,768]{1,0:T(2,128)(2,1)}, u32[]{:S(2)}) copy-start(bf16[1,768]{1,0:T(2,128)(2,1)} %refs_3_.9) | copy-start | bytes 4612
  28.7 19.1 %copy-start.26 = (bf16[1,768]{1,0:T(2,128)(2,1)S(1)}, bf16[1,768]{1,0:T(2,128)(2,1)}, u32[]{:S(2)}) copy-start(bf16[1,768]{1,0:T(2,128)(2,1)} %refs_4_.11) | copy-start | bytes 4612
  28.8 19.1 %copy-start.40 = (bf16[1,1536]{1,0:T(2,128)(2,1)S(1)}, bf16[1,1536]{1,0:T(2,128)(2,1)}, u32[]{:S(2)}) copy-start(bf16[1,1536]{1,0:T(2,128)(2,1)} %refs_10_.7) | copy-start | bytes 9220
  28.8 19.1 %copy-start.42 = (bf16[1,768]{1,0:T(2,128)(2,1)S(1)}, bf16[1,768]{1,0:T(2,128)(2,1)}, u32[]{:S(2)}) copy-start(bf16[1,768]{1,0:T(2,128)(2,1)} %refs_5_.7) | copy-start | bytes 4612
  28.8 19.1 %copy-start.44 = (bf16[1,768]{1,0:T(2,128)(2,1)S(1)}, bf16[1,768]{1,0:T(2,128)(2,1)}, u32[]{:S(2)}) copy-start(bf16[1,768]{1,0:T(2,128)(2,1)} %refs_7_.3) | copy-start | bytes 4612
  28.8 19.1 %copy-start.46 = (bf16[1,3,384]{2,1,0:T(4,128)(2,1)S(1)}, bf16[1,3,384]{2,1,0:T(4,128)(2,1)}, u32[]{:S(2)}) copy-start(bf16[1,3,384]{2,1,0:T(4,128)(2,1)} %param.22) | copy-start | bytes 6916
  28.8 19.1 %copy-start.48 = (bf16[1,768]{1,0:T(2,128)(2,1)S(1)}, bf16[1,768]{1,0:T(2,128)(2,1)}, u32[]{:S(2)}) copy-start(bf16[1,768]{1,0:T(2,128)(2,1)} %refs_9_.7) | copy-start | bytes 4612
  28.8 19.1 %copy-start.50 = (bf16[1,768]{1,0:T(2,128)(2,1)S(1)}, bf16[1,768]{1,0:T(2,128)(2,1)}, u32[]{:S(2)}) copy-start(bf16[1,768]{1,0:T(2,128)(2,1)} %refs_11_.3) | copy-start | bytes 4612
  36.2 8.5 %collective-permute-start.1 = (bf16[128,768]{1,0:T(8,128)(2,1)S(1)}, bf16[128,768]{1,0:T(8,128)(2,1)S(1)}, u32[]{:S(2)}, u32[]{:S(2)}) collective-permute-start(bf16[128,768]{1,0:T(8,128)(2,1)S(1)} %get-tuple-element.118), channel_id=1, source_target_pairs={{0,16},{1,17},{2,18},{3,19},{4,20},{5,21},{6,22},{7,23},{8,24},{9,... | collective-permute-start | bytes 589832 | tf_op jit(solution)/shard_map/ppermute | solution.py:388
  39.6 7.2 %collective-permute-start.4 = (bf16[128,768]{1,0:T(8,128)(2,1)S(1)}, bf16[128,768]{1,0:T(8,128)(2,1)S(1)}, u32[]{:S(2)}, u32[]{:S(2)}) collective-permute-start(bf16[128,768]{1,0:T(8,128)(2,1)S(1)} %get-tuple-element.119), channel_id=1, source_target_pairs={{0,16},{1,17},{2,18},{3,19},{4,20},{5,21},{6,22},{7,23},{8,24},{9,... | collective-permute-start | bytes 589832 | tf_op jit(solution)/shard_map/ppermute | solution.py:388
  60.0 8.4 %copy-start.9 = (f32[128,1536]{1,0:T(8,128)}, f32[128,1536]{1,0:T(8,128)S(1)}, u32[]{:S(2)}) copy-start(f32[128,1536]{1,0:T(8,128)S(1)} %get-tuple-element.55.refs_13_) | copy-start | bytes 2359300
  60.0 10.4 %collective-permute-start.6 = (bf16[128,768]{1,0:T(8,128)(2,1)S(1)}, bf16[128,768]{1,0:T(8,128)(2,1)S(1)}, u32[]{:S(2)}, u32[]{:S(2)}) collective-permute-start(bf16[128,768]{1,0:T(8,128)(2,1)S(1)} %get-tuple-element.50), channel_id=1, source_target_pairs={{0,8},{8,0},{1,9},{9,1},{2,10},{10,2},{3,11},{11,3},{4,12},{12,4},... | collective-permute-start | bytes 589832 | tf_op jit(solution)/shard_map/ppermute | solution.py:364
  61.8 14.1 %copy-start.79 = (bf16[2,1,128,768]{3,2,1,0:T(8,128)(2,1)S(1)}, bf16[2,1,128,768]{3,2,1,0:T(8,128)(2,1)}, u32[]{:S(2)}) copy-start(bf16[2,1,128,768]{3,2,1,0:T(8,128)(2,1)} %param.16) | copy-start | bytes 1179652
  70.1 6.7 %copy-start.33 = (bf16[128,384]{1,0:T(8,128)(2,1)}, bf16[128,384]{1,0:T(8,128)(2,1)S(1)}, u32[]{:S(2)}) copy-start(bf16[128,384]{1,0:T(8,128)(2,1)S(1)} %get-tuple-element.58.refs_9_) | copy-start | bytes 294916
  70.1 6.7 %copy-start.35 = (bf16[128,384]{1,0:T(8,128)(2,1)}, bf16[128,384]{1,0:T(8,128)(2,1)S(1)}, u32[]{:S(2)}) copy-start(bf16[128,384]{1,0:T(8,128)(2,1)S(1)} %get-tuple-element.59.refs_10_) | copy-start | bytes 294916
  70.1 8.0 %copy-start.37 = (bf16[128,384]{1,0:T(8,128)(2,1)}, bf16[128,384]{1,0:T(8,128)(2,1)S(1)}, u32[]{:S(2)}) copy-start(bf16[128,384]{1,0:T(8,128)(2,1)S(1)} %get-tuple-element.60.refs_11_) | copy-start | bytes 294916
  70.1 8.0 %copy-start.63 = (bf16[128,1536]{1,0:T(8,128)(2,1)}, bf16[128,1536]{1,0:T(8,128)(2,1)S(1)}, u32[]{:S(2)}) copy-start(bf16[128,1536]{1,0:T(8,128)(2,1)S(1)} %get-tuple-element.81) | copy-start | bytes 1179652
  70.1 8.0 %copy-start.73 = (bf16[128,768]{1,0:T(8,128)(2,1)}, bf16[128,768]{1,0:T(8,128)(2,1)S(1)}, u32[]{:S(2)}) copy-start(bf16[128,768]{1,0:T(8,128)(2,1)S(1)} %get-tuple-element.77) | copy-start | bytes 589828
  70.1 8.0 %copy-start.75 = (bf16[128,768]{1,0:T(8,128)(2,1)}, bf16[128,768]{1,0:T(8,128)(2,1)S(1)}, u32[]{:S(2)}) copy-start(bf16[128,768]{1,0:T(8,128)(2,1)S(1)} %get-tuple-element.71) | copy-start | bytes 589828
  70.1 8.0 %copy-start.78 = (bf16[128,384]{1,0:T(8,128)(2,1)}, bf16[128,384]{1,0:T(8,128)(2,1)S(1)}, u32[]{:S(2)}) copy-start(bf16[128,384]{1,0:T(8,128)(2,1)S(1)} %get-tuple-element.75) | copy-start | bytes 294916
  70.1 14.8 %copy-start.17 = (bf16[128,768]{1,0:T(8,128)(2,1)}, bf16[128,768]{1,0:T(8,128)(2,1)S(1)}, u32[]{:S(2)}) copy-start(bf16[128,768]{1,0:T(8,128)(2,1)S(1)} %get-tuple-element.49) | copy-start | bytes 589828
  70.1 5.7 %collective-permute-start.9 = (bf16[128,768]{1,0:T(8,128)(2,1)S(1)}, bf16[128,768]{1,0:T(8,128)(2,1)S(1)}, u32[]{:S(2)}, u32[]{:S(2)}) collective-permute-start(bf16[128,768]{1,0:T(8,128)(2,1)S(1)} %get-tuple-element.57), channel_id=1, source_target_pairs={{0,8},{8,0},{1,9},{9,1},{2,10},{10,2},{3,11},{11,3},{4,12},{12,4},... | collective-permute-start | bytes 589832 | tf_op jit(solution)/shard_map/ppermute | solution.py:364
  76.7 8.1 %collective-permute-start.7 = (bf16[128,768]{1,0:T(8,128)(2,1)}, bf16[128,768]{1,0:T(8,128)(2,1)}, u32[]{:S(2)}, u32[]{:S(2)}) collective-permute-start(bf16[128,768]{1,0:T(8,128)(2,1)} %get-tuple-element.112), channel_id=1, source_target_pairs={{16,0},{17,1},{18,2},{19,3},{20,4},{21,5},{22,6},{23,7},{24,8},{25... | collective-permute-start | bytes 589832 | tf_op jit(solution)/shard_map/ppermute | solution.py:395
  78.1 8.9 %collective-permute-start.10 = (bf16[128,768]{1,0:T(8,128)(2,1)}, bf16[128,768]{1,0:T(8,128)(2,1)}, u32[]{:S(2)}, u32[]{:S(2)}) collective-permute-start(bf16[128,768]{1,0:T(8,128)(2,1)} %get-tuple-element.113), channel_id=1, source_target_pairs={{16,0},{17,1},{18,2},{19,3},{20,4},{21,5},{22,6},{23,7},{24,8},{25... | collective-permute-start | bytes 589832 | tf_op jit(solution)/shard_map/ppermute | solution.py:395
  90.4 110.3 %reduce-scatter.5.cloned.1.call-start = ((), (), s32[]{:S(2)}) async-start(), calls=%async_computation.4 | async-start | bytes 1990656 | tf_op jit(solution)/shard_map/reduce_scatter | solution.py:428
  90.7 1.1 copy-start.12
  95.5 8.7 %copy-start.10 = (f32[128,1536]{1,0:T(8,128)S(1)}, f32[128,1536]{1,0:T(8,128)}, u32[]{:S(2)}) copy-start(f32[128,1536]{1,0:T(8,128)} %copy-done.9) | copy-start | bytes 2359300
  95.5 8.7 %copy-start.14 = (f32[128,768]{1,0:T(8,128)S(1)}, f32[128,768]{1,0:T(8,128)}, u32[]{:S(2)}) copy-start(f32[128,768]{1,0:T(8,128)} %copy-done.13) | copy-start | bytes 1179652
  95.5 8.7 %copy-start.28 = (bf16[128,384]{1,0:T(8,128)(2,1)S(1)}, bf16[128,384]{1,0:T(8,128)(2,1)}, u32[]{:S(2)}) copy-start(bf16[128,384]{1,0:T(8,128)(2,1)} %copy-done.27) | copy-start | bytes 294916
  95.5 8.7 %copy-start.30 = (bf16[128,384]{1,0:T(8,128)(2,1)S(1)}, bf16[128,384]{1,0:T(8,128)(2,1)}, u32[]{:S(2)}) copy-start(bf16[128,384]{1,0:T(8,128)(2,1)} %copy-done.29) | copy-start | bytes 294916
  95.5 8.7 %copy-start.32 = (bf16[128,384]{1,0:T(8,128)(2,1)S(1)}, bf16[128,384]{1,0:T(8,128)(2,1)}, u32[]{:S(2)}) copy-start(bf16[128,384]{1,0:T(8,128)(2,1)} %copy-done.31) | copy-start | bytes 294916
  104.2 6.8 %copy-start.19 = (bf16[128,768]{1,0:T(8,128)(2,1)}, bf16[128,768]{1,0:T(8,128)(2,1)S(1)}, u32[]{:S(2)}) copy-start(bf16[128,768]{1,0:T(8,128)(2,1)S(1)} %get-tuple-element.63) | copy-start | bytes 589828
  104.2 10.0 %copy-start.72 = (bf16[128,768]{1,0:T(8,128)(2,1)S(1)}, bf16[128,768]{1,0:T(8,128)(2,1)}, u32[]{:S(2)}) copy-start(bf16[128,768]{1,0:T(8,128)(2,1)} %copy-done.71) | copy-start | bytes 589828
  104.2 10.0 %copy-start.76 = (bf16[128,768]{1,0:T(8,128)(2,1)S(1)}, bf16[128,768]{1,0:T(8,128)(2,1)}, u32[]{:S(2)}) copy-start(bf16[128,768]{1,0:T(8,128)(2,1)} %copy-done.75) | copy-start | bytes 589828
  114.2 2.0 copy-start.66
  114.2 2.0 copy-start.68
  114.2 2.0 copy-start.70
  114.2 2.0 copy-start.74
  116.1 86.5 %reduce-scatter.9.cloned.1.call-start = ((), (), s32[]{:S(2)}) async-start(), calls=%async_computation.6 | async-start | bytes 2654208 | tf_op jit(solution)/shard_map/reduce_scatter | solution.py:428
  118.4 1.1 copy-start.64
  118.5 113.0 %reduce-scatter.11.cloned.1.call-start = ((), (), s32[]{:S(2)}) async-start(), calls=%async_computation.7 | async-start | bytes 2654208 | tf_op jit(solution)/shard_map/reduce_scatter | solution.py:428
  121.8 9.5 %copy-start.58 = (f32[1,1152]{1,0:T(1,128)S(1)}, f32[1,1152]{1,0:T(1,128)}, u32[]{:S(2)}) copy-start(f32[1,1152]{1,0:T(1,128)} %copy-done.57) | copy-start | bytes 13828
  121.8 9.5 %copy-start.60 = (f32[1,1152]{1,0:T(1,128)S(1)}, f32[1,1152]{1,0:T(1,128)}, u32[]{:S(2)}) copy-start(f32[1,1152]{1,0:T(1,128)} %copy-done.59) | copy-start | bytes 13828
  121.8 9.6 %copy-start.56 = (f32[1,1536]{1,0:T(1,128)S(1)}, f32[1,1536]{1,0:T(1,128)}, u32[]{:S(2)}) copy-start(f32[1,1536]{1,0:T(1,128)} %copy-done.55) | copy-start | bytes 18436
  121.8 9.8 %copy-start.52 = (f32[5,768]{1,0:T(8,128)S(1)}, f32[5,768]{1,0:T(8,128)}, u32[]{:S(2)}) copy-start(f32[5,768]{1,0:T(8,128)} %copy-done.51) | copy-start | bytes 46084
  121.9 9.8 %copy-start.54 = (f32[5,768]{1,0:T(8,128)S(1)}, f32[5,768]{1,0:T(8,128)}, u32[]{:S(2)}) copy-start(f32[5,768]{1,0:T(8,128)} %copy-done.53) | copy-start | bytes 46084
  121.9 68.5 %copy-start.20 = (bf16[128,768]{1,0:T(8,128)(2,1)S(1)}, bf16[128,768]{1,0:T(8,128)(2,1)}, u32[]{:S(2)}) copy-start(bf16[128,768]{1,0:T(8,128)(2,1)} %copy-done.19) | copy-start | bytes 589828
  121.9 69.0 %copy-start.22 = (bf16[128,768]{1,0:T(8,128)(2,1)S(1)}, bf16[128,768]{1,0:T(8,128)(2,1)}, u32[]{:S(2)}) copy-start(bf16[128,768]{1,0:T(8,128)(2,1)} %copy-done.21) | copy-start | bytes 589828
  122.7 5.7 %collective-permute-start.5 = (bf16[128,768]{1,0:T(8,128)(2,1)S(1)}, bf16[128,768]{1,0:T(8,128)(2,1)S(1)}, u32[]{:S(2)}, u32[]{:S(2)}) collective-permute-start(bf16[128,768]{1,0:T(8,128)(2,1)S(1)} %copy-done.18), channel_id=1, source_target_pairs={{0,8},{8,0},{1,9},{9,1},{2,10},{10,2},{3,11},{11,3},{4,12},{12,4},... | collective-permute-start | bytes 589832 | tf_op jit(solution)/shard_map/ppermute | solution.py:364
  123.0 7.5 %collective-permute-start.2 = (bf16[128,768]{1,0:T(8,128)(2,1)S(1)}, bf16[128,768]{1,0:T(8,128)(2,1)S(1)}, u32[]{:S(2)}, u32[]{:S(2)}) collective-permute-start(bf16[128,768]{1,0:T(8,128)(2,1)S(1)} %get-tuple-element.48), channel_id=1, source_target_pairs={{0,8},{8,0},{1,9},{9,1},{2,10},{10,2},{3,11},{11,3},{4,12},{12,4},... | collective-permute-start | bytes 589832 | tf_op jit(solution)/shard_map/ppermute | solution.py:364
  190.3 5.7 %collective-permute-start.11 = (bf16[128,768]{1,0:T(8,128)(2,1)S(1)}, bf16[128,768]{1,0:T(8,128)(2,1)S(1)}, u32[]{:S(2)}, u32[]{:S(2)}) collective-permute-start(bf16[128,768]{1,0:T(8,128)(2,1)S(1)} %copy-done.20), channel_id=1, source_target_pairs={{0,8},{8,0},{1,9},{9,1},{2,10},{10,2},{3,11},{11,3},{4,12},{12,4},... | collective-permute-start | bytes 589832 | tf_op jit(solution)/shard_map/ppermute | solution.py:364
  190.8 7.3 %collective-permute-start.8 = (bf16[128,768]{1,0:T(8,128)(2,1)S(1)}, bf16[128,768]{1,0:T(8,128)(2,1)S(1)}, u32[]{:S(2)}, u32[]{:S(2)}) collective-permute-start(bf16[128,768]{1,0:T(8,128)(2,1)S(1)} %copy-done.22), channel_id=1, source_target_pairs={{0,8},{8,0},{1,9},{9,1},{2,10},{10,2},{3,11},{11,3},{4,12},{12,4},... | collective-permute-start | bytes 589832 | tf_op jit(solution)/shard_map/ppermute | solution.py:364
  194.4 38.9 %copy-start.80 = (f32[1,48]{1,0:T(1,128)}, f32[1,48]{1,0:T(1,128)S(1)}, u32[]{:S(2)}) copy-start(f32[1,48]{1,0:T(1,128)S(1)} %get-tuple-element.154) | copy-start | bytes 580
  (33 other events, 24.2 us)
Sparse Core Ops, SparseCore 0:
  90.5 30.5 reduce-scatter.6
  123.4 33.2 reduce-scatter.4
  159.0 34.9 reduce-scatter.8
  196.2 35.2 reduce-scatter.10
where the time goes:
time: 241 us; the launch traced here: 240 us
  waiting for transfers between devices  60.2 us (25%)
  blocking collectives  58.6 us (24%)
  local copies, waits for them, and re-layouts  36.3 us (15%)
  Pallas kernels  33.3 us (14%)
  starting transfers between devices  17.2 us (7%)
  between operations  14.5 us (6%)
  other arithmetic  11.6 us (5%)
  matrix products  8.47 us (4%)
    psum x1, blocking collectives, per_device(): lax.psum(jnp.concatenate([sum_d.reshape(-1), flat]), ('tensor', 'dp'))  58.6 us
    unnamed x164, local copies, waits for them, and re-layouts  31 us
    reduce_scatter x4, waiting for transfers between devices, scatter(): lax.psum_scatter(value, 'dp', scatter_dimension=0, tiled=True).astype(F32)  27 us
    ppermute x8, waiting for transfers between devices, swap(): return lax.ppermute(value, 'tensor', [(0, 1), (1, 0)])  20.9 us
    pallas_call x2, Pallas kernels, call_b(): pl.pallas_call(b_kernel, out_shape=outs, in_specs=[VM] * 3 + [VM] * 2 + [...  13.4 us
    pallas_call x2, Pallas kernels, call_fb(): pl.pallas_call(fb_kernel, out_shape=outs, in_specs=[VM, VM, SM, VM] + [VM...  13.3 us
    ppermute x8, starting transfers between devices, swap(): return lax.ppermute(value, 'tensor', [(0, 1), (1, 0)])  9.34 us
    dot_general x4, matrix products, outer(): return jnp.einsum('ta,tb->ab', a, b, preferred_element_type=F32).astype(BF)  8.47 us
  transfers between devices with their start and end apart: 16, of which 12 were waited for; matrix products, arithmetic and copies ran while one was open for 7% of the time, Pallas kernels for 10%

commit v1 on v0

v1 whole, which is shorter than its diff:
```python
import functools
import math

import jax
import jax.numpy as jnp
import numpy as np
from jax import lax
from jax.experimental import pallas as pl
from jax.experimental.pallas import tpu as pltpu
from jax.sharding import PartitionSpec as P

HEAD = 64
ROT = 16
LANES = 128
PIECE = 512
EPSILON = 1e-05
BF = jnp.bfloat16
F32 = jnp.float32


def rope_tables(length):
    half = ROT // 2
    inverse = np.exp(-math.log(10000.0) * np.arange(half, dtype=np.float32) * np.float32(2.0) / ROT)
    angle = np.arange(length, dtype=np.float32)[:, None] * inverse[None, :].astype(np.float32)
    cosine, sine = np.cos(angle), np.sin(angle)
    table = np.zeros((3, length, LANES), np.float32)
    table[0] = 1.0
    for head in range(LANES // HEAD):
        at = head * HEAD
        table[0, :, at : at + half] = cosine
        table[0, :, at + half : at + ROT] = cosine
        table[1, :, at : at + half] = -sine
        table[2, :, at + half : at + ROT] = sine
    return table


def dot(a, b):
    return jnp.dot(a, b, preferred_element_type=F32)


def dot_nt(a, b):
    return lax.dot_general(a, b, (((1,), (1,)), ((), ())), preferred_element_type=F32)


def dot_tn(a, b):
    return lax.dot_general(a, b, (((0,), (0,)), ((), ())), preferred_element_type=F32)


def roped(value, table, sign):
    half = ROT // 2
    ahead = pltpu.roll(value, LANES - half, 1) * table[1]
    behind = pltpu.roll(value, half, 1) * table[2]
    return value * table[0] + sign * (ahead + behind)


def head_pair(value):
    low = lax.broadcasted_iota(jnp.int32, value.shape, 1) < HEAD
    zero = jnp.zeros_like(value)
    return jnp.concatenate([jnp.where(low, value, zero), jnp.where(low, zero, value)], axis=0)


def pair_merge(value):
    rows = value.shape[0] // 2
    low = lax.broadcasted_iota(jnp.int32, (rows, LANES), 1) < HEAD
    return jnp.where(low, value[:rows], value[rows:])


def normal(block):
    width = block.shape[1]
    center = block - jnp.sum(block, axis=1, keepdims=True) * (1.0 / width)
    spread = jnp.sum(center * center, axis=1, keepdims=True) * (1.0 / width)
    scale = lax.rsqrt(spread + EPSILON)
    return center * scale, scale


def forward_part(x, vec, table, w, wait, put):
    rows, width = x.shape
    unit, unused = normal(x.astype(F32))
    first = (unit * vec["g1"] + vec["b1"]).astype(BF)
    second = (unit * vec["g2"] + vec["b2"]).astype(BF)
    put("a1", first)
    put("a2", second)
    bqkv = vec["bqkv"]
    raw = []
    for j in range(3):
        wait("wqkv", j)
        raw.append(dot(first, w["wqkv"][j]) + bqkv[j : j + 1])
    local = raw[0].shape[1]
    row = lax.broadcasted_iota(jnp.int32, (rows, rows), 0)
    keep = row >= lax.broadcasted_iota(jnp.int32, (rows, rows), 1)
    for p in range(local // LANES):
        sl = slice(p * LANES, (p + 1) * LANES)
        q = roped(raw[0][:, sl], table, 1.0).astype(BF)
        k = roped(raw[1][:, sl], table, 1.0).astype(BF)
        v = raw[2][:, sl].astype(BF)
        put("q", q, sl)
        put("k", k, sl)
        put("v", v, sl)
        scores = dot_nt(q, head_pair(k)) * HEAD**-0.5
        prob = []
        for h in range(2):
            part = jnp.where(keep, scores[:, h * rows : (h + 1) * rows], -1e30)
            expo = jnp.exp(part - jnp.max(part, axis=1, keepdims=True))
            prob.append(expo * (1.0 / jnp.sum(expo, axis=1, keepdims=True)))
        prob = jnp.concatenate(prob, axis=1)
        put("prob", prob, slice(p * 2 * rows, (p + 1) * 2 * rows))
        put("mixed", dot(prob.astype(BF), head_pair(v)).astype(BF), sl)
    hidden = w["wup"].shape[1]
    step = 256
    for c in range(0, hidden, step):
        sl = slice(c, c + step)
        wait("wup", c // PIECE)
        u = dot(second, w["wup"][:, sl]) + vec["bup"][:, sl]
        phi = 0.5 + 0.5 * lax.erf(u * (2.0**-0.5))
        put("g", (u * phi).astype(BF), sl)
        put("gp", lambda: phi + u * (jnp.exp(-0.5 * u * u) * (2.0 * math.pi) ** -0.5), sl)


def output_part(mixed, active, vec, w, wait):
    wait("wout")
    total = dot(mixed[...], w["wout"][...])
    wait("wdown")
    total = total + dot(active[...], w["wdown"][...])
    return (total + vec["extra"]).astype(BF)


def backward_part(dy, saved, table, w, wait, put):
    rows = dy.shape[0]
    hidden = w["wdown"].shape[0]
    step = 256
    for c in range(0, hidden, step):
        sl = slice(c, c + step)
        wait("wdown", c // PIECE)
        du = (dot_nt(dy, w["wdown"][sl, :]) * saved["gp"][:, sl].astype(F32)).astype(BF)
        put("du", du, sl)
    wait("wout")
    d_mixed = dot_nt(dy, w["wout"][...]).astype(BF)
    local = d_mixed.shape[1]
    for p in range(local // LANES):
        sl = slice(p * LANES, (p + 1) * LANES)
        q, k, v = saved["q"][:, sl], saved["k"][:, sl], saved["v"][:, sl]
        prob = saved["prob"][:, p * 2 * rows : (p + 1) * 2 * rows]
        d_tile = d_mixed[:, sl]
        d_prob = dot_nt(d_tile, head_pair(v))
        d_value = pair_merge(dot_tn(prob.astype(BF), d_tile))
        d_scores = []
        for h in range(2):
            part = prob[:, h * rows : (h + 1) * rows]
            d_part = d_prob[:, h * rows : (h + 1) * rows]
            both = part * d_part
            d_scores.append(both - part * jnp.sum(both, axis=1, keepdims=True))
        d_scores = jnp.concatenate(d_scores, axis=1).astype(BF)
        scale = HEAD**-0.5
        d_query = dot(d_scores, head_pair(k)) * scale
        d_keys = pair_merge(dot_tn(d_scores, q)) * scale
        put("dqkv", roped(d_query, table, -1.0).astype(BF), slice(p * LANES, (p + 1) * LANES))
        at = local + p * LANES
        put("dqkv", roped(d_keys, table, -1.0).astype(BF), slice(at, at + LANES))
        at = 2 * local + p * LANES
        put("dqkv", d_value.astype(BF), slice(at, at + LANES))


def norm_back(x, du, dqkv, local, vec, w, wait):
    wait("wup")
    d_second = dot_nt(du[...], w["wup"][...])
    for j in range(3):
        wait("wqkv", j)
    d_first = dot_nt(dqkv[:, :local], w["wqkv"][0])
    for j in range(1, 3):
        d_first = d_first + dot_nt(dqkv[:, j * local : (j + 1) * local], w["wqkv"][j])
    unit, scale = normal(x.astype(F32))
    e = d_first * vec["g1"] + d_second * vec["g2"]
    width = x.shape[1]
    mean = jnp.sum(e, axis=1, keepdims=True) * (1.0 / width)
    along = jnp.sum(e * unit, axis=1, keepdims=True) * (1.0 / width)
    dx = (e - mean - unit * along) * scale
    return dx.astype(BF), d_first, d_second, unit


WEIGHTS = ("wqkv", "wout", "wup", "wdown")
VECTORS = ("g1", "b1", "g2", "b2", "bqkv", "bout", "bup", "bdown")
SAVED = ("a1", "a2", "q", "k", "v", "prob", "mixed", "g", "gp")


class Loads:
    def __init__(self, sems):
        self.sems, self.copies, self.count = sems, {}, 0

    def start(self, name, source, target):
        copy = pltpu.make_async_copy(source, target, self.sems.at[self.count])
        self.count += 1
        self.copies.setdefault(name, {})[len(self.copies.get(name, {}))] = copy
        copy.start()

    def weight(self, name, hbm, w):
        source, target = hbm[name], w[name]
        if name == "wqkv":
            for j in range(3):
                self.start(name, source.at[j], target.at[j])
        elif name == "wout":
            self.start(name, source, target)
        else:
            for c in range(0, source.shape[0 if name == "wdown" else 1], PIECE):
                at = (pl.ds(c, PIECE), slice(None)) if name == "wdown" else (slice(None), pl.ds(c, PIECE))
                self.start(name, source.at[at], target.at[at])

    def wait(self, name, index=None):
        left = self.copies[name]
        for piece in [index] if index is not None else list(left):
            copy = left.pop(piece, None)
            if copy is not None:
                copy.wait()


def unpacked(pack, width, local, hidden):
    return {
        "g1": pack[0:1, :width],
        "b1": pack[1:2, :width],
        "g2": pack[2:3, :width],
        "b2": pack[3:4, :width],
        "extra": pack[4:5, :width],
        "bup": pack[5:6, :hidden],
        "bqkv": pack[6:9, :local],
    }


def f_kernel(at, first, *refs):
    flag_ref, x_hbm, table_ref = refs[:3]
    refs = refs[3:]
    hbm = dict(zip(WEIGHTS, refs[:4]))
    refs = refs[4:]
    if first:
        vec_hbm = dict(zip(VECTORS, refs[:8]))
        refs = refs[8:]
        out_ref, pack_ref = refs[:2]
        refs = refs[2:]
    else:
        pack_ref, out_ref = refs[:2]
        refs = refs[2:]
    w = dict(zip(WEIGHTS, refs[:4]))
    mixed, active, x_ref, sems = refs[4:8]
    loads = Loads(sems)
    loads.start("x", x_hbm.at[at], x_ref)
    if first:
        vec_ref = dict(zip(VECTORS, refs[8:]))
        for name in VECTORS:
            loads.start(name, vec_hbm[name], vec_ref[name])
    for name in ("wqkv", "wup", "wout", "wdown"):
        loads.weight(name, hbm, w)
    width, (local, hidden) = x_ref.shape[1], (mixed.shape[1], active.shape[1])
    if first:
        for name in VECTORS:
            loads.wait(name)
        for i, name in enumerate(("g1", "b1", "g2", "b2")):
            pack_ref[i : i + 1, :width] = vec_ref[name][...].astype(F32)
        extra = vec_ref["bout"][...].astype(F32) + vec_ref["bdown"][...].astype(F32)
        pack_ref[4:5, :width] = jnp.where(flag_ref[1] == 0, extra, jnp.zeros_like(extra))
        pack_ref[5:6, :hidden] = vec_ref["bup"][...].astype(F32)
        pack_ref[6:9, :local] = vec_ref["bqkv"][...].astype(F32)
    vec = unpacked(pack_ref, width, local, hidden)

    def put(name, value, sl=slice(None)):
        if name == "mixed":
            mixed[:, sl] = value
        if name == "g":
            active[:, sl] = value

    loads.wait("x")
    forward_part(x_ref[...], vec, table_ref, w, loads.wait, put)
    out_ref[...] = output_part(mixed, active, vec, w, loads.wait)


def fb_kernel(at, *refs):
    flag_ref, x_hbm, dy_hbm, arrived_ref, table_ref, pack_ref = refs[:6]
    hbm = dict(zip(WEIGHTS, refs[6:10]))
    names = ("dx", "source") + SAVED
    outs = dict(zip(names, refs[10 : 10 + len(names)]))
    refs = refs[10 + len(names) :]
    held = dict(zip(names, refs[: len(names)]))
    refs = refs[len(names) :]
    w = dict(zip(WEIGHTS, refs[:4]))
    du, dqkv, x_ref, dy_ref, sems, out_sems = refs[4:]
    loads, stores = Loads(sems), Loads(out_sems)
    loads.start("x", x_hbm.at[at], x_ref)
    loads.weight("wqkv", hbm, w)
    loads.weight("wup", hbm, w)
    loads.start("dy", dy_hbm.at[at], dy_ref)
    loads.weight("wdown", hbm, w)
    loads.weight("wout", hbm, w)
    held_too = dict(held, du=du, dqkv=dqkv)

    def put(name, value, sl=slice(None)):
        ref = held_too[name]
        value = value() if callable(value) else value
        ref[:, sl] = value.astype(ref.dtype)

    width, (local, hidden) = x_ref.shape[1], (dqkv.shape[1] // 3, du.shape[1])
    vec = unpacked(pack_ref, width, local, hidden)
    loads.wait("x")
    x = jnp.where(flag_ref[0] == 0, x_ref[...], arrived_ref[...])
    held["source"][...] = x
    forward_part(x, vec, table_ref, w, loads.wait, put)
    for name in ("source",) + SAVED:
        stores.start(name, held[name], outs[name])
    loads.wait("dy")
    backward_part(dy_ref[...], held, table_ref, w, loads.wait, put)
    held["dx"][...] = norm_back(x, du, dqkv, local, vec, w, loads.wait)[0]
    stores.start("dx", held["dx"], outs["dx"])
    for name in names:
        stores.wait(name)


def b_kernel(at, first, last, *refs):
    flag_ref, x_ref, dy_hbm, arrived_ref, table_ref, pack_ref = refs[:6]
    hbm = dict(zip(WEIGHTS, refs[6:10]))
    saved = dict(zip(("q", "k", "v", "prob", "gp"), refs[10:15]))
    refs = refs[15:]
    if last:
        refs = refs[2:]
    if not first:
        own_before, other_before = refs[:2]
        refs = refs[2:]
    dx_ref, du, dqkv, own, other, dy_out = refs[:6]
    w = dict(zip(WEIGHTS, refs[6:10]))
    dy_ref, sems = refs[10:]
    loads = Loads(sems)
    loads.start("dy", dy_hbm.at[at], dy_ref)
    for name in ("wdown", "wout", "wup", "wqkv"):
        loads.weight(name, hbm, w)
    kept = {"du": du, "dqkv": dqkv}

    def put(name, value, sl=slice(None)):
        kept[name][:, sl] = value

    x = x_ref[...]
    loads.wait("dy")
    dy = jnp.where(flag_ref[0] == 0, arrived_ref[...], dy_ref[...])
    dy_out[...] = dy
    width, (local, hidden) = x.shape[1], (dqkv.shape[1] // 3, du.shape[1])
    vec = unpacked(pack_ref, width, local, hidden)
    backward_part(dy, saved, table_ref, w, loads.wait, put)
    dx, d_first, d_second, unit = norm_back(x, du, dqkv, local, vec, w, loads.wait)
    dx_ref[...] = dx
    if first:
        own[...] = jnp.zeros_like(own)
        other[...] = jnp.zeros_like(other)
    else:
        own[...] = own_before[...]
        other[...] = other_before[...]
    low = flag_ref[1] == 0
    terms = (d_first * unit, d_first, d_second * unit, d_second, dy.astype(F32))
    for i, term in enumerate(terms):
        total = jnp.sum(term, axis=0, keepdims=True)
        front, back = total[:, :local], total[:, local:]
        own[i : i + 1] += jnp.where(low, front, back)
        if i < 4:
            other[i : i + 1] += jnp.where(low, back, front)
    line = 5
    for ref in (dqkv, du):
        for c in range(0, ref.shape[1], local):
            own[line : line + 1] += jnp.sum(ref[:, c : c + local].astype(F32), axis=0, keepdims=True)
            line += 1


def deal(theirs, mine, place, at, core, value, share):
    for z in range(value.shape[0] // (2 * share)):
        front = value[2 * z * share : (2 * z + 1) * share]
        back = value[(2 * z + 1) * share : (2 * z + 2) * share]
        theirs[place + z, at : at + share] = jnp.where(core == 0, back, front)
        mine[place + z, at : at + share] = jnp.where(core == 0, front, back)


def outer(pieces, sl, right):
    return dot_tn(jnp.concatenate([piece[:, sl] for piece in pieces], axis=0), right).astype(BF)


def down_kernel(chips, micro, *refs):
    flag_ref, dy_hbm, arrived_ref = refs[:3]
    before = refs[3 : 2 + micro]
    refs = refs[2 + micro :]
    active, mixed = refs[:micro], refs[micro : 2 * micro]
    theirs, mine, dy_ref, sem = refs[2 * micro :]
    copy = pltpu.make_async_copy(dy_hbm.at[micro - 1], dy_ref, sem)
    copy.start()
    copy.wait()
    core = flag_ref[2]
    last = jnp.where(flag_ref[0] == 0, arrived_ref[...], dy_ref[...])
    dy = jnp.concatenate([ref[...] for ref in before] + [last], axis=0)
    hidden, local = active[0].shape[1], mixed[0].shape[1]
    share, step = hidden // (2 * chips), hidden // chips
    for z in range(chips):
        deal(theirs, mine, z, 0, core, outer(active, slice(z * step, (z + 1) * step), dy), share)
    deal(theirs, mine, 0, share, core, outer(mixed, slice(0, local), dy), local // (2 * chips))


def up_kernel(chips, micro, *refs):
    flag_ref = refs[0]
    a2, du, (theirs, mine) = refs[1 : 1 + micro], refs[1 + micro : 1 + 2 * micro], refs[1 + 2 * micro :]
    right = jnp.concatenate([ref[...] for ref in du], axis=0)
    width = a2[0].shape[1]
    share = width // (2 * chips)
    step = width // 2
    for j in range(2):
        value = outer(a2, slice(j * step, (j + 1) * step), right)
        deal(theirs, mine, j * chips // 2, 0, flag_ref[2], value, share)


def qkv_kernel(chips, micro, *refs):
    flag_ref = refs[0]
    a1, dqkv = refs[1 : 1 + micro], refs[1 + micro : 1 + 2 * micro]
    own, got, theirs, mine = refs[1 + 2 * micro :]
    width, local = a1[0].shape[1], own.shape[1]
    share = width // (2 * chips)
    step = width // 2
    for t in range(3):
        right = jnp.concatenate([ref[:, t * local : (t + 1) * local] for ref in dqkv], axis=0)
        for j in range(2):
            value = outer(a1, slice(j * step, (j + 1) * step), right)
            deal(theirs, mine, j * chips // 2, t * share, flag_ref[2], value, share)
    half = got.shape[0]
    lines = jnp.concatenate([own[:half] + got[...], own[half:]], axis=0).astype(BF)
    for z in range(chips):
        theirs[z, 3 * share :] = lines
        mine[z, 3 * share :] = lines


def o_kernel(micro, *refs):
    mixed_refs, active_refs = refs[:micro], refs[micro : 2 * micro]
    pack_ref, wout_hbm, wdown_hbm, out_ref, wout, wdown, mixed, active, sems = refs[2 * micro :]
    loads = Loads(sems)
    hbm, w = {"wout": wout_hbm, "wdown": wdown_hbm}, {"wout": wout, "wdown": wdown}
    loads.weight("wout", hbm, w)
    loads.weight("wdown", hbm, w)
    rows = mixed_refs[0].shape[0]
    for m in range(micro):
        mixed[m * rows : (m + 1) * rows] = mixed_refs[m][...]
        active[m * rows : (m + 1) * rows] = active_refs[m][...]
    vec = unpacked(pack_ref, wout.shape[1], wout.shape[0], wdown.shape[0])
    out_ref[...] = output_part(mixed, active, vec, w, loads.wait)


def add_kernel(at, x_hbm, one_ref, two_ref, out_ref, x_ref, sems):
    loads = Loads(sems)
    loads.start("x", x_hbm.at[at], x_ref)
    loads.wait("x")
    whole = x_ref[...].astype(F32) + (one_ref[...].astype(F32) + two_ref[...].astype(F32))
    out_ref[...] = whole.astype(BF)


VM = pl.BlockSpec(memory_space=pltpu.VMEM)
SM = pl.BlockSpec(memory_space=pltpu.SMEM)
HB = pl.BlockSpec(memory_space=pltpu.HBM)


def scratch_like(arrays):
    return [pltpu.VMEM(a.shape, a.dtype) for a in arrays]


def cost(ws, rows, passes):
    size = sum(math.prod(a.shape) for a in ws)
    return pl.CostEstimate(flops=2 * size * rows * passes, bytes_accessed=2 * size, transcendentals=0)


def params(mib):
    return pltpu.CompilerParams(vmem_limit_bytes=mib * 2**20)


def call_add(at, xs, one, two):
    rows, width = one.shape
    return pl.pallas_call(
        functools.partial(add_kernel, at),
        out_shape=jax.ShapeDtypeStruct((rows, width), BF),
        in_specs=[HB, VM, VM],
        out_specs=VM,
        scratch_shapes=[pltpu.VMEM((rows, width), BF), pltpu.SemaphoreType.DMA((1,))],
        compiler_params=params(8),
        cost_estimate=pl.CostEstimate(flops=rows * width * 2, bytes_accessed=rows * width * 8, transcendentals=0),
    )(xs, one, two)


def call_f(at, first, flags, xs, table, ws, vecs):
    rows, width = xs.shape[1:]
    local, hidden = ws[1].shape[0], ws[3].shape[0]
    out = jax.ShapeDtypeStruct((rows, width), BF)
    pack = jax.ShapeDtypeStruct((16, hidden), F32)
    scratch = scratch_like(ws) + [
        pltpu.VMEM((rows, local), BF),
        pltpu.VMEM((rows, hidden), BF),
        pltpu.VMEM((rows, width), BF),
        pltpu.SemaphoreType.DMA((24,)),
    ]
    return pl.pallas_call(
        functools.partial(f_kernel, at, first),
        out_shape=[out, pack] if first else out,
        in_specs=[SM, HB, VM] + [HB] * 4 + ([HB] * 8 if first else [VM]),
        out_specs=[VM, VM] if first else VM,
        scratch_shapes=scratch + (scratch_like(vecs) if first else []),
        compiler_params=params(60),
        cost_estimate=cost(ws, rows, 1),
    )(flags, xs, table, *ws, *vecs)


def call_fb(at, flags, xs, cots, arrived, table, pack, ws):
    rows, width = arrived.shape
    local, hidden = ws[1].shape[0], ws[3].shape[0]
    shape = jax.ShapeDtypeStruct
    outs = [shape((rows, width), BF)] * 4
    outs += [shape((rows, local), BF)] * 3
    outs += [
        shape((rows, 2 * rows * local // LANES), F32),
        shape((rows, local), BF),
        shape((rows, hidden), BF),
        shape((rows, hidden), F32),
    ]
    return pl.pallas_call(
        functools.partial(fb_kernel, at),
        out_shape=outs,
        in_specs=[SM, HB, HB, VM, VM, VM] + [HB] * 4,
        out_specs=[HB] * len(outs),
        scratch_shapes=scratch_like(outs)
        + scratch_like(ws)
        + [
            pltpu.VMEM((rows, hidden), BF),
            pltpu.VMEM((rows, 3 * local), BF),
            pltpu.VMEM((rows, width), BF),
            pltpu.VMEM((rows, width), BF),
            pltpu.SemaphoreType.DMA((16,)),
            pltpu.SemaphoreType.DMA((len(outs),)),
        ],
        compiler_params=params(60),
        cost_estimate=cost(ws, rows, 2),
    )(flags, xs, cots, arrived, table, pack, *ws)


def call_b(at, flags, x, cots, arrived, table, pack, ws, saved, after, before):
    rows, width = x.shape
    local, hidden = ws[1].shape[0], ws[3].shape[0]
    shape = jax.ShapeDtypeStruct
    outs = [
        shape((rows, width), BF),
        shape((rows, hidden), BF),
        shape((rows, 3 * local), BF),
        shape((16, local), F32),
        shape((8, local), F32),
        shape((rows, width), BF),
    ]
    return pl.pallas_call(
        functools.partial(b_kernel, at, not before, bool(after)),
        out_shape=outs,
        in_specs=[SM, VM, HB, VM, VM, VM] + [HB] * 4 + [VM] * 5 + [HB] * len(after) + [VM] * len(before),
        out_specs=[VM] * len(outs),
        scratch_shapes=scratch_like(ws) + [pltpu.VMEM((rows, width), BF), pltpu.SemaphoreType.DMA((16,))],
        compiler_params=params(60),
        cost_estimate=cost(ws, rows, 1),
    )(flags, x, cots, arrived, table, pack, *ws, *saved, *after, *before)


def call_blocks(kernel, flags, operands, specs, block, flops, scratch=()):
    outs = [jax.ShapeDtypeStruct(block, BF)] * 2
    return pl.pallas_call(
        kernel,
        out_shape=outs,
        in_specs=[SM] + specs,
        out_specs=[VM] * 2,
        scratch_shapes=list(scratch),
        compiler_params=params(60),
        cost_estimate=pl.CostEstimate(flops=flops, bytes_accessed=4 * math.prod(block), transcendentals=0),
    )(flags, *operands)


def call_o(mixed, active, pack, ws):
    micro, (rows, local) = len(mixed), mixed[0].shape
    hidden, width = ws[3].shape
    total = micro * rows
    return pl.pallas_call(
        functools.partial(o_kernel, micro),
        out_shape=jax.ShapeDtypeStruct((total, width), BF),
        in_specs=[VM] * (2 * micro + 1) + [HB] * 2,
        out_specs=VM,
        scratch_shapes=[
            pltpu.VMEM((local, width), BF),
            pltpu.VMEM((hidden, width), BF),
            pltpu.VMEM((total, local), BF),
            pltpu.VMEM((total, hidden), BF),
            pltpu.SemaphoreType.DMA((8,)),
        ],
        compiler_params=params(60),
        cost_estimate=cost((ws[1], ws[3]), total, 1),
    )(*mixed, *active, pack, ws[1], ws[3])


def swap(value):
    return lax.ppermute(value, "tensor", [(0, 1), (1, 0)])


def joined(one, two):
    return (one.astype(F32) + two.astype(F32)).astype(BF)


class Line:
    def __init__(self, theirs, mine, at):
        self.chips = mine.shape[0]
        self.place = at // 2
        parts = 2 * self.chips
        got = lax.ppermute(theirs, "dp", [(i, i ^ 1) for i in range(parts)])
        self.mine, self.got = mine, got
        self.right = self.left = None
        self.first = None
        self.sent = 0

    def block(self, index):
        index = jnp.clip(index, 0, self.chips - 1)
        one = lax.dynamic_index_in_dim(self.mine, index, 0, keepdims=False)
        two = lax.dynamic_index_in_dim(self.got, index, 0, keepdims=False)
        return one.astype(F32) + two.astype(F32)

    def step(self):
        self.sent += 1
        step, chips = self.sent, self.chips
        up = self.block(self.place + chips - step)
        down = self.block(self.place - chips + step)
        if self.right is not None:
            up = up + self.right.astype(F32)
            down = down + self.left.astype(F32)
        up, down = up.astype(BF), down.astype(BF)
        pairs = [(2 * z + c, 2 * z + 2 + c) for z in range(step) for c in range(2)]
        self.right = lax.ppermute(up, "dp", pairs)
        pairs = [(2 * z + c, 2 * z - 2 + c) for z in range(chips - step, chips) for c in range(2)]
        self.left = lax.ppermute(down, "dp", pairs)
        return [up, down]

    def result(self):
        while self.sent < self.chips - 1:
            self.step()
        return self.block(self.place) + (self.right.astype(F32) + self.left.astype(F32))


def wide(pieces, others):
    left, right = jnp.concatenate(pieces, axis=0), jnp.concatenate(others, axis=0)
    return jnp.einsum("ta,tb->ab", left, right, preferred_element_type=F32).astype(BF)


def scattered(blocks):
    parts, rows, columns = blocks.shape
    return lax.psum_scatter(blocks.reshape(parts * rows, columns), "dp", scatter_dimension=0, tiled=True).astype(F32)


def per_device(inputs, cotangent, g1, b1, g2, b2, w_qkv, b_qkv, w_out, b_out, w_up, b_up, w_down, b_down):
    section = lax.axis_index("section")
    owner = lax.axis_index("tensor")
    dp_at = lax.axis_index("dp")
    parts = lax.axis_size("dp")
    micro, seqs, length, width = inputs.shape
    rows = seqs * length
    local, hidden = w_out.shape[1], w_up.shape[2]
    flags = jnp.stack([section, owner, dp_at % 2]).astype(jnp.int32)
    table = jnp.asarray(rope_tables(length))
    vecs = (g1, b1, g2, b2, b_qkv[0], b_out, b_up, b_down)
    ws = (w_qkv[0].transpose(1, 0, 2), w_out[0], w_up[0], w_down[0])
    xs = inputs.reshape(micro, rows, width)
    cots = cotangent.reshape(micro, rows, width)
    lined = parts <= 8
    chips = parts // 2

    arrivals = []
    for m in range(micro):
        if m == 0:
            part, pack = call_f(m, True, flags, xs, table, ws, vecs)
        else:
            part = call_f(m, False, flags, xs, table, ws, (pack,))
        whole = call_add(m, xs, part, swap(part))
        arrivals.append(lax.ppermute(whole, "section", [(0, 1)]))
    kept, sources, backs = [], [], []
    for m in range(micro):
        dx, source, *saved = call_fb(m, flags, xs, cots, arrivals[m], table, pack, ws)
        whole = call_add(m, cots, dx, swap(dx))
        backs.append(lax.ppermute(whole, "section", [(1, 0)]))
        kept.append(dict(zip(SAVED, saved)))
        sources.append(source)
    a1, a2, mixed, active = ([kept[m][n] for m in range(micro)] for n in ("a1", "a2", "mixed", "g"))

    grads, dus, dqkvs, ups = [], [], [], []
    before, after = (), ()
    for m in range(micro):
        if m == micro - 1 and lined:
            block = (chips, hidden // parts + local // parts, width)
            theirs, mine = call_blocks(
                functools.partial(down_kernel, chips, micro),
                flags,
                (cots, backs[m], *ups, *active, *mixed),
                [HB] + [VM] * (3 * micro),
                block,
                2 * micro * rows * width * (hidden + local),
                [pltpu.VMEM((rows, width), BF), pltpu.SemaphoreType.DMA],
            )
            line_down = Line(theirs, mine, dp_at)
            after = tuple(line_down.step())
        saved = [kept[m][n] for n in ("q", "k", "v", "prob", "gp")]
        dx, du, dqkv, own, other, dy = call_b(
            m, flags, sources[m], cots, backs[m], table, pack, ws, saved, after, before
        )
        before = (own, other)
        grads.append(dx)
        dus.append(du)
        dqkvs.append(dqkv)
        ups.append(dy)
    got = swap(other)
    share = width // parts
    if lined:
        flops = 2 * micro * rows * width
        theirs, mine = call_blocks(
            functools.partial(up_kernel, chips, micro),
            flags,
            (*a2, *dus),
            [VM] * (2 * micro),
            (chips, share, hidden),
            flops * hidden,
        )
        line_up = Line(theirs, mine, dp_at)
        theirs, mine = call_blocks(
            functools.partial(qkv_kernel, chips, micro),
            flags,
            (*a1, *dqkvs, own, got),
            [VM] * (2 * micro + 2),
            (chips, 3 * share + own.shape[0], local),
            flops * 3 * local,
        )
        line_qkv = Line(theirs, mine, dp_at)
        d_both, d_wup, last = line_down.result(), line_up.result(), line_qkv.result()
    else:
        d_wdown = wide(active, ups).reshape(parts, -1, width)
        d_wout = wide(mixed, ups).reshape(parts, -1, width)
        d_both = scattered(jnp.concatenate([d_wdown, d_wout], axis=1))
        d_wup = scattered(wide(a2, dus).reshape(parts, -1, hidden))
        d_wqkv = wide(a1, dqkvs).reshape(parts, share, 3, local).transpose(0, 2, 1, 3)
        lines = jnp.concatenate([own[: got.shape[0]] + got, own[got.shape[0] :]]).astype(BF)
        lines = jnp.broadcast_to(lines[None], (parts,) + lines.shape)
        last = scattered(jnp.concatenate([d_wqkv.reshape(parts, 3 * share, local), lines], axis=1))
    down_rows = hidden // parts
    d_wdown, d_wout = d_both[:down_rows], d_both[down_rows:]
    d_wqkv = last[: 3 * share].reshape(3, share, local).transpose(1, 0, 2)
    lines = last[3 * share :]
    d_vec = lax.dynamic_slice(lines, (0, dp_at * (local // parts)), (8, local // parts))
    up_lines = lines[8 : 8 + hidden // local].reshape(1, hidden)
    d_bup = lax.dynamic_slice_in_dim(up_lines, dp_at * down_rows, down_rows, 1)

    part = call_o(mixed, active, pack, ws)
    other_part = swap(part)
    section_out = jnp.concatenate(sources, axis=0).astype(F32) + (part.astype(F32) + other_part.astype(F32))
    input_grad = jnp.stack([ups[m].astype(F32) + (grads[m].astype(F32) + swap(grads[m]).astype(F32)) for m in range(micro)])
    return (
        section_out.astype(BF).reshape(1, micro, seqs, length, width),
        input_grad.reshape(1, micro, seqs, length, width),
        d_vec[0:1],
        d_vec[1:2],
        d_vec[2:3],
        d_vec[3:4],
        d_wqkv[None],
        d_vec[5:8][None],
        d_wout[None],
        d_vec[4:5],
        d_wup[None],
        d_bup,
        d_wdown[None],
        d_vec[4:5],
    )


def solution(mesh):
    return jax.shard_map(
        per_device,
        mesh=mesh,
        in_specs=(
            P(None, "dp", None, None),
            P(None, "dp", None, None),
            P("section", None),
            P("section", None),
            P("section", None),
            P("section", None),
            P("section", None, None, "tensor"),
            P("section", None, "tensor"),
            P("section", "tensor", None),
            P("section", None),
            P("section", None, "tensor"),
            P("section", "tensor"),
            P("section", "tensor", None),
            P("section", None),
        ),
        out_specs=(
            P("section", None, "dp", None, None),
            P("section", None, "dp", None, None),
            P("section", ("tensor", "dp")),
            P("section", ("tensor", "dp")),
            P("section", ("tensor", "dp")),
            P("section", ("tensor", "dp")),
            P("section", "dp", None, "tensor"),
            P("section", None, ("tensor", "dp")),
            P("section", ("tensor", "dp"), None),
            P("section", ("tensor", "dp")),
            P("section", "dp", "tensor"),
            P("section", ("tensor", "dp")),
            P("section", ("tensor", "dp"), None),
            P("section", ("tensor", "dp")),
        ),
        check_vma=False,
    )
```

time: 241 us -> 185 us (0.77)
  blocking collectives: 58.6 us -> 0 us
  starting transfers between devices: 17.2 us -> 63.4 us
  Pallas kernels: 33.3 us -> 68.1 us
  waiting for transfers between devices: 60.2 us -> 25.6 us
  local copies, waits for them, and re-layouts: 36.3 us -> 9.86 us
  between operations: 14.5 us -> 1.32 us
  matrix products: 8.47 us -> 0 us
  other arithmetic: 11.6 us -> 15.5 us
    psum x1 -> x0, blocking collectives: 58.6 us -> none  [per_device(): lax.psum(jnp.concatenate([sum_d.reshape(-1), flat]), ('tensor', 'dp'))]
    ppermute x4 -> x25, starting transfers between devices: 7.46 us -> 54 us  [the longest x9 35.5 us: step(): self.right = lax.ppermute(up, 'dp', pairs)]
    pallas_call x6 -> x14, Pallas kernels: 33.3 us -> 68.1 us  [the longest x2 19.7 us: call_fb(): pl.pallas_call(functools.partial(fb_kernel, at), out_shape=outs, in_specs...]
    reduce_scatter x4 -> x0, waiting for transfers between devices: 27 us -> none  [scatter(): lax.psum_scatter(value, 'dp', scatter_dimension=0, tiled=True).astype(F32)]
    unnamed x164 -> x46, local copies, waits for them, and re-layouts: 31 us -> 6.29 us
    ppermute x8, waiting for transfers between devices: 20.9 us -> 5.01 us  [swap(): return lax.ppermute(value, 'tensor', [(0, 1), (1, 0)])]
    dot_general x4 -> x0, matrix products: 8.47 us -> none  [outer(): return jnp.einsum('ta,tb->ab', a, b, preferred_element_type=F32).astype(BF)]
    ppermute x4 -> x25, waiting for transfers between devices: 12.2 us -> 20.6 us  [the longest x9 10.1 us: step(): self.left = lax.ppermute(down, 'dp', pairs)]
  transfers between devices with their start and end apart: 16 -> 33, of which waited for: 12 -> 8; matrix products, arithmetic and copies ran while one was open for 7% -> 10% of each run, Pallas kernels for 10% -> 31%
where the time goes in v1:
time: 185 us; the launch traced here: 184 us
  Pallas kernels  68.1 us (37%)
  starting transfers between devices  63.4 us (34%)
  waiting for transfers between devices  25.6 us (14%)
  other arithmetic  15.5 us (8%)
  local copies, waits for them, and re-layouts  9.86 us (5%)
    ppermute x9, starting transfers between devices, step(): self.right = lax.ppermute(up, 'dp', pairs)  35.5 us
    pallas_call x2, Pallas kernels, call_fb(): pl.pallas_call(functools.partial(fb_kernel, at), out_shape=outs, in_specs...  19.7 us
    pallas_call x2, Pallas kernels, call_b(): pl.pallas_call(functools.partial(b_kernel, at, not before, bool(after)),...  18.1 us
    pallas_call x2, Pallas kernels, call_f(): pl.pallas_call(functools.partial(f_kernel, at, first), out_shape=[out, pa...  12.3 us
    pallas_call x3, Pallas kernels, call_blocks(): pl.pallas_call(kernel, out_shape=outs, in_specs=[SM] + specs, out_specs=[...  11.8 us
    ppermute x9, waiting for transfers between devices, step(): self.left = lax.ppermute(down, 'dp', pairs)  10.1 us
    ppermute x8, starting transfers between devices, swap(): return lax.ppermute(value, 'tensor', [(0, 1), (1, 0)])  9.47 us
    ppermute x9, waiting for transfers between devices, step(): self.right = lax.ppermute(up, 'dp', pairs)  8.74 us
  transfers between devices with their start and end apart: 33, of which 8 were waited for; matrix products, arithmetic and copies ran while one was open for 10% of the time, Pallas kernels for 31%

profile of v1, /device:TPU:0, one launch (start us, length us, event | category | flops | bytes accessed | tf_op | source)
XLA Modules:
  0.0 183.8 jit_solution(12007008534963832452)
XLA Ops:
  1.2 6.1 %shard_map.254 = (bf16[128,768]{1,0:T(8,128)(2,1)}, f32[16,1536]{1,0:T(8,128)}) custom-call(s32[3]{0:T(128)} %pad_add_fusion.refs_0_, bf16[2,128,768]{2,1,0:T(8,128)(2,1)} %bitcast.108, f32[3,128,128]{2,1,0:T(8,128)} %constant.165.clone.refs_2_.refs_4_, bf16[3,768,384]{2,1,0:T(8,128)(2,1)} %bitcast.134, bf16[384,768]{1,0:T(8,128)(2,1)} %bitcast.140, ...), custom_call_target="tpu_custom_call" | custom-call | flops 905969664 | bytes 7077888 | tf_op jit(solution)/shard_map/pallas_call | solution.py:492
  7.4 3.0 %collective-permute-start = (bf16[128,768]{1,0:T(8,128)(2,1)}, bf16[128,768]{1,0:T(8,128)(2,1)S(1)}, u32[]{:S(2)}, u32[]{:S(2)}) collective-permute-start(bf16[128,768]{1,0:T(8,128)(2,1)} %get-tuple-element.56.one_ref), channel_id=1, source_target_pairs={{0,8},{8,0},{1,9},{9,1},{2,10},{10,2},{3,11},{11,3},{4,12},{12,4},... | collective-permute-start | bytes 589832 | tf_op jit(solution)/shard_map/ppermute | solution.py:593
  10.4 6.2 %shard_map.257.one_ref = bf16[128,768]{1,0:T(8,128)(2,1)} custom-call(s32[3]{0:T(128)} %pad_add_fusion.refs_0_, bf16[2,128,768]{2,1,0:T(8,128)(2,1)} %bitcast.109, f32[3,128,128]{2,1,0:T(8,128)} %constant.165.clone.refs_2_.refs_4_, bf16[3,768,384]{2,1,0:T(8,128)(2,1)} %bitcast.135, bf16[384,768]{1,0:T(8,128)(2,1)} %bitcast.141, bf16[768,1536]{1,0:T(8,128)(2,1)} %bitcast.129, ...), custom_call_target="tpu_custom_call" | custom-call | flops 905969664 | bytes 7077888 | tf_op jit(solution)/shard_map/pallas_call | solution.py:492
  17.1 3.9 %collective-permute-start.1 = (bf16[128,768]{1,0:T(8,128)(2,1)S(1)}, bf16[128,768]{1,0:T(8,128)(2,1)S(1)}, u32[]{:S(2)}, u32[]{:S(2)}) collective-permute-start(bf16[128,768]{1,0:T(8,128)(2,1)S(1)} %shard_map.255), channel_id=1, source_target_pairs={{0,16},{1,17},{2,18},{3,19},{4,20},{5,21},{6,22},{7,23},{8,24},{9,... | collective-permute-start | bytes 589832 | tf_op jit(solution)/shard_map/ppermute | solution.py:672
  21.0 2.3 %collective-permute-done.2.two_ref = bf16[128,768]{1,0:T(8,128)(2,1)S(1)} collective-permute-done((bf16[128,768]{1,0:T(8,128)(2,1)}, bf16[128,768]{1,0:T(8,128)(2,1)S(1)}, u32[]{:S(2)}, u32[]{:S(2)}) %collective-permute-start.2) | collective-permute-done | bytes 196640 | tf_op jit(solution)/shard_map/ppermute | solution.py:593
  23.2 0.9 copy-done.2
  24.5 3.6 %collective-permute-start.3 = (bf16[128,768]{1,0:T(8,128)(2,1)S(1)}, bf16[128,768]{1,0:T(8,128)(2,1)S(1)}, u32[]{:S(2)}, u32[]{:S(2)}) collective-permute-start(bf16[128,768]{1,0:T(8,128)(2,1)S(1)} %shard_map.258), channel_id=1, source_target_pairs={{0,16},{1,17},{2,18},{3,19},{4,20},{5,21},{6,22},{7,23},{8,24},{9,... | collective-permute-start | bytes 589832 | tf_op jit(solution)/shard_map/ppermute | solution.py:672
  28.8 9.9 %shard_map.256 = (bf16[128,768]{1,0:T(8,128)(2,1)}, bf16[128,768]{1,0:T(8,128)(2,1)}, bf16[128,768]{1,0:T(8,128)(2,1)}, bf16[128,768]{1,0:T(8,128)(2,1)}, bf16[1...) custom-call(s32[3]{0:T(128)} %pad_add_fusion.refs_0_, ...), custom_call_target="tpu_custom_call" | custom-call | flops 1811939328 | bytes 7077888 | tf_op jit(solution)/shard_map/pallas_call | solution.py:515
  39.2 0.7 copy-done.16
  39.9 9.8 %shard_map.259 = (bf16[128,768]{1,0:T(8,128)(2,1)}, bf16[128,768]{1,0:T(8,128)(2,1)}, bf16[128,768]{1,0:T(8,128)(2,1)}, bf16[128,768]{1,0:T(8,128)(2,1)}, bf16[1...) custom-call(s32[3]{0:T(128)} %pad_add_fusion.refs_0_, ...), custom_call_target="tpu_custom_call" | custom-call | flops 1811939328 | bytes 7077888 | tf_op jit(solution)/shard_map/pallas_call | solution.py:515
  49.8 1.6 collective-permute-start.8
  51.7 1.3 collective-permute-start.6
  53.0 2.7 %collective-permute-done.8.two_ref = bf16[128,768]{1,0:T(8,128)(2,1)S(1)} collective-permute-done((bf16[128,768]{1,0:T(8,128)(2,1)}, bf16[128,768]{1,0:T(8,128)(2,1)S(1)}, u32[]{:S(2)}, u32[]{:S(2)}) %collective-permute-start.8) | collective-permute-done | bytes 196640 | tf_op jit(solution)/shard_map/ppermute | solution.py:593
  55.7 0.9 copy-done.4
  56.9 1.5 collective-permute-start.9
  58.5 1.7 collective-permute-done.6.refs_3_
  60.1 0.7 copy-done.18
  60.8 9.1 %shard_map.262 = (bf16[128,768]{1,0:T(8,128)(2,1)}, bf16[128,1536]{1,0:T(8,128)(2,1)}, bf16[128,1152]{1,0:T(8,128)(2,1)}, f32[16,384]{1,0:T(8,128)}, f32[8,384]{1,0:T(8,128)}, /*index=5*/bf16[128,768]{1,0:T(8,128)(2,1)}) custom-call(s32[3]{0:T(128)} %pad_add_fusion.refs_0_, bf16[128,768]{1,0:T(8,128)(2,1)} %get-tuple-element.58.refs_1_, ...), custom_call_target="tpu_custom_call" | custom-call | flops 905969664 | bytes 7077888 | tf_op jit(solution)/shard_map/pallas_call | solution.py:547
  69.9 0.7 copy-done.15
  70.6 4.8 %shard_map.264 = (bf16[4,240,768]{2,1,0:T(8,128)(2,1)}, bf16[4,240,768]{2,1,0:T(8,128)(2,1)}) custom-call(s32[3]{0:T(128)} %pad_add_fusion.refs_0_, bf16[2,128,768]{2,1,0:T(8,128)(2,1)} %bitcast.117, bf16[128,768]{1,0:T(8,128)(2,1)} %copy-done.15, bf16[128,768]{1,0:T(8,128)(2,1)} %get-tuple-element.70.refs_3_, ...), custom_call_target="tpu_custom_call" | custom-call | flops 754974720 | bytes 2949120 | tf_op jit(solution)/shard_map/pallas_call | solution.py:560
  75.5 4.9 %shard_map.260 = bf16[256,768]{1,0:T(8,128)(2,1)} custom-call(bf16[128,384]{1,0:T(8,128)(2,1)} %get-tuple-element.60.refs_0_.refs_6_, bf16[128,384]{1,0:T(8,128)(2,1)} %get-tuple-element.61.refs_1_.refs_7_, bf16[128,1536]{1,0:T(8,128)(2,1)} %get-tuple-element.62.refs_2_.refs_4_, bf16[128,1536]{1,0:T(8,128)(2,1)} %get-tuple-element.63.refs_3_.refs_5_, ...), custom_call_target="tpu_custom_call" | custom-call | flops 754974720 | bytes 2949120 | tf_op jit(solution)/shard_map/pallas_call | solution.py:575
  80.5 1.1 fusion.14
  81.6 9.1 %shard_map.265 = (bf16[128,768]{1,0:T(8,128)(2,1)}, bf16[128,1536]{1,0:T(8,128)(2,1)}, bf16[128,1152]{1,0:T(8,128)(2,1)}, f32[16,384]{1,0:T(8,128)}, f32[8,384]{1,0:T(8,128)}, /*index=5*/bf16[128,768]{1,0:T(8,128)(2,1)}) custom-call(s32[3]{0:T(128)} %pad_add_fusion.refs_0_, bf16[128,768]{1,0:T(8,128)(2,1)} %get-tuple-element.59.refs_1_, ...), custom_call_target="tpu_custom_call" | custom-call | flops 905969664 | bytes 7077888 | tf_op jit(solution)/shard_map/pallas_call | solution.py:547
  90.7 2.0 %collective-permute-start.12 = (f32[8,384]{1,0:T(8,128)}, f32[8,384]{1,0:T(8,128)S(1)}, u32[]{:S(2)}, u32[]{:S(2)}) collective-permute-start(f32[8,384]{1,0:T(8,128)} %get-tuple-element.89), channel_id=1, source_target_pairs={{0,8},{8,0},{1,9},{9,1},{2,10},{10,2},{3,11},{11,3},{4,12},{12,4},... | collective-permute-start | bytes 36872 | tf_op jit(solution)/shard_map/ppermute | solution.py:593
  92.8 4.2 %collective-permute-start.20 = (bf16[240,768]{1,0:T(8,128)(2,1)}, bf16[240,768]{1,0:T(8,128)(2,1)}, u32[]{:S(2)}, u32[]{:S(2)}) collective-permute-start(bf16[240,768]{1,0:T(8,128)(2,1)} %get-tuple-element.115.refs_15_), channel_id=1, source_target_pairs={{0,2},{1,3},{8,10},{9,11},{16,18},{17,19},{24,26},{25,27}} | collective-permute-start | bytes 1105928 | tf_op jit(solution)/shard_map/ppermute | solution.py:627
  97.7 3.4 %shard_map.266 = (bf16[4,304,384]{2,1,0:T(8,128)(2,1)}, bf16[4,304,384]{2,1,0:T(8,128)(2,1)}) custom-call(s32[3]{0:T(128)} %pad_add_fusion.refs_0_, bf16[128,768]{1,0:T(8,128)(2,1)} %get-tuple-element.84.refs_1_, bf16[128,768]{1,0:T(8,128)(2,1)} %get-tuple-element.85.refs_2_, bf16[128,1152]{1,0:T(8,128)(2,1)} %get-tuple-element.86.refs_3_, ...), custom_call_target="tpu_custom_call" | custom-call | flops 452984832 | bytes 1867776 | tf_op jit(solution)/shard_map/pallas_call | solution.py:560
  101.1 1.9 %add_convert_fusion = bf16[256,768]{1,0:T(8,128)(2,1)} fusion(bf16[256,768]{1,0:T(8,128)(2,1)} %collective-permute-done.4, bf16[256,768]{1,0:T(8,128)(2,1)S(1)} %copy-done.9, bf16[128,768]{1,0:T(8,128)(2,1)S(1)} %copy-done.11, bf16[128,768]{1,0:T(8,128)(2,1)S(1)} %copy-done.10), kind=kLoop, calls=%fused_computation.1 | loop fusion | flops 1769472 | bytes 1572864 | tf_op jit(solution)/shard_map/convert_element_type | solution.py:752
  103.1 1.0 add_bitcast_fusion.1
  104.0 0.7 collective-permute-start.23
  104.7 2.0 %collective-permute-start.11 = (bf16[128,768]{1,0:T(8,128)(2,1)}, bf16[128,768]{1,0:T(8,128)(2,1)S(1)}, u32[]{:S(2)}, u32[]{:S(2)}) collective-permute-start(bf16[128,768]{1,0:T(8,128)(2,1)} %get-tuple-element.83), channel_id=1, source_target_pairs={{0,8},{8,0},{1,9},{9,1},{2,10},{10,2},{3,11},{11,3},{4,12},{12,4},... | collective-permute-start | bytes 589832 | tf_op jit(solution)/shard_map/ppermute | solution.py:593
  106.7 3.6 %shard_map.267 = (bf16[4,96,1536]{2,1,0:T(8,128)(2,1)}, bf16[4,96,1536]{2,1,0:T(8,128)(2,1)}) custom-call(s32[3]{0:T(128)} %pad_add_fusion.refs_0_, bf16[128,768]{1,0:T(8,128)(2,1)} %get-tuple-element.92.refs_1_, bf16[128,768]{1,0:T(8,128)(2,1)} %get-tuple-element.93.refs_2_, bf16[128,1536]{1,0:T(8,128)(2,1)} %get-tuple-element.94.refs_3_, ...), custom_call_target="tpu_custom_call" | custom-call | flops 603979776 | bytes 2359296 | tf_op jit(solution)/shard_map/pallas_call | solution.py:560
  110.5 1.1 fusion.2
  111.6 1.4 collective-permute-start.21
  113.1 1.0 add_bitcast_fusion
  114.1 0.9 maximum_bitcast_fusion
  115.0 1.2 fusion.17
  116.2 4.1 %collective-permute-start.14 = (bf16[304,384]{1,0:T(8,128)(2,1)S(1)}, bf16[304,384]{1,0:T(8,128)(2,1)S(1)}, u32[]{:S(2)}, u32[]{:S(2)}) collective-permute-start(bf16[304,384]{1,0:T(8,128)(2,1)S(1)} %get-tuple-element.122), channel_id=1, source_target_pairs={{0,2},{1,3},{8,10},{9,11},{16,18},{17,19},{24,26},{25,27}} | collective-permute-start | bytes 700424 | tf_op jit(solution)/shard_map/ppermute | solution.py:627
  120.4 1.6 collective-permute-done.21
  122.3 0.7 collective-permute-start.24
  123.0 5.0 %collective-permute-start.22 = (bf16[240,768]{1,0:T(8,128)(2,1)S(1)}, bf16[240,768]{1,0:T(8,128)(2,1)S(1)}, u32[]{:S(2)}, u32[]{:S(2)}) collective-permute-start(bf16[240,768]{1,0:T(8,128)(2,1)S(1)} %get-tuple-element.112), channel_id=1, source_target_pairs={{0,2},{1,3},{2,4},{3,5},{4,6},{5,7},{8,10},{9,11},{10,12},{11,13},... | collective-permute-start | bytes 1105928 | tf_op jit(solution)/shard_map/ppermute | solution.py:627
  128.0 0.7 collective-permute-start.17
  128.7 1.0 fusion.11
  129.7 4.8 %collective-permute-start.15 = (bf16[304,384]{1,0:T(8,128)(2,1)S(1)}, bf16[304,384]{1,0:T(8,128)(2,1)S(1)}, u32[]{:S(2)}, u32[]{:S(2)}) collective-permute-start(bf16[304,384]{1,0:T(8,128)(2,1)S(1)} %fusion.11), channel_id=1, source_target_pairs={{0,2},{1,3},{2,4},{3,5},{8,10},{9,11},{10,12},{11,13},{16,18},{17,... | collective-permute-start | bytes 700424 | tf_op jit(solution)/shard_map/ppermute | solution.py:627
  134.7 4.1 %collective-permute-start.27 = (bf16[96,1536]{1,0:T(8,128)(2,1)S(1)}, bf16[96,1536]{1,0:T(8,128)(2,1)S(1)}, u32[]{:S(2)}, u32[]{:S(2)}) collective-permute-start(bf16[96,1536]{1,0:T(8,128)(2,1)S(1)} %get-tuple-element.118), channel_id=1, source_target_pairs={{0,2},{1,3},{8,10},{9,11},{16,18},{17,19},{24,26},{25,27}} | collective-permute-start | bytes 884744 | tf_op jit(solution)/shard_map/ppermute | solution.py:627
  138.9 1.3 collective-permute-start.25
  140.3 0.7 collective-permute-start.30
  140.9 1.0 collective-permute-done.15
  142.0 1.2 fusion.12
  143.2 0.7 collective-permute-start.18
  143.9 2.8 %collective-permute-done.27 = bf16[96,1536]{1,0:T(8,128)(2,1)S(1)} collective-permute-done((bf16[96,1536]{1,0:T(8,128)(2,1)S(1)}, bf16[96,1536]{1,0:T(8,128)(2,1)S(1)}, u32[]{:S(2)}, u32[]{:S(2)}) %collective-permute-start.27) | collective-permute-done | bytes 294944 | tf_op jit(solution)/shard_map/ppermute | solution.py:627
  146.7 4.4 %collective-permute-start.16 = (bf16[304,384]{1,0:T(8,128)(2,1)S(1)}, bf16[304,384]{1,0:T(8,128)(2,1)S(1)}, u32[]{:S(2)}, u32[]{:S(2)}) collective-permute-start(bf16[304,384]{1,0:T(8,128)(2,1)S(1)} %get-tuple-element.120), channel_id=1, source_target_pairs={{0,2},{1,3},{2,4},{3,5},{4,6},{5,7},{8,10},{9,11},{10,12},{11,13},... | collective-permute-start | bytes 700424 | tf_op jit(solution)/shard_map/ppermute | solution.py:627
  151.2 2.4 %collective-permute-start.28 = (bf16[96,1536]{1,0:T(8,128)(2,1)S(1)}, bf16[96,1536]{1,0:T(8,128)(2,1)S(1)}, u32[]{:S(2)}, u32[]{:S(2)}) collective-permute-start(bf16[96,1536]{1,0:T(8,128)(2,1)S(1)} %fusion.6), channel_id=1, source_target_pairs={{0,2},{1,3},{2,4},{3,5},{8,10},{9,11},{10,12},{11,13},{16,18},{17,... | collective-permute-start | bytes 884744 | tf_op jit(solution)/shard_map/ppermute | solution.py:627
  153.9 0.9 slice_bitcast_fusion
  154.7 0.7 slice_bitcast_fusion.1
  155.4 1.0 fusion.10
  156.4 1.3 collective-permute-start.19
  157.7 3.3 %collective-permute-done.28 = bf16[96,1536]{1,0:T(8,128)(2,1)S(1)} collective-permute-done((bf16[96,1536]{1,0:T(8,128)(2,1)S(1)}, bf16[96,1536]{1,0:T(8,128)(2,1)S(1)}, u32[]{:S(2)}, u32[]{:S(2)}) %collective-permute-start.28) | collective-permute-done | bytes 294944 | tf_op jit(solution)/shard_map/ppermute | solution.py:627
  161.3 0.7 collective-permute-start.31
  161.9 5.0 %collective-permute-start.29 = (bf16[96,1536]{1,0:T(8,128)(2,1)S(1)}, bf16[96,1536]{1,0:T(8,128)(2,1)S(1)}, u32[]{:S(2)}, u32[]{:S(2)}) collective-permute-start(bf16[96,1536]{1,0:T(8,128)(2,1)S(1)} %get-tuple-element.116), channel_id=1, source_target_pairs={{0,2},{1,3},{2,4},{3,5},{4,6},{5,7},{8,10},{9,11},{10,12},{11,13},... | collective-permute-start | bytes 884744 | tf_op jit(solution)/shard_map/ppermute | solution.py:627
  167.0 1.1 bitcast_add_fusion.14
  168.2 0.8 slice.47
  169.7 1.3 collective-permute-start.32
  172.1 10.1 %collective-permute-done.32 = bf16[96,1536]{1,0:T(8,128)(2,1)S(1)} collective-permute-done((bf16[96,1536]{1,0:T(8,128)(2,1)S(1)}, bf16[96,1536]{1,0:T(8,128)(2,1)S(1)}, u32[]{:S(2)}, u32[]{:S(2)}) %collective-permute-start.32) | collective-permute-done | bytes 294944 | tf_op jit(solution)/shard_map/ppermute | solution.py:629
  182.2 1.0 fusion.8
  (90 shorter events, 8.0 us)
Async XLA Ops:
  7.4 9.3 %collective-permute-start = (bf16[128,768]{1,0:T(8,128)(2,1)}, bf16[128,768]{1,0:T(8,128)(2,1)S(1)}, u32[]{:S(2)}, u32[]{:S(2)}) collective-permute-start(bf16[128,768]{1,0:T(8,128)(2,1)} %get-tuple-element.56.one_ref), channel_id=1, source_target_pairs={{0,8},{8,0},{1,9},{9,1},{2,10},{10,2},{3,11},{11,3},{4,12},{12,4},... | collective-permute-start | bytes 589832 | tf_op jit(solution)/shard_map/ppermute | solution.py:593
  10.4 6.3 %copy-start = (bf16[2,1,128,768]{3,2,1,0:T(8,128)(2,1)S(1)}, bf16[2,1,128,768]{3,2,1,0:T(8,128)(2,1)}, u32[]{:S(2)}) copy-start(bf16[2,1,128,768]{3,2,1,0:T(8,128)(2,1)} %param.15) | copy-start | bytes 1179652
  10.4 6.3 %copy-start.5 = (bf16[128,768]{1,0:T(8,128)(2,1)S(1)}, bf16[128,768]{1,0:T(8,128)(2,1)}, u32[]{:S(2)}) copy-start(bf16[128,768]{1,0:T(8,128)(2,1)} %get-tuple-element.56.one_ref) | copy-start | bytes 589828
  16.6 6.6 %collective-permute-start.2 = (bf16[128,768]{1,0:T(8,128)(2,1)}, bf16[128,768]{1,0:T(8,128)(2,1)S(1)}, u32[]{:S(2)}, u32[]{:S(2)}) collective-permute-start(bf16[128,768]{1,0:T(8,128)(2,1)} %shard_map.257.one_ref), channel_id=1, source_target_pairs={{0,8},{8,0},{1,9},{9,1},{2,10},{10,2},{3,11},{11,3},{4,12},{12,4},... | collective-permute-start | bytes 589832 | tf_op jit(solution)/shard_map/ppermute | solution.py:593
  17.1 11.0 %collective-permute-start.1 = (bf16[128,768]{1,0:T(8,128)(2,1)S(1)}, bf16[128,768]{1,0:T(8,128)(2,1)S(1)}, u32[]{:S(2)}, u32[]{:S(2)}) collective-permute-start(bf16[128,768]{1,0:T(8,128)(2,1)S(1)} %shard_map.255), channel_id=1, source_target_pairs={{0,16},{1,17},{2,18},{3,19},{4,20},{5,21},{6,22},{7,23},{8,24},{9,... | collective-permute-start | bytes 589832 | tf_op jit(solution)/shard_map/ppermute | solution.py:672
  23.2 0.9 copy-start.2
  24.5 14.8 %collective-permute-start.3 = (bf16[128,768]{1,0:T(8,128)(2,1)S(1)}, bf16[128,768]{1,0:T(8,128)(2,1)S(1)}, u32[]{:S(2)}, u32[]{:S(2)}) collective-permute-start(bf16[128,768]{1,0:T(8,128)(2,1)S(1)} %shard_map.258), channel_id=1, source_target_pairs={{0,16},{1,17},{2,18},{3,19},{4,20},{5,21},{6,22},{7,23},{8,24},{9,... | collective-permute-start | bytes 589832 | tf_op jit(solution)/shard_map/ppermute | solution.py:672
  28.1 0.7 copy-start.17
  38.6 12.7 %copy-start.1 = (bf16[2,1,128,768]{3,2,1,0:T(8,128)(2,1)S(1)}, bf16[2,1,128,768]{3,2,1,0:T(8,128)(2,1)}, u32[]{:S(2)}) copy-start(bf16[2,1,128,768]{3,2,1,0:T(8,128)(2,1)} %param.16) | copy-start | bytes 1179652
  38.6 12.7 %copy-start.3 = (bf16[128,768]{1,0:T(8,128)(2,1)S(1)}, bf16[128,768]{1,0:T(8,128)(2,1)}, u32[]{:S(2)}) copy-start(bf16[128,768]{1,0:T(8,128)(2,1)} %get-tuple-element.64.one_ref) | copy-start | bytes 589828
  38.7 12.7 %collective-permute-start.5 = (bf16[128,768]{1,0:T(8,128)(2,1)}, bf16[128,768]{1,0:T(8,128)(2,1)S(1)}, u32[]{:S(2)}, u32[]{:S(2)}) collective-permute-start(bf16[128,768]{1,0:T(8,128)(2,1)} %get-tuple-element.64.one_ref), channel_id=1, source_target_pairs={{0,8},{8,0},{1,9},{9,1},{2,10},{10,2},{3,11},{11,3},{4,12},{12,4},... | collective-permute-start | bytes 589832 | tf_op jit(solution)/shard_map/ppermute | solution.py:593
  39.2 0.7 copy-start.16
  49.8 5.9 %collective-permute-start.8 = (bf16[128,768]{1,0:T(8,128)(2,1)}, bf16[128,768]{1,0:T(8,128)(2,1)S(1)}, u32[]{:S(2)}, u32[]{:S(2)}) collective-permute-start(bf16[128,768]{1,0:T(8,128)(2,1)} %get-tuple-element.72.one_ref), channel_id=1, source_target_pairs={{0,8},{8,0},{1,9},{9,1},{2,10},{10,2},{3,11},{11,3},{4,12},{12,4},... | collective-permute-start | bytes 589832 | tf_op jit(solution)/shard_map/ppermute | solution.py:593
  51.7 8.4 %collective-permute-start.6 = (bf16[128,768]{1,0:T(8,128)(2,1)S(1)}, bf16[128,768]{1,0:T(8,128)(2,1)S(1)}, u32[]{:S(2)}, u32[]{:S(2)}) collective-permute-start(bf16[128,768]{1,0:T(8,128)(2,1)S(1)} %shard_map.261), channel_id=1, source_target_pairs={{16,0},{17,1},{18,2},{19,3},{20,4},{21,5},{22,6},{23,7},{24,8},{25... | collective-permute-start | bytes 589832 | tf_op jit(solution)/shard_map/ppermute | solution.py:677
  55.7 0.9 copy-start.4
  56.9 12.9 %collective-permute-start.9 = (bf16[128,768]{1,0:T(8,128)(2,1)S(1)}, bf16[128,768]{1,0:T(8,128)(2,1)S(1)}, u32[]{:S(2)}, u32[]{:S(2)}) collective-permute-start(bf16[128,768]{1,0:T(8,128)(2,1)S(1)} %shard_map.263), channel_id=1, source_target_pairs={{16,0},{17,1},{18,2},{19,3},{20,4},{21,5},{22,6},{23,7},{24,8},{25... | collective-permute-start | bytes 589832 | tf_op jit(solution)/shard_map/ppermute | solution.py:677
  60.1 0.7 copy-start.18
  69.9 0.7 copy-start.15
  75.4 5.1 %copy-start.6 = (bf16[4,240,768]{2,1,0:T(8,128)(2,1)S(1)}, bf16[4,240,768]{2,1,0:T(8,128)(2,1)}, u32[]{:S(2)}) copy-start(bf16[4,240,768]{2,1,0:T(8,128)(2,1)} %get-tuple-element.78) | copy-start | bytes 4423684
  75.4 5.1 %collective-permute-start.10 = (bf16[4,240,768]{2,1,0:T(8,128)(2,1)}, bf16[4,240,768]{2,1,0:T(8,128)(2,1)S(1)}, u32[]{:S(2)}, u32[]{:S(2)}) collective-permute-start(bf16[4,240,768]{2,1,0:T(8,128)(2,1)} %get-tuple-element.79), channel_id=1, source_target_pairs={{0,1},{1,0},{2,3},{3,2},{4,5},{5,4},{6,7},{7,6},{8,9},{9,8},{10,11... | collective-permute-start | bytes 4423688 | tf_op jit(solution)/shard_map/ppermute | solution.py:605
  80.4 20.7 %collective-permute-start.4 = (bf16[256,768]{1,0:T(8,128)(2,1)}, bf16[256,768]{1,0:T(8,128)(2,1)}, u32[]{:S(2)}, u32[]{:S(2)}) collective-permute-start(bf16[256,768]{1,0:T(8,128)(2,1)} %shard_map.260), channel_id=1, source_target_pairs={{0,8},{8,0},{1,9},{9,1},{2,10},{10,2},{3,11},{11,3},{4,12},{12,4},... | collective-permute-start | bytes 1179656 | tf_op jit(solution)/shard_map/ppermute | solution.py:593
  90.7 10.4 %copy-start.9 = (bf16[256,768]{1,0:T(8,128)(2,1)S(1)}, bf16[256,768]{1,0:T(8,128)(2,1)}, u32[]{:S(2)}) copy-start(bf16[256,768]{1,0:T(8,128)(2,1)} %shard_map.260) | copy-start | bytes 1179652
  90.7 10.4 %copy-start.10 = (bf16[128,768]{1,0:T(8,128)(2,1)S(1)}, bf16[128,768]{1,0:T(8,128)(2,1)}, u32[]{:S(2)}) copy-start(bf16[128,768]{1,0:T(8,128)(2,1)} %get-tuple-element.58.refs_1_) | copy-start | bytes 589828
  90.7 6.4 %collective-permute-start.12 = (f32[8,384]{1,0:T(8,128)}, f32[8,384]{1,0:T(8,128)S(1)}, u32[]{:S(2)}, u32[]{:S(2)}) collective-permute-start(f32[8,384]{1,0:T(8,128)} %get-tuple-element.89), channel_id=1, source_target_pairs={{0,8},{8,0},{1,9},{9,1},{2,10},{10,2},{3,11},{11,3},{4,12},{12,4},... | collective-permute-start | bytes 36872 | tf_op jit(solution)/shard_map/ppermute | solution.py:593
  92.7 8.4 %copy-start.11 = (bf16[128,768]{1,0:T(8,128)(2,1)S(1)}, bf16[128,768]{1,0:T(8,128)(2,1)}, u32[]{:S(2)}) copy-start(bf16[128,768]{1,0:T(8,128)(2,1)} %get-tuple-element.59.refs_1_) | copy-start | bytes 589828
  92.7 10.3 %collective-permute-start.7 = (bf16[128,768]{1,0:T(8,128)(2,1)}, bf16[128,768]{1,0:T(8,128)(2,1)}, u32[]{:S(2)}, u32[]{:S(2)}) collective-permute-start(bf16[128,768]{1,0:T(8,128)(2,1)} %get-tuple-element.71), channel_id=1, source_target_pairs={{0,8},{8,0},{1,9},{9,1},{2,10},{10,2},{3,11},{11,3},{4,12},{12,4},... | collective-permute-start | bytes 589832 | tf_op jit(solution)/shard_map/ppermute | solution.py:593
  92.8 17.6 %collective-permute-start.20 = (bf16[240,768]{1,0:T(8,128)(2,1)}, bf16[240,768]{1,0:T(8,128)(2,1)}, u32[]{:S(2)}, u32[]{:S(2)}) collective-permute-start(bf16[240,768]{1,0:T(8,128)(2,1)} %get-tuple-element.115.refs_15_), channel_id=1, source_target_pairs={{0,2},{1,3},{8,10},{9,11},{16,18},{17,19},{24,26},{25,27}} | collective-permute-start | bytes 1105928 | tf_op jit(solution)/shard_map/ppermute | solution.py:627
  97.1 0.6 copy-start.20
  97.7 5.4 %copy-start.12 = (bf16[128,768]{1,0:T(8,128)(2,1)S(1)}, bf16[128,768]{1,0:T(8,128)(2,1)}, u32[]{:S(2)}) copy-start(bf16[128,768]{1,0:T(8,128)(2,1)} %get-tuple-element.71) | copy-start | bytes 589828
  101.1 2.0 %copy-start.13 = (bf16[128,768]{1,0:T(8,128)(2,1)S(1)}, bf16[128,768]{1,0:T(8,128)(2,1)}, u32[]{:S(2)}) copy-start(bf16[128,768]{1,0:T(8,128)(2,1)} %get-tuple-element.70.refs_3_) | copy-start | bytes 589828
  101.1 13.9 %collective-permute-start.13 = (bf16[4,304,384]{2,1,0:T(8,128)(2,1)}, bf16[4,304,384]{2,1,0:T(8,128)(2,1)}, u32[]{:S(2)}, u32[]{:S(2)}) collective-permute-start(bf16[4,304,384]{2,1,0:T(8,128)(2,1)} %get-tuple-element.91), channel_id=1, source_target_pairs={{0,1},{1,0},{2,3},{3,2},{4,5},{5,4},{6,7},{7,6},{8,9},{9,8},{10,11... | collective-permute-start | bytes 2801672 | tf_op jit(solution)/shard_map/ppermute | solution.py:605
  104.0 16.3 %collective-permute-start.23 = (bf16[240,768]{1,0:T(8,128)(2,1)}, bf16[240,768]{1,0:T(8,128)(2,1)S(1)}, u32[]{:S(2)}, u32[]{:S(2)}) collective-permute-start(bf16[240,768]{1,0:T(8,128)(2,1)} %get-tuple-element.114.refs_16_), channel_id=1, source_target_pairs={{6,4},{7,5},{14,12},{15,13},{22,20},{23,21},{30,28},{31,29}} | collective-permute-start | bytes 1105928 | tf_op jit(solution)/shard_map/ppermute | solution.py:629
  104.7 8.3 %collective-permute-start.11 = (bf16[128,768]{1,0:T(8,128)(2,1)}, bf16[128,768]{1,0:T(8,128)(2,1)S(1)}, u32[]{:S(2)}, u32[]{:S(2)}) collective-permute-start(bf16[128,768]{1,0:T(8,128)(2,1)} %get-tuple-element.83), channel_id=1, source_target_pairs={{0,8},{8,0},{1,9},{9,1},{2,10},{10,2},{3,11},{11,3},{4,12},{12,4},... | collective-permute-start | bytes 589832 | tf_op jit(solution)/shard_map/ppermute | solution.py:593
  106.7 6.3 %copy-start.14 = (bf16[128,768]{1,0:T(8,128)(2,1)S(1)}, bf16[128,768]{1,0:T(8,128)(2,1)}, u32[]{:S(2)}) copy-start(bf16[128,768]{1,0:T(8,128)(2,1)} %get-tuple-element.82) | copy-start | bytes 589828
  110.3 24.2 %collective-permute-start.26 = (bf16[4,96,1536]{2,1,0:T(8,128)(2,1)}, bf16[4,96,1536]{2,1,0:T(8,128)(2,1)S(1)}, u32[]{:S(2)}, u32[]{:S(2)}) collective-permute-start(bf16[4,96,1536]{2,1,0:T(8,128)(2,1)} %get-tuple-element.97), channel_id=1, source_target_pairs={{0,1},{1,0},{2,3},{3,2},{4,5},{5,4},{6,7},{7,6},{8,9},{9,8},{10,11... | collective-permute-start | bytes 3538952 | tf_op jit(solution)/shard_map/ppermute | solution.py:605
  111.6 3.4 %copy-start.8 = (bf16[4,304,384]{2,1,0:T(8,128)(2,1)S(1)}, bf16[4,304,384]{2,1,0:T(8,128)(2,1)}, u32[]{:S(2)}) copy-start(bf16[4,304,384]{2,1,0:T(8,128)(2,1)} %get-tuple-element.90) | copy-start | bytes 2801668
  111.6 10.4 %collective-permute-start.21 = (bf16[240,768]{1,0:T(8,128)(2,1)S(1)}, bf16[240,768]{1,0:T(8,128)(2,1)S(1)}, u32[]{:S(2)}, u32[]{:S(2)}) collective-permute-start(bf16[240,768]{1,0:T(8,128)(2,1)S(1)} %fusion.2), channel_id=1, source_target_pairs={{0,2},{1,3},{2,4},{3,5},{8,10},{9,11},{10,12},{11,13},{16,18},{17,... | collective-permute-start | bytes 1105928 | tf_op jit(solution)/shard_map/ppermute | solution.py:627
  116.2 18.3 %copy-start.7 = (bf16[4,96,1536]{2,1,0:T(8,128)(2,1)S(1)}, bf16[4,96,1536]{2,1,0:T(8,128)(2,1)}, u32[]{:S(2)}) copy-start(bf16[4,96,1536]{2,1,0:T(8,128)(2,1)} %get-tuple-element.96) | copy-start | bytes 3538948
  116.2 12.5 %collective-permute-start.14 = (bf16[304,384]{1,0:T(8,128)(2,1)S(1)}, bf16[304,384]{1,0:T(8,128)(2,1)S(1)}, u32[]{:S(2)}, u32[]{:S(2)}) collective-permute-start(bf16[304,384]{1,0:T(8,128)(2,1)S(1)} %get-tuple-element.122), channel_id=1, source_target_pairs={{0,2},{1,3},{8,10},{9,11},{16,18},{17,19},{24,26},{25,27}} | collective-permute-start | bytes 700424 | tf_op jit(solution)/shard_map/ppermute | solution.py:627
  122.3 16.5 %collective-permute-start.24 = (bf16[240,768]{1,0:T(8,128)(2,1)S(1)}, bf16[240,768]{1,0:T(8,128)(2,1)S(1)}, u32[]{:S(2)}, u32[]{:S(2)}) collective-permute-start(bf16[240,768]{1,0:T(8,128)(2,1)S(1)} %get-tuple-element.113), channel_id=1, source_target_pairs={{4,2},{5,3},{6,4},{7,5},{12,10},{13,11},{14,12},{15,13},{20,18},{2... | collective-permute-start | bytes 1105928 | tf_op jit(solution)/shard_map/ppermute | solution.py:629
  123.0 28.2 %collective-permute-start.22 = (bf16[240,768]{1,0:T(8,128)(2,1)S(1)}, bf16[240,768]{1,0:T(8,128)(2,1)S(1)}, u32[]{:S(2)}, u32[]{:S(2)}) collective-permute-start(bf16[240,768]{1,0:T(8,128)(2,1)S(1)} %get-tuple-element.112), channel_id=1, source_target_pairs={{0,2},{1,3},{2,4},{3,5},{4,6},{5,7},{8,10},{9,11},{10,12},{11,13},... | collective-permute-start | bytes 1105928 | tf_op jit(solution)/shard_map/ppermute | solution.py:627
  128.0 12.3 %collective-permute-start.17 = (bf16[304,384]{1,0:T(8,128)(2,1)S(1)}, bf16[304,384]{1,0:T(8,128)(2,1)S(1)}, u32[]{:S(2)}, u32[]{:S(2)}) collective-permute-start(bf16[304,384]{1,0:T(8,128)(2,1)S(1)} %get-tuple-element.123), channel_id=1, source_target_pairs={{6,4},{7,5},{14,12},{15,13},{22,20},{23,21},{30,28},{31,29}} | collective-permute-start | bytes 700424 | tf_op jit(solution)/shard_map/ppermute | solution.py:629
  129.7 12.3 %collective-permute-start.15 = (bf16[304,384]{1,0:T(8,128)(2,1)S(1)}, bf16[304,384]{1,0:T(8,128)(2,1)S(1)}, u32[]{:S(2)}, u32[]{:S(2)}) collective-permute-start(bf16[304,384]{1,0:T(8,128)(2,1)S(1)} %fusion.11), channel_id=1, source_target_pairs={{0,2},{1,3},{2,4},{3,5},{8,10},{9,11},{10,12},{11,13},{16,18},{17,... | collective-permute-start | bytes 700424 | tf_op jit(solution)/shard_map/ppermute | solution.py:627
  134.7 12.0 %collective-permute-start.27 = (bf16[96,1536]{1,0:T(8,128)(2,1)S(1)}, bf16[96,1536]{1,0:T(8,128)(2,1)S(1)}, u32[]{:S(2)}, u32[]{:S(2)}) collective-permute-start(bf16[96,1536]{1,0:T(8,128)(2,1)S(1)} %get-tuple-element.118), channel_id=1, source_target_pairs={{0,2},{1,3},{8,10},{9,11},{16,18},{17,19},{24,26},{25,27}} | collective-permute-start | bytes 884744 | tf_op jit(solution)/shard_map/ppermute | solution.py:627
  138.9 14.7 %collective-permute-start.25 = (bf16[240,768]{1,0:T(8,128)(2,1)S(1)}, bf16[240,768]{1,0:T(8,128)(2,1)S(1)}, u32[]{:S(2)}, u32[]{:S(2)}) collective-permute-start(bf16[240,768]{1,0:T(8,128)(2,1)S(1)} %fusion.1), channel_id=1, source_target_pairs={{2,0},{3,1},{4,2},{5,3},{6,4},{7,5},{10,8},{11,9},{12,10},{13,11},... | collective-permute-start | bytes 1105928 | tf_op jit(solution)/shard_map/ppermute | solution.py:629
  140.3 17.5 %collective-permute-start.30 = (bf16[96,1536]{1,0:T(8,128)(2,1)S(1)}, bf16[96,1536]{1,0:T(8,128)(2,1)S(1)}, u32[]{:S(2)}, u32[]{:S(2)}) collective-permute-start(bf16[96,1536]{1,0:T(8,128)(2,1)S(1)} %get-tuple-element.119), channel_id=1, source_target_pairs={{6,4},{7,5},{14,12},{15,13},{22,20},{23,21},{30,28},{31,29}} | collective-permute-start | bytes 884744 | tf_op jit(solution)/shard_map/ppermute | solution.py:629
  143.2 12.2 %collective-permute-start.18 = (bf16[304,384]{1,0:T(8,128)(2,1)S(1)}, bf16[304,384]{1,0:T(8,128)(2,1)S(1)}, u32[]{:S(2)}, u32[]{:S(2)}) collective-permute-start(bf16[304,384]{1,0:T(8,128)(2,1)S(1)} %get-tuple-element.121), channel_id=1, source_target_pairs={{4,2},{5,3},{6,4},{7,5},{12,10},{13,11},{14,12},{15,13},{20,18},{2... | collective-permute-start | bytes 700424 | tf_op jit(solution)/shard_map/ppermute | solution.py:629
  146.7 20.3 %collective-permute-start.16 = (bf16[304,384]{1,0:T(8,128)(2,1)S(1)}, bf16[304,384]{1,0:T(8,128)(2,1)S(1)}, u32[]{:S(2)}, u32[]{:S(2)}) collective-permute-start(bf16[304,384]{1,0:T(8,128)(2,1)S(1)} %get-tuple-element.120), channel_id=1, source_target_pairs={{0,2},{1,3},{2,4},{3,5},{4,6},{5,7},{8,10},{9,11},{10,12},{11,13},... | collective-permute-start | bytes 700424 | tf_op jit(solution)/shard_map/ppermute | solution.py:627
  151.2 9.8 %collective-permute-start.28 = (bf16[96,1536]{1,0:T(8,128)(2,1)S(1)}, bf16[96,1536]{1,0:T(8,128)(2,1)S(1)}, u32[]{:S(2)}, u32[]{:S(2)}) collective-permute-start(bf16[96,1536]{1,0:T(8,128)(2,1)S(1)} %fusion.6), channel_id=1, source_target_pairs={{0,2},{1,3},{2,4},{3,5},{8,10},{9,11},{10,12},{11,13},{16,18},{17,... | collective-permute-start | bytes 884744 | tf_op jit(solution)/shard_map/ppermute | solution.py:627
  156.4 10.6 %collective-permute-start.19 = (bf16[304,384]{1,0:T(8,128)(2,1)S(1)}, bf16[304,384]{1,0:T(8,128)(2,1)S(1)}, u32[]{:S(2)}, u32[]{:S(2)}) collective-permute-start(bf16[304,384]{1,0:T(8,128)(2,1)S(1)} %fusion.10), channel_id=1, source_target_pairs={{2,0},{3,1},{4,2},{5,3},{6,4},{7,5},{10,8},{11,9},{12,10},{13,11},... | collective-permute-start | bytes 700424 | tf_op jit(solution)/shard_map/ppermute | solution.py:629
  161.3 8.3 %collective-permute-start.31 = (bf16[96,1536]{1,0:T(8,128)(2,1)S(1)}, bf16[96,1536]{1,0:T(8,128)(2,1)S(1)}, u32[]{:S(2)}, u32[]{:S(2)}) collective-permute-start(bf16[96,1536]{1,0:T(8,128)(2,1)S(1)} %get-tuple-element.117), channel_id=1, source_target_pairs={{4,2},{5,3},{6,4},{7,5},{12,10},{13,11},{14,12},{15,13},{20,18},{2... | collective-permute-start | bytes 884744 | tf_op jit(solution)/shard_map/ppermute | solution.py:629
  161.9 10.2 %collective-permute-start.29 = (bf16[96,1536]{1,0:T(8,128)(2,1)S(1)}, bf16[96,1536]{1,0:T(8,128)(2,1)S(1)}, u32[]{:S(2)}, u32[]{:S(2)}) collective-permute-start(bf16[96,1536]{1,0:T(8,128)(2,1)S(1)} %get-tuple-element.116), channel_id=1, source_target_pairs={{0,2},{1,3},{2,4},{3,5},{4,6},{5,7},{8,10},{9,11},{10,12},{11,13},... | collective-permute-start | bytes 884744 | tf_op jit(solution)/shard_map/ppermute | solution.py:627
  169.7 12.6 %collective-permute-start.32 = (bf16[96,1536]{1,0:T(8,128)(2,1)S(1)}, bf16[96,1536]{1,0:T(8,128)(2,1)S(1)}, u32[]{:S(2)}, u32[]{:S(2)}) collective-permute-start(bf16[96,1536]{1,0:T(8,128)(2,1)S(1)} %fusion.5), channel_id=1, source_target_pairs={{2,0},{3,1},{4,2},{5,3},{6,4},{7,5},{10,8},{11,9},{12,10},{13,11},... | collective-permute-start | bytes 884744 | tf_op jit(solution)/shard_map/ppermute | solution.py:629
  171.5 12.3 %copy-start.19 = (f32[1,48]{1,0:T(1,128)}, f32[1,48]{1,0:T(1,128)S(1)}, u32[]{:S(2)}) copy-start(f32[1,48]{1,0:T(1,128)S(1)} %get-tuple-element.156) | copy-start | bytes 580

commit v2 on v1

v2 whole, which is shorter than its diff:
```python
import functools
import math

import jax
import jax.numpy as jnp
import numpy as np
from jax import lax
from jax.experimental import pallas as pl
from jax.experimental.pallas import tpu as pltpu
from jax.sharding import PartitionSpec as P

HEAD = 64
ROT = 16
LANES = 128
PIECE = 512
AHEAD = 40
EPSILON = 1e-05
BF = jnp.bfloat16
F32 = jnp.float32


def rope_tables(length):
    half = ROT // 2
    inverse = np.exp(-math.log(10000.0) * np.arange(half, dtype=np.float32) * np.float32(2.0) / ROT)
    angle = np.arange(length, dtype=np.float32)[:, None] * inverse[None, :].astype(np.float32)
    cosine, sine = np.cos(angle), np.sin(angle)
    table = np.zeros((3, length, LANES), np.float32)
    table[0] = 1.0
    for head in range(LANES // HEAD):
        at = head * HEAD
        table[0, :, at : at + half] = cosine
        table[0, :, at + half : at + ROT] = cosine
        table[1, :, at : at + half] = -sine
        table[2, :, at + half : at + ROT] = sine
    return table


def dot(a, b):
    return jnp.dot(a, b, preferred_element_type=F32)


def dot_nt(a, b):
    return lax.dot_general(a, b, (((1,), (1,)), ((), ())), preferred_element_type=F32)


def dot_tn(a, b):
    return lax.dot_general(a, b, (((0,), (0,)), ((), ())), preferred_element_type=F32)


def roped(value, table, sign):
    half = ROT // 2
    ahead = pltpu.roll(value, LANES - half, 1) * table[1]
    behind = pltpu.roll(value, half, 1) * table[2]
    return value * table[0] + sign * (ahead + behind)


def head_pair(value):
    low = lax.broadcasted_iota(jnp.int32, value.shape, 1) < HEAD
    zero = jnp.zeros_like(value)
    return jnp.concatenate([jnp.where(low, value, zero), jnp.where(low, zero, value)], axis=0)


def pair_merge(value):
    rows = value.shape[0] // 2
    low = lax.broadcasted_iota(jnp.int32, (rows, LANES), 1) < HEAD
    return jnp.where(low, value[:rows], value[rows:])


def normal(block):
    width = block.shape[1]
    center = block - jnp.sum(block, axis=1, keepdims=True) * (1.0 / width)
    spread = jnp.sum(center * center, axis=1, keepdims=True) * (1.0 / width)
    scale = lax.rsqrt(spread + EPSILON)
    return center * scale, scale


def forward_part(x, vec, table, w, wait, put):
    rows, width = x.shape
    unit, unused = normal(x.astype(F32))
    first = (unit * vec["g1"] + vec["b1"]).astype(BF)
    second = (unit * vec["g2"] + vec["b2"]).astype(BF)
    put("a1", first)
    put("a2", second)
    bqkv = vec["bqkv"]
    raw = []
    for j in range(3):
        wait("wqkv", j)
        raw.append(dot(first, w["wqkv"][j]) + bqkv[j : j + 1])
    local = raw[0].shape[1]
    wait("table")
    length = table.shape[1]
    row = lax.broadcasted_iota(jnp.int32, (length, length), 0)
    keep = row >= lax.broadcasted_iota(jnp.int32, (length, length), 1)
    for start in range(0, rows, length):
        rs = slice(start, start + length)
        for p in range(local // LANES):
            sl = slice(p * LANES, (p + 1) * LANES)
            q = roped(raw[0][rs, sl], table, 1.0).astype(BF)
            k = roped(raw[1][rs, sl], table, 1.0).astype(BF)
            v = raw[2][rs, sl].astype(BF)
            put("q", q, sl)
            put("k", k, sl)
            put("v", v, sl)
            scores = dot_nt(q, head_pair(k)) * HEAD**-0.5
            prob = []
            for h in range(2):
                part = jnp.where(keep, scores[:, h * length : (h + 1) * length], -1e30)
                expo = jnp.exp(part - jnp.max(part, axis=1, keepdims=True))
                prob.append(expo * (1.0 / jnp.sum(expo, axis=1, keepdims=True)))
            prob = jnp.concatenate(prob, axis=1).astype(BF)
            put("prob", prob, slice(p * 2 * length, (p + 1) * 2 * length))
            put("mixed", dot(prob, head_pair(v)).astype(BF), sl, rs)
    hidden = w["wup"].shape[1]
    step = 256
    for c in range(0, hidden, step):
        sl = slice(c, c + step)
        wait("wup", c // PIECE)
        u = dot(second, w["wup"][:, sl]) + vec["bup"][:, sl]
        phi = 0.5 + 0.5 * lax.erf(u * (2.0**-0.5))
        put("g", (u * phi).astype(BF), sl)
        put("gp", lambda: phi + u * (jnp.exp(-0.5 * u * u) * (2.0 * math.pi) ** -0.5), sl)


def output_part(mixed, active, vec, w, wait):
    wait("wout")
    total = dot(mixed[...], w["wout"][...])
    wait("wdown")
    total = total + dot(active[...], w["wdown"][...])
    return (total + vec["extra"]).astype(BF)


def backward_part(dy, saved, table, w, wait, put):
    rows = dy.shape[0]
    hidden = w["wdown"].shape[0]
    step = 256
    wait("gp")
    for c in range(0, hidden, step):
        sl = slice(c, c + step)
        wait("wdown", c // PIECE)
        du = (dot_nt(dy, w["wdown"][sl, :]) * saved["gp"][:, sl].astype(F32)).astype(BF)
        put("du", du, sl)
    wait("wout")
    for name in ("table", "q", "k", "v", "prob"):
        wait(name)
    d_mixed = dot_nt(dy, w["wout"][...]).astype(BF)
    local = d_mixed.shape[1]
    length = table.shape[1]
    scale = HEAD**-0.5
    for start in range(0, rows, length):
        rs = slice(start, start + length)
        for p in range(local // LANES):
            sl = slice(p * LANES, (p + 1) * LANES)
            q, k, v = saved["q"][rs, sl], saved["k"][rs, sl], saved["v"][rs, sl]
            low = saved["prob"][rs, p * 2 * length : (p + 1) * 2 * length]
            prob = low.astype(F32)
            d_tile = d_mixed[rs, sl]
            d_prob = dot_nt(d_tile, head_pair(v))
            d_value = pair_merge(dot_tn(low, d_tile))
            d_scores = []
            for h in range(2):
                part = prob[:, h * length : (h + 1) * length]
                d_part = d_prob[:, h * length : (h + 1) * length]
                both = part * d_part
                d_scores.append(both - part * jnp.sum(both, axis=1, keepdims=True))
            d_scores = jnp.concatenate(d_scores, axis=1).astype(BF)
            d_query = dot(d_scores, head_pair(k)) * scale
            d_keys = pair_merge(dot_tn(d_scores, q)) * scale
            at = p * LANES
            put("dqkv", roped(d_query, table, -1.0).astype(BF), slice(at, at + LANES), rs)
            at += local
            put("dqkv", roped(d_keys, table, -1.0).astype(BF), slice(at, at + LANES), rs)
            at += local
            put("dqkv", d_value.astype(BF), slice(at, at + LANES), rs)


def norm_back(x, du, dqkv, local, vec, w, wait):
    wait("wup")
    d_second = dot_nt(du[...], w["wup"][...])
    for j in range(3):
        wait("wqkv", j)
    d_first = dot_nt(dqkv[:, :local], w["wqkv"][0])
    for j in range(1, 3):
        d_first = d_first + dot_nt(dqkv[:, j * local : (j + 1) * local], w["wqkv"][j])
    unit, scale = normal(x.astype(F32))
    e = d_first * vec["g1"] + d_second * vec["g2"]
    width = x.shape[1]
    mean = jnp.sum(e, axis=1, keepdims=True) * (1.0 / width)
    along = jnp.sum(e * unit, axis=1, keepdims=True) * (1.0 / width)
    dx = (e - mean - unit * along) * scale
    return dx.astype(BF), d_first, d_second, unit


WEIGHTS = ("wqkv", "wout", "wup", "wdown")
VECTORS = ("g1", "b1", "g2", "b2", "bqkv", "bout", "bup", "bdown")
NEEDED = ("q", "k", "v", "prob", "gp")
SAVED = ("a1", "a2", "q", "k", "v", "prob", "mixed", "g", "gp")


class Loads:
    def __init__(self, sems, ahead=64):
        self.sems, self.copies, self.queue, self.ahead = sems, {}, [], ahead
        self.started = self.waited = 0

    def start(self, name, source, target):
        copy = pltpu.make_async_copy(source, target, self.sems.at[len(self.queue)])
        self.copies.setdefault(name, {})[len(self.copies.get(name, {}))] = (len(self.queue), copy)
        self.queue.append(copy)
        self.pump(self.waited + self.ahead)

    def pump(self, until):
        while self.started < min(until, len(self.queue)):
            self.queue[self.started].start()
            self.started += 1

    def weight(self, name, hbm, w):
        source, target = hbm[name], w[name]
        if name == "wqkv":
            for j in range(3):
                self.start(name, source.at[j], target.at[j])
        elif name == "wout":
            self.start(name, source, target)
        else:
            for c in range(0, source.shape[0 if name == "wdown" else 1], PIECE):
                at = (pl.ds(c, PIECE), slice(None)) if name == "wdown" else (slice(None), pl.ds(c, PIECE))
                self.start(name, source.at[at], target.at[at])

    def wait(self, name, index=None):
        left = self.copies.get(name, {})
        for piece in [index] if index is not None else list(left):
            if piece in left:
                at, copy = left.pop(piece)
                self.pump(at + 1)
                copy.wait()
                self.waited += 1
                self.pump(self.waited + self.ahead)


def unpacked(pack, width, local, hidden):
    return {
        "g1": pack[0:1, :width],
        "b1": pack[1:2, :width],
        "g2": pack[2:3, :width],
        "b2": pack[3:4, :width],
        "extra": pack[4:5, :width],
        "bup": pack[5:6, :hidden],
        "bqkv": pack[6:9, :local],
    }


def f_kernel(micro, *refs):
    flag_ref, x_hbm, table_hbm = refs[:3]
    hbm = dict(zip(WEIGHTS, refs[3:7]))
    vec_hbm = dict(zip(VECTORS, refs[7:15]))
    out_refs, pack_ref = refs[15 : 15 + micro], refs[15 + micro]
    refs = refs[16 + micro :]
    w = dict(zip(WEIGHTS, refs[:4]))
    mixed, active, x_ref, table_ref, sems = refs[4:9]
    loads = Loads(sems)
    vec_ref = dict(zip(VECTORS, refs[9:]))
    rows, width = out_refs[0].shape
    for m in range(micro):
        loads.start("x", x_hbm.at[m], x_ref.at[pl.ds(m * rows, rows)])
    for name in VECTORS:
        loads.start(name, vec_hbm[name], vec_ref[name])
    loads.weight("wqkv", hbm, w)
    loads.start("table", table_hbm, table_ref)
    for name in ("wup", "wout", "wdown"):
        loads.weight(name, hbm, w)
    local, hidden = mixed.shape[1], active.shape[1]
    for name in VECTORS:
        loads.wait(name)
    for i, name in enumerate(("g1", "b1", "g2", "b2")):
        pack_ref[i : i + 1, :width] = vec_ref[name][...].astype(F32)
    extra = vec_ref["bout"][...].astype(F32) + vec_ref["bdown"][...].astype(F32)
    pack_ref[4:5, :width] = jnp.where(flag_ref[1] == 0, extra, jnp.zeros_like(extra))
    pack_ref[5:6, :hidden] = vec_ref["bup"][...].astype(F32)
    pack_ref[6:9, :local] = vec_ref["bqkv"][...].astype(F32)
    vec = unpacked(pack_ref, width, local, hidden)

    def put(name, value, sl=slice(None), rs=slice(None)):
        if name == "mixed":
            mixed[rs, sl] = value
        if name == "g":
            active[rs, sl] = value

    loads.wait("x")
    forward_part(x_ref[...], vec, table_ref, w, loads.wait, put)
    out = output_part(mixed, active, vec, w, loads.wait)
    for m in range(micro):
        out_refs[m][...] = out[m * rows : (m + 1) * rows]


def fb_kernel(at, *refs):
    flag_ref, x_hbm, dy_hbm, arrived_hbm, table_hbm, pack_hbm = refs[:6]
    hbm = dict(zip(WEIGHTS, refs[6:10]))
    names = ("dx", "source") + SAVED
    outs = dict(zip(names, refs[10 : 10 + len(names)]))
    refs = refs[10 + len(names) :]
    held = dict(zip(names, refs[: len(names)]))
    refs = refs[len(names) :]
    w = dict(zip(WEIGHTS, refs[:4]))
    du, dqkv, x_ref, dy_ref, arrived_ref, table_ref, pack_ref, sems, out_sems = refs[4:]
    loads, stores = Loads(sems, AHEAD + 2), Loads(out_sems)
    loads.start("x", x_hbm.at[at], x_ref)
    loads.start("arrived", arrived_hbm, arrived_ref)
    loads.start("pack", pack_hbm, pack_ref)
    loads.weight("wqkv", hbm, w)
    loads.start("table", table_hbm, table_ref)
    loads.weight("wup", hbm, w)
    loads.start("dy", dy_hbm.at[at], dy_ref)
    loads.weight("wdown", hbm, w)
    loads.weight("wout", hbm, w)
    held_too = dict(held, du=du, dqkv=dqkv)

    def put(name, value, sl=slice(None), rs=slice(None)):
        ref = held_too[name]
        value = value() if callable(value) else value
        ref[rs, sl] = value.astype(ref.dtype)

    width, (local, hidden) = x_ref.shape[1], (dqkv.shape[1] // 3, du.shape[1])
    loads.wait("x")
    loads.wait("arrived")
    x = jnp.where(flag_ref[0] == 0, x_ref[...], arrived_ref[...])
    loads.wait("pack")
    vec = unpacked(pack_ref, width, local, hidden)
    held["source"][...] = x
    forward_part(x, vec, table_ref, w, loads.wait, put)
    for name in ("source",) + SAVED:
        stores.start(name, held[name], outs[name])
    loads.wait("dy")
    backward_part(dy_ref[...], held, table_ref, w, loads.wait, put)
    held["dx"][...] = norm_back(x, du, dqkv, local, vec, w, loads.wait)[0]
    stores.start("dx", held["dx"], outs["dx"])
    for name in names:
        stores.wait(name)


def b_kernel(micro, *refs):
    flag_ref, dy_hbm, table_hbm, pack_hbm = refs[:4]
    hbm = dict(zip(WEIGHTS, refs[4:8]))
    names = ("arrived", "x") + NEEDED
    pieces = {n: refs[8 + i * micro : 8 + (i + 1) * micro] for i, n in enumerate(names)}
    refs = refs[-(6 + 4 + 3 + len(names) + 1) :]
    dx_ref, du, dqkv, own, other, dy_out = refs[:6]
    w = dict(zip(WEIGHTS, refs[6:10]))
    dy_ref, table_ref, pack_ref = refs[10:13]
    saved = dict(zip(names, refs[13:-1]))
    loads = Loads(refs[-1])
    rows = pieces["x"][0].shape[0]

    def both(name):
        for m in range(micro):
            loads.start(name, pieces[name][m], saved[name].at[pl.ds(m * rows, rows)])

    for m in range(micro):
        loads.start("dy", dy_hbm.at[m], dy_ref.at[pl.ds(m * rows, rows)])
    both("arrived")
    both("gp")
    loads.weight("wdown", hbm, w)
    loads.weight("wout", hbm, w)
    loads.start("table", table_hbm, table_ref)
    for name in NEEDED[:4]:
        both(name)
    loads.weight("wup", hbm, w)
    loads.weight("wqkv", hbm, w)
    both("x")
    loads.start("pack", pack_hbm, pack_ref)
    kept = {"du": du, "dqkv": dqkv}

    def put(name, value, sl=slice(None), rs=slice(None)):
        kept[name][rs, sl] = value

    loads.wait("dy")
    loads.wait("arrived")
    dy = jnp.where(flag_ref[0] == 0, saved["arrived"][...], dy_ref[...])
    dy_out[...] = dy
    width, (local, hidden) = dy.shape[1], (dqkv.shape[1] // 3, du.shape[1])
    backward_part(dy, saved, table_ref, w, loads.wait, put)
    loads.wait("x")
    loads.wait("pack")
    vec = unpacked(pack_ref, width, local, hidden)
    dx, d_first, d_second, unit = norm_back(saved["x"][...], du, dqkv, local, vec, w, loads.wait)
    dx_ref[...] = dx
    own[...] = jnp.zeros_like(own)
    other[...] = jnp.zeros_like(other)
    low = flag_ref[1] == 0
    terms = (d_first * unit, d_first, d_second * unit, d_second, dy.astype(F32))
    for i, term in enumerate(terms):
        total = jnp.sum(term, axis=0, keepdims=True)
        front, back = total[:, :local], total[:, local:]
        own[i : i + 1] = jnp.where(low, front, back)
        if i < 4:
            other[i : i + 1] = jnp.where(low, back, front)
    line = 5
    for ref in (dqkv, du):
        for c in range(0, ref.shape[1], local):
            own[line : line + 1] = jnp.sum(ref[:, c : c + local].astype(F32), axis=0, keepdims=True)
            line += 1


def deal(theirs, mine, place, at, core, value, share):
    for z in range(value.shape[0] // (2 * share)):
        front = value[2 * z * share : (2 * z + 1) * share]
        back = value[(2 * z + 1) * share : (2 * z + 2) * share]
        theirs[place + z, at : at + share] = jnp.where(core == 0, back, front)
        mine[place + z, at : at + share] = jnp.where(core == 0, front, back)


def outer(pieces, sl, right):
    return dot_tn(jnp.concatenate([piece[:, sl] for piece in pieces], axis=0), right).astype(BF)


def down_kernel(chips, micro, *refs):
    flag_ref, dy_hbm = refs[:2]
    arrived, active, mixed = (refs[2 + i * micro : 2 + (i + 1) * micro] for i in range(3))
    theirs, mine, dy_ref, sem = refs[2 + 3 * micro :]
    copy = pltpu.make_async_copy(dy_hbm, dy_ref, sem)
    copy.start()
    copy.wait()
    core = flag_ref[2]
    dy = [jnp.where(flag_ref[0] == 0, arrived[m][...], dy_ref[m]) for m in range(micro)]
    dy = jnp.concatenate(dy, axis=0)
    hidden, local = active[0].shape[1], mixed[0].shape[1]
    share, step = hidden // (2 * chips), hidden // chips
    for z in range(chips):
        deal(theirs, mine, z, 0, core, outer(active, slice(z * step, (z + 1) * step), dy), share)
    deal(theirs, mine, 0, share, core, outer(mixed, slice(0, local), dy), local // (2 * chips))


def rest_kernel(chips, micro, *refs):
    flag_ref, du, dqkv, own, got = refs[:5]
    a1, a2, (theirs, mine) = refs[5 : 5 + micro], refs[5 + micro : 5 + 2 * micro], refs[-2:]
    width, local = a1[0].shape[1], own.shape[1]
    share = width // (2 * chips)
    step = width // 2
    at = 0
    for left, right in ((a2, du), (a1, dqkv)):
        for c in range(0, right.shape[1], local):
            columns = right[:, c : c + local]
            for j in range(2):
                value = outer(left, slice(j * step, (j + 1) * step), columns)
                deal(theirs, mine, j * chips // 2, at, flag_ref[2], value, share)
            at += share
    half = got.shape[0]
    lines = jnp.concatenate([own[:half] + got[...], own[half:]], axis=0).astype(BF)
    for z in range(chips):
        theirs[z, at:] = lines
        mine[z, at:] = lines


def arrived_sum(flag_ref, refs, scratch, sems):
    place = flag_ref[3]
    loads = Loads(sems)
    for i in range(2):
        loads.start(i, refs[i].at[place], scratch.at[i])
    edge = jnp.logical_or(place == 0, place == 3)
    for i in range(2):
        loads.wait(i)

    def total(at, rows):
        sl = slice(at, at + rows)
        value = refs[2][sl, :].astype(F32)
        value = jnp.where(edge, value, jnp.zeros_like(value))
        value = value + (scratch[0, sl, :].astype(F32) + scratch[1, sl, :].astype(F32))
        for ref in refs[3:7]:
            value = value + ref[sl, :].astype(F32)
        return value

    return total


def final_down_kernel(flag_ref, *refs):
    down_ref, out_ref, scratch, sems = refs[-4:]
    total = arrived_sum(flag_ref, refs[:7], scratch, sems)
    rows = down_ref.shape[0]
    down_ref[...] = total(0, rows)
    out_ref[...] = total(rows, out_ref.shape[0])


def final_rest_kernel(flag_ref, *refs):
    up_ref, qkv_ref, vec_ref, bqkv_ref, bup_ref, lines, scratch, sems = refs[-8:]
    total = arrived_sum(flag_ref, refs[:7], scratch, sems)
    share, local = qkv_ref.shape[1:]
    at = 0
    for c in range(0, up_ref.shape[1], local):
        up_ref[:, c : c + local] = total(at, share)
        at += share
    for t in range(3):
        qkv_ref[t] = total(at, share)
        at += share
    lines[...] = total(at, lines.shape[0])
    dp_at = 2 * flag_ref[3] + flag_ref[2]
    width = bqkv_ref.shape[1]
    front = pltpu.roll(lines[0:8], local - dp_at * width, 1)
    vec_ref[...] = front[0:5, :width]
    bqkv_ref[...] = front[5:8, :width]
    width = bup_ref.shape[1]
    per_line = local // width
    line = pltpu.roll(lines[8:16], local - (dp_at % per_line) * width, 1)
    row = dp_at // per_line
    picked = jnp.zeros((1, width), F32)
    for i in range(per_line and 8 // per_line):
        picked = jnp.where(row == i, line[i : i + 1, :width], picked)
    bup_ref[...] = picked


def tail_kernel(micro, *refs):
    part, other, up, grad, other_grad = refs[:5]
    sources = refs[5 : 5 + micro]
    out_ref, grad_ref = refs[-2:]
    rows = sources[0].shape[0]
    for m in range(micro):
        sl = slice(m * rows, (m + 1) * rows)
        both = part[sl].astype(F32) + other[sl].astype(F32)
        out_ref[sl] = (sources[m][...].astype(F32) + both).astype(BF)
    grad_ref[...] = up[...].astype(F32) + (grad[...].astype(F32) + other_grad[...].astype(F32))


def o_kernel(micro, *refs):
    mixed_refs, active_refs = refs[:micro], refs[micro : 2 * micro]
    pack_ref, wout_hbm, wdown_hbm = refs[2 * micro : 2 * micro + 3]
    out_ref, wout, wdown, mixed, active, sems = refs[-6:]
    loads = Loads(sems)
    hbm, w = {"wout": wout_hbm, "wdown": wdown_hbm}, {"wout": wout, "wdown": wdown}
    loads.weight("wout", hbm, w)
    loads.weight("wdown", hbm, w)
    rows = mixed_refs[0].shape[0]
    for m in range(micro):
        mixed[m * rows : (m + 1) * rows] = mixed_refs[m][...]
        active[m * rows : (m + 1) * rows] = active_refs[m][...]
    vec = unpacked(pack_ref, wout.shape[1], wout.shape[0], wdown.shape[0])
    out_ref[...] = output_part(mixed, active, vec, w, loads.wait)


def add_kernel(at, x_hbm, one_ref, two_ref, out_ref, x_ref, sems):
    loads = Loads(sems)
    loads.start("x", x_hbm.at[at], x_ref)
    loads.wait("x")
    whole = x_ref[...].astype(F32) + (one_ref[...].astype(F32) + two_ref[...].astype(F32))
    out_ref[...] = whole.astype(BF)


VM = pl.BlockSpec(memory_space=pltpu.VMEM)
SM = pl.BlockSpec(memory_space=pltpu.SMEM)
HB = pl.BlockSpec(memory_space=pltpu.HBM)


def scratch_like(arrays):
    return [pltpu.VMEM(a.shape, a.dtype) for a in arrays]


def cost(ws, rows, passes):
    size = sum(math.prod(a.shape) for a in ws)
    return pl.CostEstimate(flops=2 * size * rows * passes, bytes_accessed=2 * size, transcendentals=0)


def params(mib):
    return pltpu.CompilerParams(vmem_limit_bytes=mib * 2**20)


def call_add(at, xs, one, two):
    rows, width = one.shape
    return pl.pallas_call(
        functools.partial(add_kernel, at),
        out_shape=jax.ShapeDtypeStruct((rows, width), BF),
        in_specs=[HB, VM, VM],
        out_specs=VM,
        scratch_shapes=[pltpu.VMEM((rows, width), BF), pltpu.SemaphoreType.DMA((1,))],
        compiler_params=params(8),
        cost_estimate=pl.CostEstimate(flops=rows * width * 2, bytes_accessed=rows * width * 8, transcendentals=0),
    )(xs, one, two)


def call_f(flags, xs, table, ws, vecs):
    micro, rows, width = xs.shape
    local, hidden = ws[1].shape[0], ws[3].shape[0]
    total = micro * rows
    scratch = scratch_like(ws) + [
        pltpu.VMEM((total, local), BF),
        pltpu.VMEM((total, hidden), BF),
        pltpu.VMEM((total, width), BF),
        pltpu.VMEM(table.shape, F32),
        pltpu.SemaphoreType.DMA((24,)),
    ]
    out = [jax.ShapeDtypeStruct((rows, width), BF)] * micro + [jax.ShapeDtypeStruct((16, hidden), F32)]
    return pl.pallas_call(
        functools.partial(f_kernel, micro),
        out_shape=out,
        in_specs=[SM] + [HB] * 14,
        out_specs=[VM] * len(out),
        scratch_shapes=scratch + scratch_like(vecs),
        compiler_params=params(54),
        cost_estimate=cost(ws, total, 1),
    )(flags, xs, table, *ws, *vecs)


def call_fb(at, flags, xs, cots, arrived, table, pack, ws):
    rows, width = arrived.shape
    local, hidden = ws[1].shape[0], ws[3].shape[0]
    shape = jax.ShapeDtypeStruct
    outs = [shape((rows, width), BF)] * 4
    outs += [shape((rows, local), BF)] * 3
    outs += [
        shape((rows, 2 * rows * local // LANES), BF),
        shape((rows, local), BF),
        shape((rows, hidden), BF),
        shape((rows, hidden), BF),
    ]
    return pl.pallas_call(
        functools.partial(fb_kernel, at),
        out_shape=outs,
        in_specs=[SM] + [HB] * 9,
        out_specs=[HB] * len(outs),
        scratch_shapes=scratch_like(outs)
        + scratch_like(ws)
        + [
            pltpu.VMEM((rows, hidden), BF),
            pltpu.VMEM((rows, 3 * local), BF),
            pltpu.VMEM((rows, width), BF),
            pltpu.VMEM((rows, width), BF),
            pltpu.VMEM((rows, width), BF),
            pltpu.VMEM(table.shape, F32),
            pltpu.VMEM(pack.shape, F32),
            pltpu.SemaphoreType.DMA((24,)),
            pltpu.SemaphoreType.DMA((len(outs),)),
        ],
        compiler_params=params(54),
        cost_estimate=cost(ws, rows, 2),
    )(flags, xs, cots, arrived, table, pack, *ws)


def call_b(flags, cots, table, pack, ws, pieces, after):
    micro, rows, width = cots.shape
    local, hidden = ws[1].shape[0], ws[3].shape[0]
    shape = jax.ShapeDtypeStruct
    total = micro * rows
    outs = [
        shape((total, width), BF),
        shape((total, hidden), BF),
        shape((total, 3 * local), BF),
        shape((16, local), F32),
        shape((8, local), F32),
        shape((total, width), BF),
    ]
    flat = [array for group in pieces for array in group]
    return pl.pallas_call(
        functools.partial(b_kernel, micro),
        out_shape=outs,
        in_specs=[SM] + [HB] * (7 + len(flat) + len(after)),
        out_specs=[VM] * len(outs),
        scratch_shapes=scratch_like(ws)
        + [pltpu.VMEM((total, width), BF)]
        + scratch_like([table, pack])
        + [pltpu.VMEM((total, group[0].shape[1]), group[0].dtype) for group in pieces]
        + [pltpu.SemaphoreType.DMA((32,))],
        compiler_params=params(54),
        cost_estimate=cost(ws, total, 1),
    )(flags, cots, table, pack, *ws, *flat, *after)


def call_blocks(kernel, flags, operands, specs, block, flops, scratch=()):
    outs = [jax.ShapeDtypeStruct(block, BF)] * 2
    return pl.pallas_call(
        kernel,
        out_shape=outs,
        in_specs=[SM] + specs,
        out_specs=[VM] * 2,
        scratch_shapes=list(scratch),
        compiler_params=params(54),
        cost_estimate=pl.CostEstimate(flops=flops, bytes_accessed=4 * math.prod(block), transcendentals=0),
    )(flags, *operands)


def call_final(kernel, flags, parts, outs, after, scratch=()):
    return pl.pallas_call(
        kernel,
        out_shape=[jax.ShapeDtypeStruct(shape, F32) for shape in outs],
        in_specs=[SM, HB, HB] + [VM] * 5 + [HB] * len(after),
        out_specs=[VM] * len(outs),
        scratch_shapes=list(scratch)
        + [pltpu.VMEM((2,) + parts[2].shape, BF), pltpu.SemaphoreType.DMA((2,))],
        compiler_params=params(16),
    )(flags, *parts, *after)


def call_tail(part, other, up, grad, other_grad, sources, after):
    micro = len(sources)
    return pl.pallas_call(
        functools.partial(tail_kernel, micro),
        out_shape=[jax.ShapeDtypeStruct(part.shape, BF), jax.ShapeDtypeStruct(part.shape, F32)],
        in_specs=[VM] * (5 + micro) + [HB] * len(after),
        out_specs=[VM] * 2,
        compiler_params=params(16),
    )(part, other, up, grad, other_grad, *sources, *after)


def call_o(mixed, active, pack, ws, after=()):
    micro, (rows, local) = len(mixed), mixed[0].shape
    hidden, width = ws[3].shape
    total = micro * rows
    return pl.pallas_call(
        functools.partial(o_kernel, micro),
        out_shape=jax.ShapeDtypeStruct((total, width), BF),
        in_specs=[VM] * (2 * micro + 1) + [HB] * (2 + len(after)),
        out_specs=VM,
        scratch_shapes=[
            pltpu.VMEM((local, width), BF),
            pltpu.VMEM((hidden, width), BF),
            pltpu.VMEM((total, local), BF),
            pltpu.VMEM((total, hidden), BF),
            pltpu.SemaphoreType.DMA((8,)),
        ],
        compiler_params=params(54),
        cost_estimate=cost((ws[1], ws[3]), total, 1),
    )(*mixed, *active, pack, ws[1], ws[3], *after)


def swap(value):
    return lax.ppermute(value, "tensor", [(0, 1), (1, 0)])


class Line:
    def __init__(self, theirs, mine, at):
        self.place = at // 2
        self.mine = mine
        self.got = lax.ppermute(theirs, "dp", [(i, i ^ 1) for i in range(8)])

    def block(self, index):
        one = lax.dynamic_index_in_dim(self.mine, index, 0, keepdims=False)
        two = lax.dynamic_index_in_dim(self.got, index, 0, keepdims=False)
        return one.astype(F32) + two.astype(F32)

    def send(self, value, pairs):
        return lax.ppermute(value, "dp", [(2 * a + c, 2 * b + c) for a, b in pairs for c in range(2)])

    def start(self):
        place = self.place
        values = [
            self.block(index).astype(BF)
            for index in (
                jnp.where(place % 2 == 0, 3, 0),
                jnp.where(place == 1, 2, 1),
                jnp.where(place == 0, 2, 1),
                jnp.where(place == 0, 1, 2),
            )
        ]
        self.one = self.send(values[0], [(0, 1), (1, 0), (2, 3), (3, 2)])
        self.three = self.send(values[1], [(1, 2), (2, 1)])
        self.four = self.send(values[2], [(0, 2), (3, 1)])
        self.two = self.send(values[3], [(0, 1), (3, 2)])
        return tuple(values)

    def relay(self):
        value = (self.block(jnp.where(self.place == 1, 3, 0)) + self.one.astype(F32)).astype(BF)
        self.five = self.send(value, [(1, 3), (2, 0)])
        return value

    def parts(self):
        return self.mine, self.got, self.one, self.two, self.three, self.four, self.five


def wide(pieces, others):
    left, right = jnp.concatenate(pieces, axis=0), jnp.concatenate(others, axis=0)
    return jnp.einsum("ta,tb->ab", left, right, preferred_element_type=F32).astype(BF)


def scattered(blocks):
    parts, rows, columns = blocks.shape
    return lax.psum_scatter(blocks.reshape(parts * rows, columns), "dp", scatter_dimension=0, tiled=True).astype(F32)


def per_device(inputs, cotangent, g1, b1, g2, b2, w_qkv, b_qkv, w_out, b_out, w_up, b_up, w_down, b_down):
    section = lax.axis_index("section")
    owner = lax.axis_index("tensor")
    dp_at = lax.axis_index("dp")
    parts = lax.axis_size("dp")
    micro, seqs, length, width = inputs.shape
    rows = seqs * length
    local, hidden = w_out.shape[1], w_up.shape[2]
    flags = jnp.stack([section, owner, dp_at % 2, dp_at // 2]).astype(jnp.int32)
    table = jnp.asarray(rope_tables(length))
    vecs = (g1, b1, g2, b2, b_qkv[0], b_out, b_up, b_down)
    ws = (w_qkv[0].transpose(1, 0, 2), w_out[0], w_up[0], w_down[0])
    xs = inputs.reshape(micro, rows, width)
    cots = cotangent.reshape(micro, rows, width)
    lined = parts == 8
    chips = parts // 2

    *outs, pack = call_f(flags, xs, table, ws, vecs)
    arrivals = []
    for m in range(micro):
        whole = call_add(m, xs, outs[m], swap(outs[m]))
        arrivals.append(lax.ppermute(whole, "section", [(0, 1)]))
    kept, sources, backs = [], [], []
    for m in range(micro):
        dx, source, *saved = call_fb(m, flags, xs, cots, arrivals[m], table, pack, ws)
        whole = call_add(m, cots, dx, swap(dx))
        backs.append(lax.ppermute(whole, "section", [(1, 0)]))
        kept.append(dict(zip(SAVED, saved)))
        sources.append(source)
    a1, a2, mixed, active = ([kept[m][n] for m in range(micro)] for n in ("a1", "a2", "mixed", "g"))

    after = ()
    if lined:
        theirs, mine = call_blocks(
            functools.partial(down_kernel, chips, micro),
            flags,
            (cots, *backs, *active, *mixed),
            [HB] + [VM] * (3 * micro),
            (chips, hidden // parts + local // parts, width),
            2 * micro * rows * width * (hidden + local),
            [pltpu.VMEM(cots.shape, BF), pltpu.SemaphoreType.DMA],
        )
        line_down = Line(theirs, mine, dp_at)
        after = line_down.start()
    pieces = [backs, sources] + [[kept[m][n] for m in range(micro)] for n in NEEDED]
    grad, du, dqkv, own, other, up = call_b(flags, cots, table, pack, ws, pieces, after)
    got = swap(other)
    share = width // parts
    if lined:
        after = (line_down.relay(), line_down.two, line_down.three, line_down.four)
        slabs = hidden // local
        lines = own.shape[0]
        theirs, mine = call_blocks(
            functools.partial(rest_kernel, chips, micro),
            flags,
            (du, dqkv, own, got, *a1, *a2, *after),
            [VM] * (4 + 2 * micro) + [HB] * len(after),
            (chips, (slabs + 3) * share + lines, local),
            2 * micro * rows * width * (hidden + 3 * local),
        )
        line_rest = Line(theirs, mine, dp_at)
        part = call_o(mixed, active, pack, ws, (mine,))
        line_rest.start()
        line_rest.relay()
        after = (line_rest.one,)
        down_rows = hidden // parts
        outs = [(down_rows, width), (local // parts, width)]
        d_wdown, d_wout = call_final(final_down_kernel, flags, line_down.parts(), outs, after)
        section_out, input_grad = call_tail(part, swap(part), up, grad, swap(grad), sources, after)
        outs = [(share, hidden), (3, share, local), (5, local // parts), (3, local // parts), (1, down_rows)]
        d_wup, d_wqkv, d_vec, d_bqkv, d_bup = call_final(
            final_rest_kernel, flags, line_rest.parts(), outs, (), [pltpu.VMEM((lines, local), F32)]
        )
        d_wqkv = d_wqkv.transpose(1, 0, 2)
    else:
        d_wdown = wide(active, [up]).reshape(parts, -1, width)
        d_wout = wide(mixed, [up]).reshape(parts, -1, width)
        d_both = scattered(jnp.concatenate([d_wdown, d_wout], axis=1))
        d_wup = scattered(wide(a2, [du]).reshape(parts, -1, hidden))
        d_wqkv = wide(a1, [dqkv]).reshape(parts, share, 3, local).transpose(0, 2, 1, 3)
        lines = jnp.concatenate([own[: got.shape[0]] + got, own[got.shape[0] :]]).astype(BF)
        lines = jnp.broadcast_to(lines[None], (parts,) + lines.shape)
        last = scattered(jnp.concatenate([d_wqkv.reshape(parts, 3 * share, local), lines], axis=1))
        down_rows = hidden // parts
        d_wdown, d_wout = d_both[:down_rows], d_both[down_rows:]
        d_wqkv = last[: 3 * share].reshape(3, share, local).transpose(1, 0, 2)
        lines = last[3 * share :]
        d_vec = lax.dynamic_slice(lines, (0, dp_at * (local // parts)), (8, local // parts))
        d_vec, d_bqkv = d_vec[:5], d_vec[5:]
        up_lines = lines[8 : 8 + hidden // local].reshape(1, hidden)
        d_bup = lax.dynamic_slice_in_dim(up_lines, dp_at * down_rows, down_rows, 1)
        part = call_o(mixed, active, pack, ws)
        section_out, input_grad = call_tail(part, swap(part), up, grad, swap(grad), sources, ())
    return (
        section_out.reshape(1, micro, seqs, length, width),
        input_grad.reshape(1, micro, seqs, length, width),
        d_vec[0:1],
        d_vec[1:2],
        d_vec[2:3],
        d_vec[3:4],
        d_wqkv[None],
        d_bqkv[None],
        d_wout[None],
        d_vec[4:5],
        d_wup[None],
        d_bup,
        d_wdown[None],
        d_vec[4:5],
    )


def solution(mesh):
    return jax.shard_map(
        per_device,
        mesh=mesh,
        in_specs=(
            P(None, "dp", None, None),
            P(None, "dp", None, None),
            P("section", None),
            P("section", None),
            P("section", None),
            P("section", None),
            P("section", None, None, "tensor"),
            P("section", None, "tensor"),
            P("section", "tensor", None),
            P("section", None),
            P("section", None, "tensor"),
            P("section", "tensor"),
            P("section", "tensor", None),
            P("section", None),
        ),
        out_specs=(
            P("section", None, "dp", None, None),
            P("section", None, "dp", None, None),
            P("section", ("tensor", "dp")),
            P("section", ("tensor", "dp")),
            P("section", ("tensor", "dp")),
            P("section", ("tensor", "dp")),
            P("section", "dp", None, "tensor"),
            P("section", None, ("tensor", "dp")),
            P("section", ("tensor", "dp"), None),
            P("section", ("tensor", "dp")),
            P("section", "dp", "tensor"),
            P("section", ("tensor", "dp")),
            P("section", ("tensor", "dp"), None),
            P("section", ("tensor", "dp")),
        ),
        check_vma=False,
    )
```

time: 185 us -> 172 us (0.930)
  waiting for transfers between devices: 25.6 us -> 54.9 us
  starting transfers between devices: 63.4 us -> 38.4 us
  Pallas kernels: 68.1 us -> 60.5 us
  other arithmetic: 15.5 us -> 9.26 us
  local copies, waits for them, and re-layouts: 9.86 us -> 7.2 us
    ppermute x21 -> x12, starting transfers between devices: 43.7 us -> 23 us  [the longest x10 22.9 us: send(): lax.ppermute(value, 'dp', [(2 * a + c, 2 * b + c) for a, b in pairs for c...]
    ppermute x8 -> x7, waiting for transfers between devices: 5.01 us -> 19.9 us  [swap(): return lax.ppermute(value, 'tensor', [(0, 1), (1, 0)])]
    ppermute x21 -> x12, waiting for transfers between devices: 18.9 us -> 27.7 us  [the longest x10 19.9 us: send(): lax.ppermute(value, 'dp', [(2 * a + c, 2 * b + c) for a, b in pairs for c...]
    pallas_call x4 -> x5, Pallas kernels: 30.4 us -> 24.5 us  [the longest x1 10.3 us: call_b(): pl.pallas_call(functools.partial(b_kernel, micro), out_shape=outs, in_spe...]
    ppermute x2, waiting for transfers between devices: 1.67 us -> 6.26 us  [per_device(): backs.append(lax.ppermute(whole, 'section', [(1, 0)]))]
    ppermute x8 -> x7, starting transfers between devices: 9.47 us -> 6.89 us  [swap(): return lax.ppermute(value, 'tensor', [(0, 1), (1, 0)])]
    another operation x3 -> x1, other arithmetic: 2.58 us -> 0.59 us  [per_device(): flags = jnp.stack([section, owner, dp_at % 2, dp_at // 2]).astype(jnp.int32)]
    pallas_call x3 -> x2, Pallas kernels: 11.8 us -> 10.1 us  [call_blocks(): pl.pallas_call(kernel, out_shape=outs, in_specs=[SM] + specs, out_specs=[...]
  transfers between devices with their start and end apart: 33 -> 23, of which waited for: 8 -> 12; matrix products, arithmetic and copies ran while one was open for 10% -> 2% of each run, Pallas kernels for 31% -> 23%
where the time goes in v2:
time: 172 us; the launch traced here: 171 us
  Pallas kernels  60.5 us (35%)
  waiting for transfers between devices  54.9 us (32%)
  starting transfers between devices  38.4 us (22%)
  other arithmetic  9.26 us (5%)
  local copies, waits for them, and re-layouts  7.2 us (4%)
    ppermute x10, starting transfers between devices, send(): lax.ppermute(value, 'dp', [(2 * a + c, 2 * b + c) for a, b in pairs for c...  22.9 us
    ppermute x7, waiting for transfers between devices, swap(): return lax.ppermute(value, 'tensor', [(0, 1), (1, 0)])  19.9 us
    ppermute x10, waiting for transfers between devices, send(): lax.ppermute(value, 'dp', [(2 * a + c, 2 * b + c) for a, b in pairs for c...  19.9 us
    pallas_call x2, Pallas kernels, call_fb(): pl.pallas_call(functools.partial(fb_kernel, at), out_shape=outs, in_specs...  19.8 us
    pallas_call x1, Pallas kernels, call_b(): pl.pallas_call(functools.partial(b_kernel, micro), out_shape=outs, in_spe...  10.3 us
    pallas_call x2, Pallas kernels, call_blocks(): pl.pallas_call(kernel, out_shape=outs, in_specs=[SM] + specs, out_specs=[...  10.1 us
    pallas_call x1, Pallas kernels, call_f(): pl.pallas_call(functools.partial(f_kernel, micro), out_shape=out, in_spec...  8.47 us
    ppermute x2, waiting for transfers between devices, __init__(): self.got = lax.ppermute(theirs, 'dp', [(i, i ^ 1) for i in range(8)])  7.82 us
  transfers between devices with their start and end apart: 23, of which 12 were waited for; matrix products, arithmetic and copies ran while one was open for 2% of the time, Pallas kernels for 23%

profile of v2, /device:TPU:0, one launch (start us, length us, event | category | flops | bytes accessed | tf_op | source)
XLA Modules:
  0.0 171.3 jit_solution(1693411455312866317)
XLA Ops:
  0.7 0.6 pad_add_fusion.refs_0_.flag_ref
  1.3 8.5 %shard_map.254 = (bf16[128,768]{1,0:T(8,128)(2,1)}, bf16[128,768]{1,0:T(8,128)(2,1)}, f32[16,1536]{1,0:T(8,128)}) custom-call(s32[4]{0:T(128)} %pad_add_fusion.refs_0_.flag_ref, bf16[2,128,768]{2,1,0:T(8,128)(2,1)} %bitcast.50, f32[3,128,128]{2,1,0:T(8,128)} %constant.102.clone.refs_2_.refs_4_, bf16[3,768,384]{2,1,0:T(8,128)(2,1)} %bitcast.71, ...), custom_call_target="tpu_custom_call" | custom-call | flops 1811939328 | bytes 7077888 | tf_op jit(solution)/shard_map/pallas_call | solution.py:586
  9.7 3.0 %collective-permute-start.2 = (bf16[128,768]{1,0:T(8,128)(2,1)}, bf16[128,768]{1,0:T(8,128)(2,1)S(1)}, u32[]{:S(2)}, u32[]{:S(2)}) collective-permute-start(bf16[128,768]{1,0:T(8,128)(2,1)} %get-tuple-element.61.one_ref), channel_id=1, source_target_pairs={{0,8},{8,0},{1,9},{9,1},{2,10},{10,2},{3,11},{11,3},{4,12},{12,4},... | collective-permute-start | bytes 589832 | tf_op jit(solution)/shard_map/ppermute | solution.py:719
  12.8 0.1 collective-permute-start
  12.8 5.9 %collective-permute-done.2.two_ref = bf16[128,768]{1,0:T(8,128)(2,1)S(1)} collective-permute-done((bf16[128,768]{1,0:T(8,128)(2,1)}, bf16[128,768]{1,0:T(8,128)(2,1)S(1)}, u32[]{:S(2)}, u32[]{:S(2)}) %collective-permute-start.2) | collective-permute-done | bytes 196640 | tf_op jit(solution)/shard_map/ppermute | solution.py:719
  18.7 0.9 copy-done.18
  19.6 0.3 shard_map.257
  19.9 3.9 %collective-permute-start.3 = (bf16[128,768]{1,0:T(8,128)(2,1)S(1)}, bf16[128,768]{1,0:T(8,128)(2,1)S(1)}, u32[]{:S(2)}, u32[]{:S(2)}) collective-permute-start(bf16[128,768]{1,0:T(8,128)(2,1)S(1)} %shard_map.257), channel_id=1, source_target_pairs={{0,16},{1,17},{2,18},{3,19},{4,20},{5,21},{6,22},{7,23},{8,24},{9,... | collective-permute-start | bytes 589832 | tf_op jit(solution)/shard_map/ppermute | solution.py:793
  23.9 0.0 copy-start.17
  23.9 0.9 copy-done.17
  24.8 0.3 shard_map.255
  25.1 2.0 %collective-permute-start.1 = (bf16[128,768]{1,0:T(8,128)(2,1)S(1)}, bf16[128,768]{1,0:T(8,128)(2,1)S(1)}, u32[]{:S(2)}, u32[]{:S(2)}) collective-permute-start(bf16[128,768]{1,0:T(8,128)(2,1)S(1)} %shard_map.255), channel_id=1, source_target_pairs={{0,16},{1,17},{2,18},{3,19},{4,20},{5,21},{6,22},{7,23},{8,24},{9,... | collective-permute-start | bytes 589832 | tf_op jit(solution)/shard_map/ppermute | solution.py:793
  27.1 1.0 collective-permute-done.3.refs_3_
  28.1 0.7 copy-done.24
  28.8 9.9 %shard_map.258 = (bf16[128,768]{1,0:T(8,128)(2,1)}, bf16[128,768]{1,0:T(8,128)(2,1)}, bf16[128,768]{1,0:T(8,128)(2,1)}, bf16[128,768]{1,0:T(8,128)(2,1)}, bf16[1...) custom-call(s32[4]{0:T(128)} %pad_add_fusion.refs_0_.flag_ref, ...), custom_call_target="tpu_custom_call" | custom-call | flops 1811939328 | bytes 7077888 | tf_op jit(solution)/shard_map/pallas_call | solution.py:609
  38.7 1.6 collective-permute-start.6
  40.3 0.7 copy-done.23
  41.0 9.9 %shard_map.256 = (bf16[128,768]{1,0:T(8,128)(2,1)}, bf16[128,768]{1,0:T(8,128)(2,1)}, bf16[128,768]{1,0:T(8,128)(2,1)}, bf16[128,768]{1,0:T(8,128)(2,1)}, bf16[1...) custom-call(s32[4]{0:T(128)} %pad_add_fusion.refs_0_.flag_ref, ...), custom_call_target="tpu_custom_call" | custom-call | flops 1811939328 | bytes 7077888 | tf_op jit(solution)/shard_map/pallas_call | solution.py:609
  50.9 0.6 collective-permute-start.4
  51.5 0.3 shard_map.260
  51.8 1.3 collective-permute-start.7
  53.1 3.7 %collective-permute-done.4.two_ref = bf16[128,768]{1,0:T(8,128)(2,1)S(1)} collective-permute-done((bf16[128,768]{1,0:T(8,128)(2,1)}, bf16[128,768]{1,0:T(8,128)(2,1)S(1)}, u32[]{:S(2)}, u32[]{:S(2)}) %collective-permute-start.4) | collective-permute-done | bytes 196640 | tf_op jit(solution)/shard_map/ppermute | solution.py:719
  56.9 0.9 copy-done.16
  57.8 0.3 shard_map.259
  58.1 1.3 collective-permute-start.5
  59.4 0.4 collective-permute-done.7.refs_3_.refs_9_
  59.8 5.8 %collective-permute-done.5.refs_2_.refs_8_ = bf16[128,768]{1,0:T(8,128)(2,1)S(1)} collective-permute-done((bf16[128,768]{1,0:T(8,128)(2,1)S(1)}, bf16[128,768]{1,0:T(8,128)(2,1)S(1)}, u32[]{:S(2)}, u32[]{:S(2)}) %collective-permute-start.5) | collective-permute-done | bytes 196640 | tf_op jit(solution)/shard_map/ppermute | solution.py:798
  65.7 0.7 copy-done.22
  66.3 4.9 %shard_map.261 = (bf16[4,240,768]{2,1,0:T(8,128)(2,1)}, bf16[4,240,768]{2,1,0:T(8,128)(2,1)}) custom-call(s32[4]{0:T(128)} %pad_add_fusion.refs_0_.flag_ref, bf16[2,128,768]{2,1,0:T(8,128)(2,1)} %bitcast.57, bf16[128,768]{1,0:T(8,128)(2,1)} %copy-done.22, bf16[128,768]{1,0:T(8,128)(2,1)} %copy-done.21, bf16[128,1536]{1,0:T(8,128)(2,1)} %get-tuple-element.63.refs_4_.refs_2_, ...), custom_call_target="tpu_custom_call" | custom-call | flops 754974720 | bytes 2949120 | tf_op jit(solution)/shard_map/pallas_call | solution.py:663
  71.2 0.1 collective-permute-start.8
  71.4 3.4 %collective-permute-done.8.refs_1_ = bf16[4,240,768]{2,1,0:T(8,128)(2,1)S(1)} collective-permute-done((bf16[4,240,768]{2,1,0:T(8,128)(2,1)}, bf16[4,240,768]{2,1,0:T(8,128)(2,1)S(1)}, u32[]{:S(2)}, u32[]{:S(2)}) %collective-permute-start.8) | collective-permute-done | bytes 1474592 | tf_op jit(solution)/shard_map/ppermute | solution.py:726
  74.8 2.6 %fusion.9 = (bf16[240,768]{1,0:T(8,128)(2,1)}, bf16[240,768]{1,0:T(8,128)(2,1)S(1)}, bf16[240,768]{1,0:T(8,128)(2,1)}, bf16[240,768]{1,0:T(8,128)(2,1)}) fusion(bf16[4,240,768]{2,1,0:T(8,128)(2,1)S(1)} %collective-permute-done.8.refs_1_, s32[]{:T(128)S(6)} %select_n.68, bf16[4,240,768]{2,1,0:T(8,128)(2,1)} %get-tuple-element.79.refs_0_, s32[]{:T(128)S(6)} %select_n.67, ...), kind=kLoop, calls=%fused_computation.19 | loop fusion | flops 2949120 | bytes 4423696 | tf_op jit(solution)/shard_map/convert_element_type | solution.py:739
  77.4 1.6 collective-permute-start.10
  78.9 2.4 %collective-permute-start.11 = (bf16[240,768]{1,0:T(8,128)(2,1)}, bf16[240,768]{1,0:T(8,128)(2,1)S(1)}, u32[]{:S(2)}, u32[]{:S(2)}) collective-permute-start(bf16[240,768]{1,0:T(8,128)(2,1)} %get-tuple-element.120.refs_25_), channel_id=1, source_target_pairs={{0,2},{1,3},{6,4},{7,5},{8,10},{9,11},{14,12},{15,13},{16,18},{17,... | collective-permute-start | bytes 1105928 | tf_op jit(solution)/shard_map/ppermute | solution.py:734
  81.3 0.7 collective-permute-start.12
  82.0 4.9 %collective-permute-start.13 = (bf16[240,768]{1,0:T(8,128)(2,1)S(1)}, bf16[240,768]{1,0:T(8,128)(2,1)S(1)}, u32[]{:S(2)}, u32[]{:S(2)}) collective-permute-start(bf16[240,768]{1,0:T(8,128)(2,1)S(1)} %get-tuple-element.121.refs_24_), channel_id=1, source_target_pairs={{0,4},{1,5},{6,2},{7,3},{8,12},{9,13},{14,10},{15,11},{16,20},{17,... | collective-permute-start | bytes 1105928 | tf_op jit(solution)/shard_map/ppermute | solution.py:734
  86.9 10.3 %shard_map.262 = (bf16[256,768]{1,0:T(8,128)(2,1)}, bf16[256,1536]{1,0:T(8,128)(2,1)}, bf16[256,1152]{1,0:T(8,128)(2,1)}, f32[16,384]{1,0:T(8,128)}, f32[8,384]{1,0:T(8,128)}, /*index=5*/bf16[256,768]{1,0:T(8,128)(2,1)}) custom-call(s32[4]{0:T(128)} %pad_add_fusion.refs_0_.flag_ref, bf16[2,128,768]{2,1,0:T(8,128)(2,1)} %bitcast.58, ...), custom_call_target="tpu_custom_call" | custom-call | flops 1811939328 | bytes 7077888 | tf_op jit(solution)/shard_map/pallas_call | solution.py:646
  97.2 0.6 collective-permute-start.9
  97.8 0.9 fusion.1.refs_9_
  98.7 2.5 %collective-permute-done.9.refs_4_ = f32[8,384]{1,0:T(8,128)S(1)} collective-permute-done((f32[8,384]{1,0:T(8,128)}, f32[8,384]{1,0:T(8,128)S(1)}, u32[]{:S(2)}, u32[]{:S(2)}) %collective-permute-start.9) | collective-permute-done | bytes 12320 | tf_op jit(solution)/shard_map/ppermute | solution.py:719
  101.2 1.9 %collective-permute-done.13.refs_12_.refs_5_ = bf16[240,768]{1,0:T(8,128)(2,1)S(1)} collective-permute-done((bf16[240,768]{1,0:T(8,128)(2,1)S(1)}, bf16[240,768]{1,0:T(8,128)(2,1)S(1)}, u32[]{:S(2)}, u32[]{:S(2)}) %collective-permute-start.13) | collective-permute-done | bytes 368672 | tf_op jit(solution)/shard_map/ppermute | solution.py:734
  103.1 0.7 copy-done.13
  103.8 5.2 %shard_map.263 = (bf16[4,688,384]{2,1,0:T(8,128)(2,1)}, bf16[4,688,384]{2,1,0:T(8,128)(2,1)}) custom-call(s32[4]{0:T(128)} %pad_add_fusion.refs_0_.flag_ref, bf16[256,1536]{1,0:T(8,128)(2,1)} %get-tuple-element.81.refs_1_, bf16[256,1152]{1,0:T(8,128)(2,1)} %get-tuple-element.82.refs_2_, f32[16,384]{1,0:T(8,128)} %get-tuple-element.83.refs_3_, ...), custom_call_target="tpu_custom_call" | custom-call | flops 1056964608 | bytes 4227072 | tf_op jit(solution)/shard_map/pallas_call | solution.py:663
  109.0 4.4 %collective-permute-done.16.refs_1_ = bf16[4,688,384]{2,1,0:T(8,128)(2,1)S(1)} collective-permute-done((bf16[4,688,384]{2,1,0:T(8,128)(2,1)}, bf16[4,688,384]{2,1,0:T(8,128)(2,1)S(1)}, u32[]{:S(2)}, u32[]{:S(2)}) %collective-permute-start.16) | collective-permute-done | bytes 2113568 | tf_op jit(solution)/shard_map/ppermute | solution.py:726
  113.4 3.1 %fusion.5 = (bf16[688,384]{1,0:T(8,128)(2,1)}, bf16[688,384]{1,0:T(8,128)(2,1)}, bf16[688,384]{1,0:T(8,128)(2,1)}, bf16[688,384]{1,0:T(8,128)(2,1)S(1)}) fusion(bf16[4,688,384]{2,1,0:T(8,128)(2,1)S(1)} %collective-permute-done.16.refs_1_, s32[]{:T(128)S(6)} %select_n.67, bf16[4,688,384]{2,1,0:T(8,128)(2,1)} %get-tuple-element.89.refs_7_.refs_0_, ...), kind=kLoop, calls=%fused_computation.15 | loop fusion | flops 4227072 | bytes 6340624 | tf_op jit(solution)/shard_map/convert_element_type | solution.py:739
  116.6 3.5 %collective-permute-start.17 = (bf16[688,384]{1,0:T(8,128)(2,1)S(1)}, bf16[688,384]{1,0:T(8,128)(2,1)S(1)}, u32[]{:S(2)}, u32[]{:S(2)}) collective-permute-start(bf16[688,384]{1,0:T(8,128)(2,1)S(1)} %get-tuple-element.119), channel_id=1, source_target_pairs={{0,2},{1,3},{2,0},{3,1},{4,6},{5,7},{6,4},{7,5},{8,10},{9,11},{10,... | collective-permute-start | bytes 1585160 | tf_op jit(solution)/shard_map/ppermute | solution.py:734
  120.1 0.5 collective-permute-start.15
  120.6 1.3 collective-permute-start.22
  121.8 5.2 %collective-permute-start.18 = (bf16[688,384]{1,0:T(8,128)(2,1)}, bf16[688,384]{1,0:T(8,128)(2,1)S(1)}, u32[]{:S(2)}, u32[]{:S(2)}) collective-permute-start(bf16[688,384]{1,0:T(8,128)(2,1)} %get-tuple-element.118), channel_id=1, source_target_pairs={{0,2},{1,3},{6,4},{7,5},{8,10},{9,11},{14,12},{15,13},{16,18},{17,... | collective-permute-start | bytes 1585160 | tf_op jit(solution)/shard_map/ppermute | solution.py:734
  127.1 0.7 collective-permute-start.19
  127.8 12.5 %collective-permute-done.17.refs_7_.refs_2_ = bf16[688,384]{1,0:T(8,128)(2,1)S(1)} collective-permute-done((bf16[688,384]{1,0:T(8,128)(2,1)S(1)}, bf16[688,384]{1,0:T(8,128)(2,1)S(1)}, u32[]{:S(2)}, u32[]{:S(2)}) %collective-permute-start.17) | collective-permute-done | bytes 528416 | tf_op jit(solution)/shard_map/ppermute | solution.py:734
  140.3 1.4 collective-permute-start.20
  141.6 2.0 %fusion = bf16[688,384]{1,0:T(8,128)(2,1)} fusion(bf16[688,384]{1,0:T(8,128)(2,1)S(1)} %collective-permute-done.17.refs_7_.refs_2_, bf16[4,688,384]{2,1,0:T(8,128)(2,1)S(1)} %collective-permute-done.16.refs_1_, s32[]{:T(128)S(6)} %select_n.69, bf16[4,688,384]{2,1,0:T(8,128)(2,1)} %get-tuple-element.89.refs_7_.refs_0_), kind=kLoop, calls=%fused_computation.1 | loop fusion | flops 1585152 | bytes 2113540 | tf_op jit(solution)/shard_map/convert_element_type | solution.py:754
  143.7 1.4 collective-permute-start.21
  145.1 4.8 %shard_map.264.refs_0_ = bf16[256,768]{1,0:T(8,128)(2,1)} custom-call(bf16[128,384]{1,0:T(8,128)(2,1)} %get-tuple-element.60.refs_6_.refs_0_, bf16[128,384]{1,0:T(8,128)(2,1)} %get-tuple-element.62.refs_7_.refs_1_, bf16[128,1536]{1,0:T(8,128)(2,1)} %get-tuple-element.63.refs_4_.refs_2_, bf16[128,1536]{1,0:T(8,128)(2,1)} %get-tuple-element.64.refs_5_.refs_3_, ...), custom_call_target="tpu_custom_call" | custom-call | flops 754974720 | bytes 2949120 | tf_op jit(solution)/shard_map/pallas_call | solution.py:701
  150.0 0.6 collective-permute-start.14
  150.6 2.5 %shard_map.267 = (f32[192,768]{1,0:T(8,128)}, f32[48,768]{1,0:T(8,128)}) custom-call(s32[4]{0:T(128)S(1)} %copy-done.19, bf16[4,240,768]{2,1,0:T(8,128)(2,1)S(1)} %copy-done.3, bf16[4,240,768]{2,1,0:T(8,128)(2,1)S(1)} %collective-permute-done.8.refs_1_, bf16[240,768]{1,0:T(8,128)(2,1)S(1)} %collective-permute-done.10.refs_2_, ...), custom_call_target="tpu_custom_call" | custom-call | tf_op jit(solution)/shard_map/pallas_call | solution.py:675
  153.1 7.8 %collective-permute-done.14.refs_1_ = bf16[256,768]{1,0:T(8,128)(2,1)S(1)} collective-permute-done((bf16[256,768]{1,0:T(8,128)(2,1)}, bf16[256,768]{1,0:T(8,128)(2,1)S(1)}, u32[]{:S(2)}, u32[]{:S(2)}) %collective-permute-start.14) | collective-permute-done | bytes 393248 | tf_op jit(solution)/shard_map/ppermute | solution.py:719
  160.9 1.2 shard_map.265
  162.1 5.5 %collective-permute-done.21.refs_6_ = bf16[688,384]{1,0:T(8,128)(2,1)S(1)} collective-permute-done((bf16[688,384]{1,0:T(8,128)(2,1)}, bf16[688,384]{1,0:T(8,128)(2,1)S(1)}, u32[]{:S(2)}, u32[]{:S(2)}) %collective-permute-start.21) | collective-permute-done | bytes 528416 | tf_op jit(solution)/shard_map/ppermute | solution.py:734
  167.6 2.0 %shard_map.266 = (f32[96,1536]{1,0:T(8,128)}, f32[3,96,384]{2,1,0:T(8,128)}, f32[5,48]{1,0:T(8,128)S(1)}, f32[3,48]{1,0:T(4,128)S(1)}, f32[1,192]{1,0:T(1,128)}) custom-call(s32[4]{0:T(128)S(1)} %copy-done.19, bf16[4,688,384]{2,1,0:T(8,128)(2,1)S(1)} %copy-done, bf16[4,688,384]{2,1,0:T(8,128)(2,1)S(1)} %collective-permute-done.16.refs_1_, ...), custom_call_target="tpu_custom_call" | custom-call | tf_op jit(solution)/shard_map/pallas_call | solution.py:675
  169.7 0.5 fusion.10
  170.2 0.6 copy.31
  170.8 0.5 copy.33
  (58 shorter events, 0.1 us)
Async XLA Ops:
  1.3 17.5 %copy-start.1 = (bf16[2,1,128,768]{3,2,1,0:T(8,128)(2,1)S(1)}, bf16[2,1,128,768]{3,2,1,0:T(8,128)(2,1)}, u32[]{:S(2)}) copy-start(bf16[2,1,128,768]{3,2,1,0:T(8,128)(2,1)} %param.15) | copy-start | bytes 1179652
  9.7 9.0 %collective-permute-start.2 = (bf16[128,768]{1,0:T(8,128)(2,1)}, bf16[128,768]{1,0:T(8,128)(2,1)S(1)}, u32[]{:S(2)}, u32[]{:S(2)}) collective-permute-start(bf16[128,768]{1,0:T(8,128)(2,1)} %get-tuple-element.61.one_ref), channel_id=1, source_target_pairs={{0,8},{8,0},{1,9},{9,1},{2,10},{10,2},{3,11},{11,3},{4,12},{12,4},... | collective-permute-start | bytes 589832 | tf_op jit(solution)/shard_map/ppermute | solution.py:719
  12.8 11.1 %collective-permute-start = (bf16[128,768]{1,0:T(8,128)(2,1)}, bf16[128,768]{1,0:T(8,128)(2,1)S(1)}, u32[]{:S(2)}, u32[]{:S(2)}) collective-permute-start(bf16[128,768]{1,0:T(8,128)(2,1)} %get-tuple-element.58.one_ref), channel_id=1, source_target_pairs={{0,8},{8,0},{1,9},{9,1},{2,10},{10,2},{3,11},{11,3},{4,12},{12,4},... | collective-permute-start | bytes 589832 | tf_op jit(solution)/shard_map/ppermute | solution.py:719
  18.7 0.9 copy-start.18
  19.9 8.2 %collective-permute-start.3 = (bf16[128,768]{1,0:T(8,128)(2,1)S(1)}, bf16[128,768]{1,0:T(8,128)(2,1)S(1)}, u32[]{:S(2)}, u32[]{:S(2)}) collective-permute-start(bf16[128,768]{1,0:T(8,128)(2,1)S(1)} %shard_map.257), channel_id=1, source_target_pairs={{0,16},{1,17},{2,18},{3,19},{4,20},{5,21},{6,22},{7,23},{8,24},{9,... | collective-permute-start | bytes 589832 | tf_op jit(solution)/shard_map/ppermute | solution.py:793
  23.9 0.9 copy-start.17
  25.1 15.2 %collective-permute-start.1 = (bf16[128,768]{1,0:T(8,128)(2,1)S(1)}, bf16[128,768]{1,0:T(8,128)(2,1)S(1)}, u32[]{:S(2)}, u32[]{:S(2)}) collective-permute-start(bf16[128,768]{1,0:T(8,128)(2,1)S(1)} %shard_map.255), channel_id=1, source_target_pairs={{0,16},{1,17},{2,18},{3,19},{4,20},{5,21},{6,22},{7,23},{8,24},{9,... | collective-permute-start | bytes 589832 | tf_op jit(solution)/shard_map/ppermute | solution.py:793
  28.1 0.7 copy-start.24
  38.7 12.8 %copy-start.2 = (bf16[2,1,128,768]{3,2,1,0:T(8,128)(2,1)S(1)}, bf16[2,1,128,768]{3,2,1,0:T(8,128)(2,1)}, u32[]{:S(2)}) copy-start(bf16[2,1,128,768]{3,2,1,0:T(8,128)(2,1)} %param.16) | copy-start | bytes 1179652
  38.7 12.8 %copy-start.15 = (bf16[128,768]{1,0:T(8,128)(2,1)S(1)}, bf16[128,768]{1,0:T(8,128)(2,1)}, u32[]{:S(2)}) copy-start(bf16[128,768]{1,0:T(8,128)(2,1)} %get-tuple-element.66.one_ref) | copy-start | bytes 589828
  38.7 12.8 %collective-permute-start.6 = (bf16[128,768]{1,0:T(8,128)(2,1)}, bf16[128,768]{1,0:T(8,128)(2,1)S(1)}, u32[]{:S(2)}, u32[]{:S(2)}) collective-permute-start(bf16[128,768]{1,0:T(8,128)(2,1)} %get-tuple-element.66.one_ref), channel_id=1, source_target_pairs={{0,8},{8,0},{1,9},{9,1},{2,10},{10,2},{3,11},{11,3},{4,12},{12,4},... | collective-permute-start | bytes 589832 | tf_op jit(solution)/shard_map/ppermute | solution.py:719
  40.3 0.7 copy-start.23
  50.9 5.9 %collective-permute-start.4 = (bf16[128,768]{1,0:T(8,128)(2,1)}, bf16[128,768]{1,0:T(8,128)(2,1)S(1)}, u32[]{:S(2)}, u32[]{:S(2)}) collective-permute-start(bf16[128,768]{1,0:T(8,128)(2,1)} %get-tuple-element.65.one_ref), channel_id=1, source_target_pairs={{0,8},{8,0},{1,9},{9,1},{2,10},{10,2},{3,11},{11,3},{4,12},{12,4},... | collective-permute-start | bytes 589832 | tf_op jit(solution)/shard_map/ppermute | solution.py:719
  51.8 8.0 %collective-permute-start.7 = (bf16[128,768]{1,0:T(8,128)(2,1)S(1)}, bf16[128,768]{1,0:T(8,128)(2,1)S(1)}, u32[]{:S(2)}, u32[]{:S(2)}) collective-permute-start(bf16[128,768]{1,0:T(8,128)(2,1)S(1)} %shard_map.260), channel_id=1, source_target_pairs={{16,0},{17,1},{18,2},{19,3},{20,4},{21,5},{22,6},{23,7},{24,8},{25... | collective-permute-start | bytes 589832 | tf_op jit(solution)/shard_map/ppermute | solution.py:798
  56.9 0.9 copy-start.16
  58.1 7.6 %collective-permute-start.5 = (bf16[128,768]{1,0:T(8,128)(2,1)S(1)}, bf16[128,768]{1,0:T(8,128)(2,1)S(1)}, u32[]{:S(2)}, u32[]{:S(2)}) collective-permute-start(bf16[128,768]{1,0:T(8,128)(2,1)S(1)} %shard_map.259), channel_id=1, source_target_pairs={{16,0},{17,1},{18,2},{19,3},{20,4},{21,5},{22,6},{23,7},{24,8},{25... | collective-permute-start | bytes 589832 | tf_op jit(solution)/shard_map/ppermute | solution.py:798
  59.8 5.8 %copy-start.21 = (bf16[128,768]{1,0:T(8,128)(2,1)}, bf16[128,768]{1,0:T(8,128)(2,1)S(1)}, u32[]{:S(2)}) copy-start(bf16[128,768]{1,0:T(8,128)(2,1)S(1)} %collective-permute-done.7.refs_3_.refs_9_) | copy-start | bytes 589828
  65.7 0.7 copy-start.22
  71.2 3.5 %collective-permute-start.8 = (bf16[4,240,768]{2,1,0:T(8,128)(2,1)}, bf16[4,240,768]{2,1,0:T(8,128)(2,1)S(1)}, u32[]{:S(2)}, u32[]{:S(2)}) collective-permute-start(bf16[4,240,768]{2,1,0:T(8,128)(2,1)} %get-tuple-element.80), channel_id=1, source_target_pairs={{0,1},{1,0},{2,3},{3,2},{4,5},{5,4},{6,7},{7,6},{8,9},{9,8},{10,11... | collective-permute-start | bytes 4423688 | tf_op jit(solution)/shard_map/ppermute | solution.py:726
  77.4 9.5 %copy-start.20 = (bf16[240,768]{1,0:T(8,128)(2,1)}, bf16[240,768]{1,0:T(8,128)(2,1)S(1)}, u32[]{:S(2)}) copy-start(bf16[240,768]{1,0:T(8,128)(2,1)S(1)} %get-tuple-element.121.refs_24_) | copy-start | bytes 1105924
  77.4 20.4 %collective-permute-start.10 = (bf16[240,768]{1,0:T(8,128)(2,1)}, bf16[240,768]{1,0:T(8,128)(2,1)S(1)}, u32[]{:S(2)}, u32[]{:S(2)}) collective-permute-start(bf16[240,768]{1,0:T(8,128)(2,1)} %get-tuple-element.123.refs_22_), channel_id=1, source_target_pairs={{0,2},{1,3},{2,0},{3,1},{4,6},{5,7},{6,4},{7,5},{8,10},{9,11},{10,... | collective-permute-start | bytes 1105928 | tf_op jit(solution)/shard_map/ppermute | solution.py:734
  78.9 22.3 %collective-permute-start.11 = (bf16[240,768]{1,0:T(8,128)(2,1)}, bf16[240,768]{1,0:T(8,128)(2,1)S(1)}, u32[]{:S(2)}, u32[]{:S(2)}) collective-permute-start(bf16[240,768]{1,0:T(8,128)(2,1)} %get-tuple-element.120.refs_25_), channel_id=1, source_target_pairs={{0,2},{1,3},{6,4},{7,5},{8,10},{9,11},{14,12},{15,13},{16,18},{17,... | collective-permute-start | bytes 1105928 | tf_op jit(solution)/shard_map/ppermute | solution.py:734
  81.3 19.9 %collective-permute-start.12 = (bf16[240,768]{1,0:T(8,128)(2,1)}, bf16[240,768]{1,0:T(8,128)(2,1)S(1)}, u32[]{:S(2)}, u32[]{:S(2)}) collective-permute-start(bf16[240,768]{1,0:T(8,128)(2,1)} %get-tuple-element.122.refs_23_), channel_id=1, source_target_pairs={{2,4},{3,5},{4,2},{5,3},{10,12},{11,13},{12,10},{13,11},{18,20},{1... | collective-permute-start | bytes 1105928 | tf_op jit(solution)/shard_map/ppermute | solution.py:734
  82.0 21.1 %collective-permute-start.13 = (bf16[240,768]{1,0:T(8,128)(2,1)S(1)}, bf16[240,768]{1,0:T(8,128)(2,1)S(1)}, u32[]{:S(2)}, u32[]{:S(2)}) collective-permute-start(bf16[240,768]{1,0:T(8,128)(2,1)S(1)} %get-tuple-element.121.refs_24_), channel_id=1, source_target_pairs={{0,4},{1,5},{6,2},{7,3},{8,12},{9,13},{14,10},{15,11},{16,20},{17,... | collective-permute-start | bytes 1105928 | tf_op jit(solution)/shard_map/ppermute | solution.py:734
  86.9 10.9 %copy-start.3 = (bf16[4,240,768]{2,1,0:T(8,128)(2,1)S(1)}, bf16[4,240,768]{2,1,0:T(8,128)(2,1)}, u32[]{:S(2)}) copy-start(bf16[4,240,768]{2,1,0:T(8,128)(2,1)} %get-tuple-element.79.refs_0_) | copy-start | bytes 4423684
  97.2 4.0 %collective-permute-start.9 = (f32[8,384]{1,0:T(8,128)}, f32[8,384]{1,0:T(8,128)S(1)}, u32[]{:S(2)}, u32[]{:S(2)}) collective-permute-start(f32[8,384]{1,0:T(8,128)} %get-tuple-element.84), channel_id=1, source_target_pairs={{0,8},{8,0},{1,9},{9,1},{2,10},{10,2},{3,11},{11,3},{4,12},{12,4},... | collective-permute-start | bytes 36872 | tf_op jit(solution)/shard_map/ppermute | solution.py:719
  101.2 1.9 %copy-start.26 = (f32[8,384]{1,0:T(8,128)}, f32[8,384]{1,0:T(8,128)S(1)}, u32[]{:S(2)}) copy-start(f32[8,384]{1,0:T(8,128)S(1)} %collective-permute-done.9.refs_4_) | copy-start | bytes 36868
  101.2 1.9 %copy-start.9 = (bf16[240,768]{1,0:T(8,128)(2,1)}, bf16[240,768]{1,0:T(8,128)(2,1)S(1)}, u32[]{:S(2)}) copy-start(bf16[240,768]{1,0:T(8,128)(2,1)S(1)} %collective-permute-done.11.refs_10_.refs_3_) | copy-start | bytes 1105924
  101.2 1.9 %copy-start.11 = (bf16[240,768]{1,0:T(8,128)(2,1)}, bf16[240,768]{1,0:T(8,128)(2,1)S(1)}, u32[]{:S(2)}) copy-start(bf16[240,768]{1,0:T(8,128)(2,1)S(1)} %collective-permute-done.12.refs_11_.refs_4_) | copy-start | bytes 1105924
  103.1 0.7 copy-start.13
  109.0 4.4 %collective-permute-start.16 = (bf16[4,688,384]{2,1,0:T(8,128)(2,1)}, bf16[4,688,384]{2,1,0:T(8,128)(2,1)S(1)}, u32[]{:S(2)}, u32[]{:S(2)}) collective-permute-start(bf16[4,688,384]{2,1,0:T(8,128)(2,1)} %get-tuple-element.92), channel_id=1, source_target_pairs={{0,1},{1,0},{2,3},{3,2},{4,5},{5,4},{6,7},{7,6},{8,9},{9,8},{10,11... | collective-permute-start | bytes 6340616 | tf_op jit(solution)/shard_map/ppermute | solution.py:726
  113.4 6.6 %copy-start.7 = (bf16[256,768]{1,0:T(8,128)(2,1)S(1)}, bf16[256,768]{1,0:T(8,128)(2,1)}, u32[]{:S(2)}) copy-start(bf16[256,768]{1,0:T(8,128)(2,1)} %get-tuple-element.91.refs_3_) | copy-start | bytes 1179652
  116.6 23.7 %collective-permute-start.17 = (bf16[688,384]{1,0:T(8,128)(2,1)S(1)}, bf16[688,384]{1,0:T(8,128)(2,1)S(1)}, u32[]{:S(2)}, u32[]{:S(2)}) collective-permute-start(bf16[688,384]{1,0:T(8,128)(2,1)S(1)} %get-tuple-element.119), channel_id=1, source_target_pairs={{0,2},{1,3},{2,0},{3,1},{4,6},{5,7},{6,4},{7,5},{8,10},{9,11},{10,... | collective-permute-start | bytes 1585160 | tf_op jit(solution)/shard_map/ppermute | solution.py:734
  120.1 23.6 %collective-permute-start.15 = (bf16[256,768]{1,0:T(8,128)(2,1)S(1)}, bf16[256,768]{1,0:T(8,128)(2,1)S(1)}, u32[]{:S(2)}, u32[]{:S(2)}) collective-permute-start(bf16[256,768]{1,0:T(8,128)(2,1)S(1)} %copy-done.7), channel_id=1, source_target_pairs={{0,8},{8,0},{1,9},{9,1},{2,10},{10,2},{3,11},{11,3},{4,12},{12,4},... | collective-permute-start | bytes 1179656 | tf_op jit(solution)/shard_map/ppermute | solution.py:719
  120.6 29.4 %collective-permute-start.22 = (bf16[240,768]{1,0:T(8,128)(2,1)}, bf16[240,768]{1,0:T(8,128)(2,1)}, u32[]{:S(2)}, u32[]{:S(2)}) collective-permute-start(bf16[240,768]{1,0:T(8,128)(2,1)} %fusion.1.refs_9_), channel_id=1, source_target_pairs={{2,6},{3,7},{4,0},{5,1},{10,14},{11,15},{12,8},{13,9},{18,22},{19,... | collective-permute-start | bytes 1105928 | tf_op jit(solution)/shard_map/ppermute | solution.py:734
  121.8 40.3 %collective-permute-start.18 = (bf16[688,384]{1,0:T(8,128)(2,1)}, bf16[688,384]{1,0:T(8,128)(2,1)S(1)}, u32[]{:S(2)}, u32[]{:S(2)}) collective-permute-start(bf16[688,384]{1,0:T(8,128)(2,1)} %get-tuple-element.118), channel_id=1, source_target_pairs={{0,2},{1,3},{6,4},{7,5},{8,10},{9,11},{14,12},{15,13},{16,18},{17,... | collective-permute-start | bytes 1585160 | tf_op jit(solution)/shard_map/ppermute | solution.py:734
  127.1 35.1 %collective-permute-start.19 = (bf16[688,384]{1,0:T(8,128)(2,1)}, bf16[688,384]{1,0:T(8,128)(2,1)S(1)}, u32[]{:S(2)}, u32[]{:S(2)}) collective-permute-start(bf16[688,384]{1,0:T(8,128)(2,1)} %get-tuple-element.117), channel_id=1, source_target_pairs={{2,4},{3,5},{4,2},{5,3},{10,12},{11,13},{12,10},{13,11},{18,20},{1... | collective-permute-start | bytes 1585160 | tf_op jit(solution)/shard_map/ppermute | solution.py:734
  140.3 21.9 %collective-permute-start.20 = (bf16[688,384]{1,0:T(8,128)(2,1)}, bf16[688,384]{1,0:T(8,128)(2,1)S(1)}, u32[]{:S(2)}, u32[]{:S(2)}) collective-permute-start(bf16[688,384]{1,0:T(8,128)(2,1)} %get-tuple-element.116), channel_id=1, source_target_pairs={{0,4},{1,5},{6,2},{7,3},{8,12},{9,13},{14,10},{15,11},{16,20},{17,... | collective-permute-start | bytes 1585160 | tf_op jit(solution)/shard_map/ppermute | solution.py:734
  143.7 6.9 %copy-start.10 = (bf16[240,768]{1,0:T(8,128)(2,1)S(1)}, bf16[240,768]{1,0:T(8,128)(2,1)}, u32[]{:S(2)}) copy-start(bf16[240,768]{1,0:T(8,128)(2,1)} %copy-done.9) | copy-start | bytes 1105924
  143.7 6.9 %copy-start.12 = (bf16[240,768]{1,0:T(8,128)(2,1)S(1)}, bf16[240,768]{1,0:T(8,128)(2,1)}, u32[]{:S(2)}) copy-start(bf16[240,768]{1,0:T(8,128)(2,1)} %copy-done.11) | copy-start | bytes 1105924
  143.7 6.9 %copy-start.14 = (bf16[240,768]{1,0:T(8,128)(2,1)S(1)}, bf16[240,768]{1,0:T(8,128)(2,1)}, u32[]{:S(2)}) copy-start(bf16[240,768]{1,0:T(8,128)(2,1)} %copy-done.13) | copy-start | bytes 1105924
  143.7 6.9 %copy-start.19 = (s32[4]{0:T(128)S(1)}, s32[4]{0:T(128)}, u32[]{:S(2)}) copy-start(s32[4]{0:T(128)} %pad_add_fusion.refs_0_.flag_ref) | copy-start | bytes 52
  143.7 23.9 %collective-permute-start.21 = (bf16[688,384]{1,0:T(8,128)(2,1)}, bf16[688,384]{1,0:T(8,128)(2,1)S(1)}, u32[]{:S(2)}, u32[]{:S(2)}) collective-permute-start(bf16[688,384]{1,0:T(8,128)(2,1)} %fusion), channel_id=1, source_target_pairs={{2,6},{3,7},{4,0},{5,1},{10,14},{11,15},{12,8},{13,9},{18,22},{19,... | collective-permute-start | bytes 1585160 | tf_op jit(solution)/shard_map/ppermute | solution.py:734
  149.9 10.9 %copy-start.4 = (bf16[256,768]{1,0:T(8,128)(2,1)S(1)}, bf16[256,768]{1,0:T(8,128)(2,1)}, u32[]{:S(2)}) copy-start(bf16[256,768]{1,0:T(8,128)(2,1)} %shard_map.264.refs_0_) | copy-start | bytes 1179652
  150.0 10.9 %copy-start.5 = (bf16[128,768]{1,0:T(8,128)(2,1)S(1)}, bf16[128,768]{1,0:T(8,128)(2,1)}, u32[]{:S(2)}) copy-start(bf16[128,768]{1,0:T(8,128)(2,1)} %get-tuple-element.68.refs_11_.refs_6_) | copy-start | bytes 589828
  150.0 10.9 %copy-start.6 = (bf16[128,768]{1,0:T(8,128)(2,1)S(1)}, bf16[128,768]{1,0:T(8,128)(2,1)}, u32[]{:S(2)}) copy-start(bf16[128,768]{1,0:T(8,128)(2,1)} %get-tuple-element.67.refs_10_.refs_5_) | copy-start | bytes 589828
  150.0 10.9 %copy-start.8 = (bf16[256,768]{1,0:T(8,128)(2,1)S(1)}, bf16[256,768]{1,0:T(8,128)(2,1)}, u32[]{:S(2)}) copy-start(bf16[256,768]{1,0:T(8,128)(2,1)} %get-tuple-element.90.refs_2_) | copy-start | bytes 1179652
  150.0 10.9 %collective-permute-start.14 = (bf16[256,768]{1,0:T(8,128)(2,1)}, bf16[256,768]{1,0:T(8,128)(2,1)S(1)}, u32[]{:S(2)}, u32[]{:S(2)}) collective-permute-start(bf16[256,768]{1,0:T(8,128)(2,1)} %shard_map.264.refs_0_), channel_id=1, source_target_pairs={{0,8},{8,0},{1,9},{9,1},{2,10},{10,2},{3,11},{11,3},{4,12},{12,4},... | collective-permute-start | bytes 1179656 | tf_op jit(solution)/shard_map/ppermute | solution.py:719
  153.0 14.6 %copy-start = (bf16[4,688,384]{2,1,0:T(8,128)(2,1)S(1)}, bf16[4,688,384]{2,1,0:T(8,128)(2,1)}, u32[]{:S(2)}) copy-start(bf16[4,688,384]{2,1,0:T(8,128)(2,1)} %get-tuple-element.89.refs_7_.refs_0_) | copy-start | bytes 6340612
  170.2 1.1 copy-start.25

commit v3 on v2

--- a/solution.py
+++ b/solution.py
@@ -290,8 +290,13 @@
         out_refs[m][...] = out[m * rows : (m + 1) * rows]
 
 
+def received(base, one, two):
+    return (base.astype(F32) + (one.astype(F32) + two.astype(F32))).astype(BF)
+
+
 def fb_kernel(at, *refs):
-    flag_ref, x_hbm, dy_hbm, arrived_hbm, table_hbm, pack_hbm = refs[:6]
+    flag_ref, x_hbm, dy_hbm, arrived_hbm, beside_hbm, table_hbm, pack_hbm = refs[:7]
+    refs = refs[1:]
     hbm = dict(zip(WEIGHTS, refs[6:10]))
     names = ("dx", "source") + SAVED
     outs = dict(zip(names, refs[10 : 10 + len(names)]))
@@ -299,10 +304,11 @@
     held = dict(zip(names, refs[: len(names)]))
     refs = refs[len(names) :]
     w = dict(zip(WEIGHTS, refs[:4]))
-    du, dqkv, x_ref, dy_ref, arrived_ref, table_ref, pack_ref, sems, out_sems = refs[4:]
-    loads, stores = Loads(sems, AHEAD + 2), Loads(out_sems)
+    du, dqkv, x_ref, dy_ref, arrived_ref, beside_ref, table_ref, pack_ref, sems, out_sems = refs[4:]
+    loads, stores = Loads(sems), Loads(out_sems)
     loads.start("x", x_hbm.at[at], x_ref)
     loads.start("arrived", arrived_hbm, arrived_ref)
+    loads.start("arrived", beside_hbm, beside_ref)
     loads.start("pack", pack_hbm, pack_ref)
     loads.weight("wqkv", hbm, w)
     loads.start("table", table_hbm, table_ref)
@@ -320,7 +326,8 @@
     width, (local, hidden) = x_ref.shape[1], (dqkv.shape[1] // 3, du.shape[1])
     loads.wait("x")
     loads.wait("arrived")
-    x = jnp.where(flag_ref[0] == 0, x_ref[...], arrived_ref[...])
+    x = x_ref[...]
+    x = jnp.where(flag_ref[0] == 0, x, received(x, arrived_ref[...], beside_ref[...]))
     loads.wait("pack")
     vec = unpacked(pack_ref, width, local, hidden)
     held["source"][...] = x
@@ -338,7 +345,7 @@
 def b_kernel(micro, *refs):
     flag_ref, dy_hbm, table_hbm, pack_hbm = refs[:4]
     hbm = dict(zip(WEIGHTS, refs[4:8]))
-    names = ("arrived", "x") + NEEDED
+    names = ("arrived", "beside", "x") + NEEDED
     pieces = {n: refs[8 + i * micro : 8 + (i + 1) * micro] for i, n in enumerate(names)}
     refs = refs[-(6 + 4 + 3 + len(names) + 1) :]
     dx_ref, du, dqkv, own, other, dy_out = refs[:6]
@@ -355,6 +362,7 @@
     for m in range(micro):
         loads.start("dy", dy_hbm.at[m], dy_ref.at[pl.ds(m * rows, rows)])
     both("arrived")
+    both("beside")
     both("gp")
     loads.weight("wdown", hbm, w)
     loads.weight("wout", hbm, w)
@@ -372,7 +380,9 @@
 
     loads.wait("dy")
     loads.wait("arrived")
-    dy = jnp.where(flag_ref[0] == 0, saved["arrived"][...], dy_ref[...])
+    loads.wait("beside")
+    dy = dy_ref[...]
+    dy = jnp.where(flag_ref[0] == 0, received(dy, saved["arrived"][...], saved["beside"][...]), dy)
     dy_out[...] = dy
     width, (local, hidden) = dy.shape[1], (dqkv.shape[1] // 3, du.shape[1])
     backward_part(dy, saved, table_ref, w, loads.wait, put)
@@ -412,13 +422,15 @@
 
 def down_kernel(chips, micro, *refs):
     flag_ref, dy_hbm = refs[:2]
-    arrived, active, mixed = (refs[2 + i * micro : 2 + (i + 1) * micro] for i in range(3))
-    theirs, mine, dy_ref, sem = refs[2 + 3 * micro :]
+    arrived, beside, active, mixed = (refs[2 + i * micro : 2 + (i + 1) * micro] for i in range(4))
+    theirs, mine, dy_ref, sem = refs[2 + 4 * micro :]
     copy = pltpu.make_async_copy(dy_hbm, dy_ref, sem)
     copy.start()
     copy.wait()
     core = flag_ref[2]
-    dy = [jnp.where(flag_ref[0] == 0, arrived[m][...], dy_ref[m]) for m in range(micro)]
+    dy = [dy_ref[m] for m in range(micro)]
+    for m in range(micro):
+        dy[m] = jnp.where(flag_ref[0] == 0, received(dy[m], arrived[m][...], beside[m][...]), dy[m])
     dy = jnp.concatenate(dy, axis=0)
     hidden, local = active[0].shape[1], mixed[0].shape[1]
     share, step = hidden // (2 * chips), hidden // chips
@@ -446,6 +458,34 @@
     for z in range(chips):
         theirs[z, at:] = lines
         mine[z, at:] = lines
+
+
+def split_kernel(which, *refs):
+    flag_ref, mine, got = refs[:3]
+    count = len(which)
+    outs, (one, two, extra, sems) = refs[-4 - count : -4], refs[-4:]
+    place = flag_ref[3]
+    loads = Loads(sems)
+    index = (
+        jnp.where(place % 2 == 0, 3, 0),
+        jnp.where(place == 1, 2, 1),
+        jnp.where(place == 0, 2, 1),
+        jnp.where(place == 0, 1, 2),
+        jnp.where(place == 1, 3, 0),
+    )
+    for i, pick in enumerate(which):
+        loads.start(2 * i, mine.at[index[pick]], one.at[i])
+        loads.start(2 * i + 1, got.at[index[pick]], two.at[i])
+        if pick == 4:
+            loads.start("extra", refs[3], extra)
+    for i, pick in enumerate(which):
+        loads.wait(2 * i)
+        loads.wait(2 * i + 1)
+        value = one[i].astype(F32) + two[i].astype(F32)
+        if pick == 4:
+            loads.wait("extra")
+            value = value + extra[...].astype(F32)
+        outs[i][...] = value.astype(BF)
 
 
 def arrived_sum(flag_ref, refs, scratch, sems):
@@ -532,14 +572,6 @@
     out_ref[...] = output_part(mixed, active, vec, w, loads.wait)
 
 
-def add_kernel(at, x_hbm, one_ref, two_ref, out_ref, x_ref, sems):
-    loads = Loads(sems)
-    loads.start("x", x_hbm.at[at], x_ref)
-    loads.wait("x")
-    whole = x_ref[...].astype(F32) + (one_ref[...].astype(F32) + two_ref[...].astype(F32))
-    out_ref[...] = whole.astype(BF)
-
-
 VM = pl.BlockSpec(memory_space=pltpu.VMEM)
 SM = pl.BlockSpec(memory_space=pltpu.SMEM)
 HB = pl.BlockSpec(memory_space=pltpu.HBM)
@@ -556,19 +588,6 @@
 
 def params(mib):
     return pltpu.CompilerParams(vmem_limit_bytes=mib * 2**20)
-
-
-def call_add(at, xs, one, two):
-    rows, width = one.shape
-    return pl.pallas_call(
-        functools.partial(add_kernel, at),
-        out_shape=jax.ShapeDtypeStruct((rows, width), BF),
-        in_specs=[HB, VM, VM],
-        out_specs=VM,
-        scratch_shapes=[pltpu.VMEM((rows, width), BF), pltpu.SemaphoreType.DMA((1,))],
-        compiler_params=params(8),
-        cost_estimate=pl.CostEstimate(flops=rows * width * 2, bytes_accessed=rows * width * 8, transcendentals=0),
-    )(xs, one, two)
 
 
 def call_f(flags, xs, table, ws, vecs):
@@ -595,7 +614,7 @@
 
 
 def call_fb(at, flags, xs, cots, arrived, table, pack, ws):
-    rows, width = arrived.shape
+    rows, width = xs.shape[1:]
     local, hidden = ws[1].shape[0], ws[3].shape[0]
     shape = jax.ShapeDtypeStruct
     outs = [shape((rows, width), BF)] * 4
@@ -609,13 +628,14 @@
     return pl.pallas_call(
         functools.partial(fb_kernel, at),
         out_shape=outs,
-        in_specs=[SM] + [HB] * 9,
+        in_specs=[SM] + [HB] * 10,
         out_specs=[HB] * len(outs),
         scratch_shapes=scratch_like(outs)
         + scratch_like(ws)
         + [
             pltpu.VMEM((rows, hidden), BF),
             pltpu.VMEM((rows, 3 * local), BF),
+            pltpu.VMEM((rows, width), BF),
             pltpu.VMEM((rows, width), BF),
             pltpu.VMEM((rows, width), BF),
             pltpu.VMEM((rows, width), BF),
@@ -626,7 +646,7 @@
         ],
         compiler_params=params(54),
         cost_estimate=cost(ws, rows, 2),
-    )(flags, xs, cots, arrived, table, pack, *ws)
+    )(flags, xs, cots, *arrived, table, pack, *ws)
 
 
 def call_b(flags, cots, table, pack, ws, pieces, after):
@@ -671,6 +691,19 @@
     )(flags, *operands)
 
 
+def call_split(flags, mine, got, which, after):
+    block, count = mine.shape[1:], len(which)
+    return pl.pallas_call(
+        functools.partial(split_kernel, which),
+        out_shape=[jax.ShapeDtypeStruct(block, BF)] * count,
+        in_specs=[SM] + [HB] * (2 + len(after)),
+        out_specs=[VM] * count,
+        scratch_shapes=[pltpu.VMEM((count,) + block, BF)] * 2
+        + [pltpu.VMEM(block, BF), pltpu.SemaphoreType.DMA((8,))],
+        compiler_params=params(16),
+    )(flags, mine, got, *after)
+
+
 def call_final(kernel, flags, parts, outs, after, scratch=()):
     return pl.pallas_call(
         kernel,
@@ -715,8 +748,21 @@
     )(*mixed, *active, pack, ws[1], ws[3], *after)
 
 
+def handed(value, source, target):
+    straight = lax.ppermute(value, "section", [(source, target)])
+    across = [(2 * source, 2 * target + 1), (2 * source + 1, 2 * target)]
+    return straight, lax.ppermute(value, ("section", "tensor"), across)
+
+
 def swap(value):
     return lax.ppermute(value, "tensor", [(0, 1), (1, 0)])
+
+
+ONE = [(0, 1), (1, 0), (2, 3), (3, 2)]
+TWO = [(0, 1), (3, 2)]
+THREE = [(1, 2), (2, 1)]
+FOUR = [(0, 2), (3, 1)]
+FIVE = [(1, 3), (2, 0)]
 
 
 class Line:
@@ -744,16 +790,25 @@
                 jnp.where(place == 0, 1, 2),
             )
         ]
-        self.one = self.send(values[0], [(0, 1), (1, 0), (2, 3), (3, 2)])
-        self.three = self.send(values[1], [(1, 2), (2, 1)])
-        self.four = self.send(values[2], [(0, 2), (3, 1)])
-        self.two = self.send(values[3], [(0, 1), (3, 2)])
+        self.one = self.send(values[0], ONE)
+        self.three = self.send(values[1], THREE)
+        self.four = self.send(values[2], FOUR)
+        self.two = self.send(values[3], TWO)
         return tuple(values)
 
     def relay(self):
         value = (self.block(jnp.where(self.place == 1, 3, 0)) + self.one.astype(F32)).astype(BF)
-        self.five = self.send(value, [(1, 3), (2, 0)])
+        self.five = self.send(value, FIVE)
         return value
+
+    def staged(self, flags):
+        first = call_split(flags, self.mine, self.got, (0, 1), ())
+        self.one = self.send(first[0], ONE)
+        self.three = self.send(first[1], THREE)
+        rest = call_split(flags, self.mine, self.got, (4, 2, 3), (self.one, self.three))
+        self.five = self.send(rest[0], FIVE)
+        self.four = self.send(rest[1], FOUR)
+        self.two = self.send(rest[2], TWO)
 
     def parts(self):
         return self.mine, self.got, self.one, self.two, self.three, self.four, self.five
@@ -789,31 +844,30 @@
     *outs, pack = call_f(flags, xs, table, ws, vecs)
     arrivals = []
     for m in range(micro):
-        whole = call_add(m, xs, outs[m], swap(outs[m]))
-        arrivals.append(lax.ppermute(whole, "section", [(0, 1)]))
+        arrivals.append(handed(outs[m], 0, 1))
     kept, sources, backs = [], [], []
     for m in range(micro):
         dx, source, *saved = call_fb(m, flags, xs, cots, arrivals[m], table, pack, ws)
-        whole = call_add(m, cots, dx, swap(dx))
-        backs.append(lax.ppermute(whole, "section", [(1, 0)]))
+        backs.append(handed(dx, 1, 0))
         kept.append(dict(zip(SAVED, saved)))
         sources.append(source)
     a1, a2, mixed, active = ([kept[m][n] for m in range(micro)] for n in ("a1", "a2", "mixed", "g"))
 
     after = ()
+    arrived, beside = ([back[i] for back in backs] for i in range(2))
     if lined:
         theirs, mine = call_blocks(
             functools.partial(down_kernel, chips, micro),
             flags,
-            (cots, *backs, *active, *mixed),
-            [HB] + [VM] * (3 * micro),
+            (cots, *arrived, *beside, *active, *mixed),
+            [HB] + [VM] * (4 * micro),
             (chips, hidden // parts + local // parts, width),
             2 * micro * rows * width * (hidden + local),
             [pltpu.VMEM(cots.shape, BF), pltpu.SemaphoreType.DMA],
         )
         line_down = Line(theirs, mine, dp_at)
         after = line_down.start()
-    pieces = [backs, sources] + [[kept[m][n] for m in range(micro)] for n in NEEDED]
+    pieces = [arrived, beside, sources] + [[kept[m][n] for m in range(micro)] for n in NEEDED]
     grad, du, dqkv, own, other, up = call_b(flags, cots, table, pack, ws, pieces, after)
     got = swap(other)
     share = width // parts
@@ -831,8 +885,7 @@
         )
         line_rest = Line(theirs, mine, dp_at)
         part = call_o(mixed, active, pack, ws, (mine,))
-        line_rest.start()
-        line_rest.relay()
+        line_rest.staged(flags)
         after = (line_rest.one,)
         down_rows = hidden // parts
         outs = [(down_rows, width), (local // parts, width)]

time: 172 us -> 169 us (0.983)
  other arithmetic: 9.26 us -> 4.08 us
  waiting for transfers between devices: 54.9 us -> 49.9 us
  starting transfers between devices: 38.4 us -> 43.2 us
  Pallas kernels: 60.5 us -> 63.4 us
    ppermute x7 -> x3, waiting for transfers between devices: 19.9 us -> 9.73 us  [swap(): return lax.ppermute(value, 'tensor', [(0, 1), (1, 0)])]
    ppermute x4 -> x8, waiting for transfers between devices: 7.22 us -> 14.2 us  [the longest x4 7.91 us: handed(): straight = lax.ppermute(value, 'section', [(source, target)])]
    ppermute x4 -> x8, starting transfers between devices: 8.51 us -> 15.1 us  [the longest x4 8.74 us: handed(): straight = lax.ppermute(value, 'section', [(source, target)])]
    ppermute x7 -> x3, starting transfers between devices: 6.89 us -> 3.71 us  [swap(): return lax.ppermute(value, 'tensor', [(0, 1), (1, 0)])]
    convert_element_type x2 -> x1, other arithmetic: 5.73 us -> 2.59 us  [start(): self.block(index).astype(BF)]
    pallas_call x4 -> x2, Pallas kernels: 1.24 us -> 3.57 us  [call_split(): pl.pallas_call(functools.partial(split_kernel, which), out_shape=[jax.Sha...]
    convert_element_type x2 -> x1, other arithmetic: 2.94 us -> 0.9 us  [relay(): (self.block(jnp.where(self.place == 1, 3, 0)) + self.one.astype(F32)).ast...]
    ppermute x10, waiting for transfers between devices: 19.9 us -> 18.1 us  [send(): lax.ppermute(value, 'dp', [(2 * a + c, 2 * b + c) for a, b in pairs for c...]
  transfers between devices with their start and end apart: 23 -> 23, of which waited for: 12 -> 12; matrix products, arithmetic and copies ran while one was open for 2% -> 1% of each run, Pallas kernels for 23% -> 25%
where the time goes in v3:
time: 169 us; the launch traced here: 168 us
  Pallas kernels  63.4 us (38%)
  waiting for transfers between devices  49.9 us (30%)
  starting transfers between devices  43.2 us (26%)
  local copies, waits for them, and re-layouts  6.69 us (4%)
  other arithmetic  4.08 us (2%)
    ppermute x10, starting transfers between devices, send(): lax.ppermute(value, 'dp', [(2 * a + c, 2 * b + c) for a, b in pairs for c...  24.3 us
    pallas_call x2, Pallas kernels, call_fb(): pl.pallas_call(functools.partial(fb_kernel, at), out_shape=outs, in_specs...  20.2 us
    ppermute x10, waiting for transfers between devices, send(): lax.ppermute(value, 'dp', [(2 * a + c, 2 * b + c) for a, b in pairs for c...  18.1 us
    pallas_call x1, Pallas kernels, call_b(): pl.pallas_call(functools.partial(b_kernel, micro), out_shape=outs, in_spe...  10.4 us
    pallas_call x2, Pallas kernels, call_blocks(): pl.pallas_call(kernel, out_shape=outs, in_specs=[SM] + specs, out_specs=[...  10.3 us
    ppermute x3, waiting for transfers between devices, swap(): return lax.ppermute(value, 'tensor', [(0, 1), (1, 0)])  9.73 us
    ppermute x4, starting transfers between devices, handed(): straight = lax.ppermute(value, 'section', [(source, target)])  8.74 us
    pallas_call x1, Pallas kernels, call_f(): pl.pallas_call(functools.partial(f_kernel, micro), out_shape=out, in_spec...  8.34 us
  transfers between devices with their start and end apart: 23, of which 12 were waited for; matrix products, arithmetic and copies ran while one was open for 1% of the time, Pallas kernels for 25%

profile of v3, /device:TPU:0, one launch (start us, length us, event | category | flops | bytes accessed | tf_op | source)
XLA Modules:
  0.0 168.3 jit_solution(7446016625939926460)
XLA Ops:
  0.7 0.6 pad_add_fusion.refs_0_.flag_ref
  1.3 8.3 %shard_map.254 = (bf16[128,768]{1,0:T(8,128)(2,1)}, bf16[128,768]{1,0:T(8,128)(2,1)}, f32[16,1536]{1,0:T(8,128)}) custom-call(s32[4]{0:T(128)} %pad_add_fusion.refs_0_.flag_ref, bf16[2,128,768]{2,1,0:T(8,128)(2,1)} %bitcast.57, f32[3,128,128]{2,1,0:T(8,128)} %constant.76.clone.refs_2_.refs_5_, bf16[3,768,384]{2,1,0:T(8,128)(2,1)} %bitcast.48, ...), custom_call_target="tpu_custom_call" | custom-call | flops 1811939328 | bytes 7077888 | tf_op jit(solution)/shard_map/pallas_call | solution.py:605
  9.6 4.9 %collective-permute-start.2 = (bf16[128,768]{1,0:T(8,128)(2,1)}, bf16[128,768]{1,0:T(8,128)(2,1)S(1)}, u32[]{:S(2)}, u32[]{:S(2)}) collective-permute-start(bf16[128,768]{1,0:T(8,128)(2,1)} %get-tuple-element.66), channel_id=1, source_target_pairs={{0,16},{1,17},{2,18},{3,19},{4,20},{5,21},{6,22},{7,23},{8,24},{9,... | collective-permute-start | bytes 589832 | tf_op jit(solution)/shard_map/ppermute | solution.py:752
  14.5 2.2 %collective-permute-start.3 = (bf16[128,768]{1,0:T(8,128)(2,1)}, bf16[128,768]{1,0:T(8,128)(2,1)S(1)}, u32[]{:S(2)}, u32[]{:S(2)}) collective-permute-start(bf16[128,768]{1,0:T(8,128)(2,1)} %get-tuple-element.66), channel_id=1, source_target_pairs={{0,24},{8,16},{1,25},{9,17},{2,26},{10,18},{3,27},{11,19},{4,28},{... | collective-permute-start | bytes 589832 | tf_op jit(solution)/shard_map/ppermute | solution.py:754
  16.7 1.3 collective-permute-start
  18.0 1.3 collective-permute-start.1
  19.3 0.7 collective-permute-done.2.refs_3_
  20.1 4.2 %collective-permute-done.3.refs_4_ = bf16[128,768]{1,0:T(8,128)(2,1)S(1)} collective-permute-done((bf16[128,768]{1,0:T(8,128)(2,1)}, bf16[128,768]{1,0:T(8,128)(2,1)S(1)}, u32[]{:S(2)}, u32[]{:S(2)}) %collective-permute-start.3) | collective-permute-done | bytes 196640 | tf_op jit(solution)/shard_map/ppermute | solution.py:754
  24.3 0.7 copy-done.23
  24.9 10.1 %shard_map.256 = (bf16[128,768]{1,0:T(8,128)(2,1)}, bf16[128,768]{1,0:T(8,128)(2,1)}, bf16[128,768]{1,0:T(8,128)(2,1)}, bf16[128,768]{1,0:T(8,128)(2,1)}, bf16[1...) custom-call(s32[4]{0:T(128)} %pad_add_fusion.refs_0_.flag_ref, ...), custom_call_target="tpu_custom_call" | custom-call | flops 1811939328 | bytes 7077888 | tf_op jit(solution)/shard_map/pallas_call | solution.py:628
  35.0 1.3 collective-permute-start.5
  36.3 1.5 collective-permute-start.7
  37.8 0.0 collective-permute-done.refs_3_
  37.8 0.0 copy-start.20
  37.8 0.0 collective-permute-done.1.refs_4_
  37.9 0.7 copy-done.20
  38.5 0.7 copy-done.21
  39.2 10.1 %shard_map.255 = (bf16[128,768]{1,0:T(8,128)(2,1)}, bf16[128,768]{1,0:T(8,128)(2,1)}, bf16[128,768]{1,0:T(8,128)(2,1)}, bf16[128,768]{1,0:T(8,128)(2,1)}, bf16[1...) custom-call(s32[4]{0:T(128)} %pad_add_fusion.refs_0_.flag_ref, ...), custom_call_target="tpu_custom_call" | custom-call | flops 1811939328 | bytes 7077888 | tf_op jit(solution)/shard_map/pallas_call | solution.py:628
  49.3 1.3 collective-permute-start.4
  50.6 1.3 collective-permute-start.6
  51.9 0.0 collective-permute-done.5.refs_3_.refs_9_
  51.9 0.0 collective-permute-done.7.refs_5_.refs_11_
  51.9 7.2 %collective-permute-done.4.refs_2_.refs_8_ = bf16[128,768]{1,0:T(8,128)(2,1)S(1)} collective-permute-done((bf16[128,768]{1,0:T(8,128)(2,1)}, bf16[128,768]{1,0:T(8,128)(2,1)S(1)}, u32[]{:S(2)}, u32[]{:S(2)}) %collective-permute-start.4) | collective-permute-done | bytes 196640 | tf_op jit(solution)/shard_map/ppermute | solution.py:752
  59.1 2.1 %collective-permute-done.6.refs_4_.refs_10_ = bf16[128,768]{1,0:T(8,128)(2,1)S(1)} collective-permute-done((bf16[128,768]{1,0:T(8,128)(2,1)}, bf16[128,768]{1,0:T(8,128)(2,1)S(1)}, u32[]{:S(2)}, u32[]{:S(2)}) %collective-permute-start.6) | collective-permute-done | bytes 196640 | tf_op jit(solution)/shard_map/ppermute | solution.py:754
  61.2 0.7 copy-done.19
  61.9 5.1 %shard_map.257 = (bf16[4,240,768]{2,1,0:T(8,128)(2,1)}, bf16[4,240,768]{2,1,0:T(8,128)(2,1)}) custom-call(s32[4]{0:T(128)} %pad_add_fusion.refs_0_.flag_ref, bf16[2,128,768]{2,1,0:T(8,128)(2,1)} %bitcast.62, bf16[128,768]{1,0:T(8,128)(2,1)} %copy-done.18, bf16[128,768]{1,0:T(8,128)(2,1)} %copy-done.16, bf16[128,768]{1,0:T(8,128)(2,1)} %copy-done.19, ...), custom_call_target="tpu_custom_call" | custom-call | flops 754974720 | bytes 2949120 | tf_op jit(solution)/shard_map/pallas_call | solution.py:683
  67.0 0.1 collective-permute-start.8
  67.1 3.4 %collective-permute-done.8.refs_1_ = bf16[4,240,768]{2,1,0:T(8,128)(2,1)S(1)} collective-permute-done((bf16[4,240,768]{2,1,0:T(8,128)(2,1)}, bf16[4,240,768]{2,1,0:T(8,128)(2,1)S(1)}, u32[]{:S(2)}, u32[]{:S(2)}) %collective-permute-start.8) | collective-permute-done | bytes 1474592 | tf_op jit(solution)/shard_map/ppermute | solution.py:772
  70.6 2.6 %fusion.4 = (bf16[240,768]{1,0:T(8,128)(2,1)}, bf16[240,768]{1,0:T(8,128)(2,1)S(1)}, bf16[240,768]{1,0:T(8,128)(2,1)}, bf16[240,768]{1,0:T(8,128)(2,1)}) fusion(bf16[4,240,768]{2,1,0:T(8,128)(2,1)S(1)} %collective-permute-done.8.refs_1_, s32[]{:T(128)S(6)} %select_n.49, bf16[4,240,768]{2,1,0:T(8,128)(2,1)} %get-tuple-element.84.refs_0_, s32[]{:T(128)S(6)} %select_n.48, ...), kind=kLoop, calls=%fused_computation.9 | loop fusion | flops 2949120 | bytes 4423696 | tf_op jit(solution)/shard_map/convert_element_type | solution.py:785
  73.2 1.6 collective-permute-start.10
  74.7 2.4 %collective-permute-start.11 = (bf16[240,768]{1,0:T(8,128)(2,1)}, bf16[240,768]{1,0:T(8,128)(2,1)S(1)}, u32[]{:S(2)}, u32[]{:S(2)}) collective-permute-start(bf16[240,768]{1,0:T(8,128)(2,1)} %get-tuple-element.126.refs_27_), channel_id=1, source_target_pairs={{0,2},{1,3},{6,4},{7,5},{8,10},{9,11},{14,12},{15,13},{16,18},{17,... | collective-permute-start | bytes 1105928 | tf_op jit(solution)/shard_map/ppermute | solution.py:780
  77.1 0.7 collective-permute-start.12
  77.8 4.9 %collective-permute-start.13 = (bf16[240,768]{1,0:T(8,128)(2,1)S(1)}, bf16[240,768]{1,0:T(8,128)(2,1)S(1)}, u32[]{:S(2)}, u32[]{:S(2)}) collective-permute-start(bf16[240,768]{1,0:T(8,128)(2,1)S(1)} %get-tuple-element.127.refs_26_), channel_id=1, source_target_pairs={{0,4},{1,5},{6,2},{7,3},{8,12},{9,13},{14,10},{15,11},{16,20},{17,... | collective-permute-start | bytes 1105928 | tf_op jit(solution)/shard_map/ppermute | solution.py:780
  82.7 10.4 %shard_map.258 = (bf16[256,768]{1,0:T(8,128)(2,1)}, bf16[256,1536]{1,0:T(8,128)(2,1)}, bf16[256,1152]{1,0:T(8,128)(2,1)}, f32[16,384]{1,0:T(8,128)}, f32[8,384]{1,0:T(8,128)}, /*index=5*/bf16[256,768]{1,0:T(8,128)(2,1)}) custom-call(s32[4]{0:T(128)} %pad_add_fusion.refs_0_.flag_ref, bf16[2,128,768]{2,1,0:T(8,128)(2,1)} %bitcast.63, ...), custom_call_target="tpu_custom_call" | custom-call | flops 1811939328 | bytes 7077888 | tf_op jit(solution)/shard_map/pallas_call | solution.py:666
  93.1 1.6 collective-permute-start.9
  94.7 0.9 fusion.refs_9_
  95.6 1.5 collective-permute-done.9.refs_4_
  97.1 1.7 %collective-permute-done.13.refs_12_.refs_5_ = bf16[240,768]{1,0:T(8,128)(2,1)S(1)} collective-permute-done((bf16[240,768]{1,0:T(8,128)(2,1)S(1)}, bf16[240,768]{1,0:T(8,128)(2,1)S(1)}, u32[]{:S(2)}, u32[]{:S(2)}) %collective-permute-start.13) | collective-permute-done | bytes 368672 | tf_op jit(solution)/shard_map/ppermute | solution.py:780
  98.9 0.7 copy-done.12
  99.6 5.2 %shard_map.259 = (bf16[4,688,384]{2,1,0:T(8,128)(2,1)}, bf16[4,688,384]{2,1,0:T(8,128)(2,1)}) custom-call(s32[4]{0:T(128)} %pad_add_fusion.refs_0_.flag_ref, bf16[256,1536]{1,0:T(8,128)(2,1)} %get-tuple-element.86.refs_1_, bf16[256,1152]{1,0:T(8,128)(2,1)} %get-tuple-element.87.refs_2_, f32[16,384]{1,0:T(8,128)} %get-tuple-element.88.refs_3_, ...), custom_call_target="tpu_custom_call" | custom-call | flops 1056964608 | bytes 4227072 | tf_op jit(solution)/shard_map/pallas_call | solution.py:683
  104.8 4.4 %collective-permute-done.16.refs_2_.refs_1_ = bf16[4,688,384]{2,1,0:T(8,128)(2,1)S(1)} collective-permute-done((bf16[4,688,384]{2,1,0:T(8,128)(2,1)}, bf16[4,688,384]{2,1,0:T(8,128)(2,1)S(1)}, u32[]{:S(2)}, u32[]{:S(2)}) %collective-permute-start.16) | collective-permute-done | bytes 2113568 | tf_op jit(solution)/shard_map/ppermute | solution.py:772
  109.2 1.6 copy-done
  110.8 1.0 shard_map.261
  111.9 3.6 %collective-permute-start.17 = (bf16[688,384]{1,0:T(8,128)(2,1)S(1)}, bf16[688,384]{1,0:T(8,128)(2,1)S(1)}, u32[]{:S(2)}, u32[]{:S(2)}) collective-permute-start(bf16[688,384]{1,0:T(8,128)(2,1)S(1)} %get-tuple-element.98), channel_id=1, source_target_pairs={{0,2},{1,3},{2,0},{3,1},{4,6},{5,7},{6,4},{7,5},{8,10},{9,11},{10,... | collective-permute-start | bytes 1585160 | tf_op jit(solution)/shard_map/ppermute | solution.py:780
  115.5 0.8 collective-permute-start.18
  116.3 1.3 collective-permute-start.22
  117.6 10.2 %collective-permute-done.17.refs_7_.refs_3_.refs_2_ = bf16[688,384]{1,0:T(8,128)(2,1)S(1)} collective-permute-done((bf16[688,384]{1,0:T(8,128)(2,1)S(1)}, bf16[688,384]{1,0:T(8,128)(2,1)S(1)}, u32[]{:S(2)}, u32[]{:S(2)}) %collective-permute-start.17) | collective-permute-done | bytes 528416 | tf_op jit(solution)/shard_map/ppermute | solution.py:780
  127.8 2.5 %shard_map.263 = (bf16[688,384]{1,0:T(8,128)(2,1)}, bf16[688,384]{1,0:T(8,128)(2,1)}, bf16[688,384]{1,0:T(8,128)(2,1)}) custom-call(s32[4]{0:T(128)S(1)} %copy-done.14, bf16[4,688,384]{2,1,0:T(8,128)(2,1)S(1)} %copy-done, bf16[4,688,384]{2,1,0:T(8,128)(2,1)S(1)} %collective-permute-done.16.refs_2_.refs_1_, ...), custom_call_target="tpu_custom_call" | custom-call | tf_op jit(solution)/shard_map/pallas_call | solution.py:696
  130.3 6.5 %collective-permute-start.19 = (bf16[688,384]{1,0:T(8,128)(2,1)}, bf16[688,384]{1,0:T(8,128)(2,1)S(1)}, u32[]{:S(2)}, u32[]{:S(2)}) collective-permute-start(bf16[688,384]{1,0:T(8,128)(2,1)} %get-tuple-element.102), channel_id=1, source_target_pairs={{0,2},{1,3},{6,4},{7,5},{8,10},{9,11},{14,12},{15,13},{16,18},{17,... | collective-permute-start | bytes 1585160 | tf_op jit(solution)/shard_map/ppermute | solution.py:780
  136.8 1.3 collective-permute-start.20
  138.2 1.3 collective-permute-start.21
  139.5 1.6 collective-permute-start.15
  141.1 4.8 %shard_map.260.refs_0_ = bf16[256,768]{1,0:T(8,128)(2,1)} custom-call(bf16[128,384]{1,0:T(8,128)(2,1)} %get-tuple-element.65.refs_8_.refs_0_, bf16[128,384]{1,0:T(8,128)(2,1)} %get-tuple-element.67.refs_9_.refs_1_, bf16[128,1536]{1,0:T(8,128)(2,1)} %get-tuple-element.68.refs_6_.refs_2_, bf16[128,1536]{1,0:T(8,128)(2,1)} %get-tuple-element.69.refs_7_.refs_3_, ...), custom_call_target="tpu_custom_call" | custom-call | flops 754974720 | bytes 2949120 | tf_op jit(solution)/shard_map/pallas_call | solution.py:734
  145.9 0.0 copy-start.3
  145.9 0.6 collective-permute-start.14
  146.6 2.5 %shard_map.265 = (f32[192,768]{1,0:T(8,128)}, f32[48,768]{1,0:T(8,128)}) custom-call(s32[4]{0:T(128)S(1)} %copy-done.14, bf16[4,240,768]{2,1,0:T(8,128)(2,1)S(1)} %copy-done.2, bf16[4,240,768]{2,1,0:T(8,128)(2,1)S(1)} %collective-permute-done.8.refs_1_, bf16[240,768]{1,0:T(8,128)(2,1)S(1)} %collective-permute-done.10.refs_2_, ...), custom_call_target="tpu_custom_call" | custom-call | tf_op jit(solution)/shard_map/pallas_call | solution.py:708
  149.0 1.8 %collective-permute-done.15.refs_4_ = bf16[256,768]{1,0:T(8,128)(2,1)S(1)} collective-permute-done((bf16[256,768]{1,0:T(8,128)(2,1)S(1)}, bf16[256,768]{1,0:T(8,128)(2,1)S(1)}, u32[]{:S(2)}, u32[]{:S(2)}) %collective-permute-start.15) | collective-permute-done | bytes 393248 | tf_op jit(solution)/shard_map/ppermute | solution.py:758
  150.8 6.4 %collective-permute-done.14.refs_1_ = bf16[256,768]{1,0:T(8,128)(2,1)S(1)} collective-permute-done((bf16[256,768]{1,0:T(8,128)(2,1)}, bf16[256,768]{1,0:T(8,128)(2,1)S(1)}, u32[]{:S(2)}, u32[]{:S(2)}) %collective-permute-start.14) | collective-permute-done | bytes 393248 | tf_op jit(solution)/shard_map/ppermute | solution.py:758
  157.3 1.2 shard_map.262
  158.5 6.2 %collective-permute-done.21.refs_6_ = bf16[688,384]{1,0:T(8,128)(2,1)S(1)} collective-permute-done((bf16[688,384]{1,0:T(8,128)(2,1)}, bf16[688,384]{1,0:T(8,128)(2,1)S(1)}, u32[]{:S(2)}, u32[]{:S(2)}) %collective-permute-start.21) | collective-permute-done | bytes 528416 | tf_op jit(solution)/shard_map/ppermute | solution.py:780
  164.6 2.0 %shard_map.264 = (f32[96,1536]{1,0:T(8,128)}, f32[3,96,384]{2,1,0:T(8,128)}, f32[5,48]{1,0:T(8,128)S(1)}, f32[3,48]{1,0:T(4,128)S(1)}, f32[1,192]{1,0:T(1,128)}) custom-call(s32[4]{0:T(128)S(1)} %copy-done.14, bf16[4,688,384]{2,1,0:T(8,128)(2,1)S(1)} %copy-done.1, bf16[4,688,384]{2,1,0:T(8,128)(2,1)S(1)} %collective-permute-done.16.refs_2_.refs_1_, ...), custom_call_target="tpu_custom_call" | custom-call | tf_op jit(solution)/shard_map/pallas_call | solution.py:708
  166.7 0.5 fusion.5
  167.2 0.6 copy.31
  167.8 0.5 copy.33
  (52 shorter events, 0.1 us)
Async XLA Ops:
  9.6 10.5 %collective-permute-start.2 = (bf16[128,768]{1,0:T(8,128)(2,1)}, bf16[128,768]{1,0:T(8,128)(2,1)S(1)}, u32[]{:S(2)}, u32[]{:S(2)}) collective-permute-start(bf16[128,768]{1,0:T(8,128)(2,1)} %get-tuple-element.66), channel_id=1, source_target_pairs={{0,16},{1,17},{2,18},{3,19},{4,20},{5,21},{6,22},{7,23},{8,24},{9,... | collective-permute-start | bytes 589832 | tf_op jit(solution)/shard_map/ppermute | solution.py:752
  14.5 9.8 %collective-permute-start.3 = (bf16[128,768]{1,0:T(8,128)(2,1)}, bf16[128,768]{1,0:T(8,128)(2,1)S(1)}, u32[]{:S(2)}, u32[]{:S(2)}) collective-permute-start(bf16[128,768]{1,0:T(8,128)(2,1)} %get-tuple-element.66), channel_id=1, source_target_pairs={{0,24},{8,16},{1,25},{9,17},{2,26},{10,18},{3,27},{11,19},{4,28},{... | collective-permute-start | bytes 589832 | tf_op jit(solution)/shard_map/ppermute | solution.py:754
  16.7 21.1 %collective-permute-start = (bf16[128,768]{1,0:T(8,128)(2,1)}, bf16[128,768]{1,0:T(8,128)(2,1)S(1)}, u32[]{:S(2)}, u32[]{:S(2)}) collective-permute-start(bf16[128,768]{1,0:T(8,128)(2,1)} %get-tuple-element.63), channel_id=1, source_target_pairs={{0,16},{1,17},{2,18},{3,19},{4,20},{5,21},{6,22},{7,23},{8,24},{9,... | collective-permute-start | bytes 589832 | tf_op jit(solution)/shard_map/ppermute | solution.py:752
  18.0 19.8 %collective-permute-start.1 = (bf16[128,768]{1,0:T(8,128)(2,1)}, bf16[128,768]{1,0:T(8,128)(2,1)S(1)}, u32[]{:S(2)}, u32[]{:S(2)}) collective-permute-start(bf16[128,768]{1,0:T(8,128)(2,1)} %get-tuple-element.63), channel_id=1, source_target_pairs={{0,24},{8,16},{1,25},{9,17},{2,26},{10,18},{3,27},{11,19},{4,28},{... | collective-permute-start | bytes 589832 | tf_op jit(solution)/shard_map/ppermute | solution.py:754
  20.1 4.2 %copy-start.22 = (bf16[128,768]{1,0:T(8,128)(2,1)}, bf16[128,768]{1,0:T(8,128)(2,1)S(1)}, u32[]{:S(2)}) copy-start(bf16[128,768]{1,0:T(8,128)(2,1)S(1)} %collective-permute-done.2.refs_3_) | copy-start | bytes 589828
  24.3 0.7 copy-start.23
  35.0 16.9 %collective-permute-start.5 = (bf16[128,768]{1,0:T(8,128)(2,1)}, bf16[128,768]{1,0:T(8,128)(2,1)S(1)}, u32[]{:S(2)}, u32[]{:S(2)}) collective-permute-start(bf16[128,768]{1,0:T(8,128)(2,1)} %get-tuple-element.71), channel_id=1, source_target_pairs={{16,0},{17,1},{18,2},{19,3},{20,4},{21,5},{22,6},{23,7},{24,8},{25... | collective-permute-start | bytes 589832 | tf_op jit(solution)/shard_map/ppermute | solution.py:752
  36.3 15.6 %collective-permute-start.7 = (bf16[128,768]{1,0:T(8,128)(2,1)}, bf16[128,768]{1,0:T(8,128)(2,1)S(1)}, u32[]{:S(2)}, u32[]{:S(2)}) collective-permute-start(bf16[128,768]{1,0:T(8,128)(2,1)} %get-tuple-element.71), channel_id=1, source_target_pairs={{16,8},{24,0},{17,9},{25,1},{18,10},{26,2},{19,11},{27,3},{20,12},... | collective-permute-start | bytes 589832 | tf_op jit(solution)/shard_map/ppermute | solution.py:754
  37.8 0.7 copy-start.20
  38.5 0.7 copy-start.21
  49.3 9.8 %collective-permute-start.4 = (bf16[128,768]{1,0:T(8,128)(2,1)}, bf16[128,768]{1,0:T(8,128)(2,1)S(1)}, u32[]{:S(2)}, u32[]{:S(2)}) collective-permute-start(bf16[128,768]{1,0:T(8,128)(2,1)} %get-tuple-element.70), channel_id=1, source_target_pairs={{16,0},{17,1},{18,2},{19,3},{20,4},{21,5},{22,6},{23,7},{24,8},{25... | collective-permute-start | bytes 589832 | tf_op jit(solution)/shard_map/ppermute | solution.py:752
  50.6 10.6 %collective-permute-start.6 = (bf16[128,768]{1,0:T(8,128)(2,1)}, bf16[128,768]{1,0:T(8,128)(2,1)S(1)}, u32[]{:S(2)}, u32[]{:S(2)}) collective-permute-start(bf16[128,768]{1,0:T(8,128)(2,1)} %get-tuple-element.70), channel_id=1, source_target_pairs={{16,8},{24,0},{17,9},{25,1},{18,10},{26,2},{19,11},{27,3},{20,12},... | collective-permute-start | bytes 589832 | tf_op jit(solution)/shard_map/ppermute | solution.py:754
  51.9 9.3 %copy-start.16 = (bf16[128,768]{1,0:T(8,128)(2,1)}, bf16[128,768]{1,0:T(8,128)(2,1)S(1)}, u32[]{:S(2)}) copy-start(bf16[128,768]{1,0:T(8,128)(2,1)S(1)} %collective-permute-done.5.refs_3_.refs_9_) | copy-start | bytes 589828
  51.9 9.3 %copy-start.17 = (bf16[128,768]{1,0:T(8,128)(2,1)}, bf16[128,768]{1,0:T(8,128)(2,1)S(1)}, u32[]{:S(2)}) copy-start(bf16[128,768]{1,0:T(8,128)(2,1)S(1)} %collective-permute-done.7.refs_5_.refs_11_) | copy-start | bytes 589828
  59.1 2.1 %copy-start.18 = (bf16[128,768]{1,0:T(8,128)(2,1)}, bf16[128,768]{1,0:T(8,128)(2,1)S(1)}, u32[]{:S(2)}) copy-start(bf16[128,768]{1,0:T(8,128)(2,1)S(1)} %collective-permute-done.4.refs_2_.refs_8_) | copy-start | bytes 589828
  61.2 0.7 copy-start.19
  67.0 3.5 %collective-permute-start.8 = (bf16[4,240,768]{2,1,0:T(8,128)(2,1)}, bf16[4,240,768]{2,1,0:T(8,128)(2,1)S(1)}, u32[]{:S(2)}, u32[]{:S(2)}) collective-permute-start(bf16[4,240,768]{2,1,0:T(8,128)(2,1)} %get-tuple-element.85), channel_id=1, source_target_pairs={{0,1},{1,0},{2,3},{3,2},{4,5},{5,4},{6,7},{7,6},{8,9},{9,8},{10,11... | collective-permute-start | bytes 4423688 | tf_op jit(solution)/shard_map/ppermute | solution.py:772
  73.2 9.5 %copy-start.15 = (bf16[240,768]{1,0:T(8,128)(2,1)}, bf16[240,768]{1,0:T(8,128)(2,1)S(1)}, u32[]{:S(2)}) copy-start(bf16[240,768]{1,0:T(8,128)(2,1)S(1)} %get-tuple-element.127.refs_26_) | copy-start | bytes 1105924
  73.2 21.5 %collective-permute-start.10 = (bf16[240,768]{1,0:T(8,128)(2,1)}, bf16[240,768]{1,0:T(8,128)(2,1)S(1)}, u32[]{:S(2)}, u32[]{:S(2)}) collective-permute-start(bf16[240,768]{1,0:T(8,128)(2,1)} %get-tuple-element.129.refs_24_), channel_id=1, source_target_pairs={{0,2},{1,3},{2,0},{3,1},{4,6},{5,7},{6,4},{7,5},{8,10},{9,11},{10,... | collective-permute-start | bytes 1105928 | tf_op jit(solution)/shard_map/ppermute | solution.py:780
  74.7 22.4 %collective-permute-start.11 = (bf16[240,768]{1,0:T(8,128)(2,1)}, bf16[240,768]{1,0:T(8,128)(2,1)S(1)}, u32[]{:S(2)}, u32[]{:S(2)}) collective-permute-start(bf16[240,768]{1,0:T(8,128)(2,1)} %get-tuple-element.126.refs_27_), channel_id=1, source_target_pairs={{0,2},{1,3},{6,4},{7,5},{8,10},{9,11},{14,12},{15,13},{16,18},{17,... | collective-permute-start | bytes 1105928 | tf_op jit(solution)/shard_map/ppermute | solution.py:780
  77.1 20.0 %collective-permute-start.12 = (bf16[240,768]{1,0:T(8,128)(2,1)}, bf16[240,768]{1,0:T(8,128)(2,1)S(1)}, u32[]{:S(2)}, u32[]{:S(2)}) collective-permute-start(bf16[240,768]{1,0:T(8,128)(2,1)} %get-tuple-element.128.refs_25_), channel_id=1, source_target_pairs={{2,4},{3,5},{4,2},{5,3},{10,12},{11,13},{12,10},{13,11},{18,20},{1... | collective-permute-start | bytes 1105928 | tf_op jit(solution)/shard_map/ppermute | solution.py:780
  77.8 21.1 %collective-permute-start.13 = (bf16[240,768]{1,0:T(8,128)(2,1)S(1)}, bf16[240,768]{1,0:T(8,128)(2,1)S(1)}, u32[]{:S(2)}, u32[]{:S(2)}) collective-permute-start(bf16[240,768]{1,0:T(8,128)(2,1)S(1)} %get-tuple-element.127.refs_26_), channel_id=1, source_target_pairs={{0,4},{1,5},{6,2},{7,3},{8,12},{9,13},{14,10},{15,11},{16,20},{17,... | collective-permute-start | bytes 1105928 | tf_op jit(solution)/shard_map/ppermute | solution.py:780
  82.7 12.0 %copy-start.2 = (bf16[4,240,768]{2,1,0:T(8,128)(2,1)S(1)}, bf16[4,240,768]{2,1,0:T(8,128)(2,1)}, u32[]{:S(2)}) copy-start(bf16[4,240,768]{2,1,0:T(8,128)(2,1)} %get-tuple-element.84.refs_0_) | copy-start | bytes 4423684
  93.1 4.0 %collective-permute-start.9 = (f32[8,384]{1,0:T(8,128)}, f32[8,384]{1,0:T(8,128)S(1)}, u32[]{:S(2)}, u32[]{:S(2)}) collective-permute-start(f32[8,384]{1,0:T(8,128)} %get-tuple-element.89), channel_id=1, source_target_pairs={{0,8},{8,0},{1,9},{9,1},{2,10},{10,2},{3,11},{11,3},{4,12},{12,4},... | collective-permute-start | bytes 36872 | tf_op jit(solution)/shard_map/ppermute | solution.py:758
  97.1 1.8 %copy-start.25 = (f32[8,384]{1,0:T(8,128)}, f32[8,384]{1,0:T(8,128)S(1)}, u32[]{:S(2)}) copy-start(f32[8,384]{1,0:T(8,128)S(1)} %collective-permute-done.9.refs_4_) | copy-start | bytes 36868
  97.1 1.8 %copy-start.8 = (bf16[240,768]{1,0:T(8,128)(2,1)}, bf16[240,768]{1,0:T(8,128)(2,1)S(1)}, u32[]{:S(2)}) copy-start(bf16[240,768]{1,0:T(8,128)(2,1)S(1)} %collective-permute-done.11.refs_10_.refs_3_) | copy-start | bytes 1105924
  97.1 1.8 %copy-start.10 = (bf16[240,768]{1,0:T(8,128)(2,1)}, bf16[240,768]{1,0:T(8,128)(2,1)S(1)}, u32[]{:S(2)}) copy-start(bf16[240,768]{1,0:T(8,128)(2,1)S(1)} %collective-permute-done.12.refs_11_.refs_4_) | copy-start | bytes 1105924
  98.9 0.7 copy-start.12
  99.6 9.6 %copy-start.14 = (s32[4]{0:T(128)S(1)}, s32[4]{0:T(128)}, u32[]{:S(2)}) copy-start(s32[4]{0:T(128)} %pad_add_fusion.refs_0_.flag_ref) | copy-start | bytes 52
  104.8 4.4 %collective-permute-start.16 = (bf16[4,688,384]{2,1,0:T(8,128)(2,1)}, bf16[4,688,384]{2,1,0:T(8,128)(2,1)S(1)}, u32[]{:S(2)}, u32[]{:S(2)}) collective-permute-start(bf16[4,688,384]{2,1,0:T(8,128)(2,1)} %get-tuple-element.97), channel_id=1, source_target_pairs={{0,1},{1,0},{2,3},{3,2},{4,5},{5,4},{6,7},{7,6},{8,9},{9,8},{10,11... | collective-permute-start | bytes 6340616 | tf_op jit(solution)/shard_map/ppermute | solution.py:772
  109.2 1.6 copy-start
  111.9 15.9 %collective-permute-start.17 = (bf16[688,384]{1,0:T(8,128)(2,1)S(1)}, bf16[688,384]{1,0:T(8,128)(2,1)S(1)}, u32[]{:S(2)}, u32[]{:S(2)}) collective-permute-start(bf16[688,384]{1,0:T(8,128)(2,1)S(1)} %get-tuple-element.98), channel_id=1, source_target_pairs={{0,2},{1,3},{2,0},{3,1},{4,6},{5,7},{6,4},{7,5},{8,10},{9,11},{10,... | collective-permute-start | bytes 1585160 | tf_op jit(solution)/shard_map/ppermute | solution.py:780
  115.5 24.0 %copy-start.6 = (bf16[256,768]{1,0:T(8,128)(2,1)S(1)}, bf16[256,768]{1,0:T(8,128)(2,1)}, u32[]{:S(2)}) copy-start(bf16[256,768]{1,0:T(8,128)(2,1)} %get-tuple-element.96.refs_3_) | copy-start | bytes 1179652
  115.5 12.3 %collective-permute-start.18 = (bf16[688,384]{1,0:T(8,128)(2,1)S(1)}, bf16[688,384]{1,0:T(8,128)(2,1)S(1)}, u32[]{:S(2)}, u32[]{:S(2)}) collective-permute-start(bf16[688,384]{1,0:T(8,128)(2,1)S(1)} %get-tuple-element.101), channel_id=1, source_target_pairs={{2,4},{3,5},{4,2},{5,3},{10,12},{11,13},{12,10},{13,11},{18,20},{1... | collective-permute-start | bytes 1585160 | tf_op jit(solution)/shard_map/ppermute | solution.py:780
  116.3 29.6 %collective-permute-start.22 = (bf16[240,768]{1,0:T(8,128)(2,1)}, bf16[240,768]{1,0:T(8,128)(2,1)}, u32[]{:S(2)}, u32[]{:S(2)}) collective-permute-start(bf16[240,768]{1,0:T(8,128)(2,1)} %fusion.refs_9_), channel_id=1, source_target_pairs={{2,6},{3,7},{4,0},{5,1},{10,14},{11,15},{12,8},{13,9},{18,22},{19,... | collective-permute-start | bytes 1105928 | tf_op jit(solution)/shard_map/ppermute | solution.py:780
  130.3 28.2 %collective-permute-start.19 = (bf16[688,384]{1,0:T(8,128)(2,1)}, bf16[688,384]{1,0:T(8,128)(2,1)S(1)}, u32[]{:S(2)}, u32[]{:S(2)}) collective-permute-start(bf16[688,384]{1,0:T(8,128)(2,1)} %get-tuple-element.102), channel_id=1, source_target_pairs={{0,2},{1,3},{6,4},{7,5},{8,10},{9,11},{14,12},{15,13},{16,18},{17,... | collective-permute-start | bytes 1585160 | tf_op jit(solution)/shard_map/ppermute | solution.py:780
  136.8 21.6 %collective-permute-start.20 = (bf16[688,384]{1,0:T(8,128)(2,1)}, bf16[688,384]{1,0:T(8,128)(2,1)S(1)}, u32[]{:S(2)}, u32[]{:S(2)}) collective-permute-start(bf16[688,384]{1,0:T(8,128)(2,1)} %get-tuple-element.103), channel_id=1, source_target_pairs={{0,4},{1,5},{6,2},{7,3},{8,12},{9,13},{14,10},{15,11},{16,20},{17,... | collective-permute-start | bytes 1585160 | tf_op jit(solution)/shard_map/ppermute | solution.py:780
  138.2 26.5 %collective-permute-start.21 = (bf16[688,384]{1,0:T(8,128)(2,1)}, bf16[688,384]{1,0:T(8,128)(2,1)S(1)}, u32[]{:S(2)}, u32[]{:S(2)}) collective-permute-start(bf16[688,384]{1,0:T(8,128)(2,1)} %get-tuple-element.104), channel_id=1, source_target_pairs={{2,6},{3,7},{4,0},{5,1},{10,14},{11,15},{12,8},{13,9},{18,22},{19,... | collective-permute-start | bytes 1585160 | tf_op jit(solution)/shard_map/ppermute | solution.py:780
  139.5 7.1 %copy-start.9 = (bf16[240,768]{1,0:T(8,128)(2,1)S(1)}, bf16[240,768]{1,0:T(8,128)(2,1)}, u32[]{:S(2)}) copy-start(bf16[240,768]{1,0:T(8,128)(2,1)} %copy-done.8) | copy-start | bytes 1105924
  139.5 7.1 %copy-start.11 = (bf16[240,768]{1,0:T(8,128)(2,1)S(1)}, bf16[240,768]{1,0:T(8,128)(2,1)}, u32[]{:S(2)}) copy-start(bf16[240,768]{1,0:T(8,128)(2,1)} %copy-done.10) | copy-start | bytes 1105924
  139.5 7.0 %copy-start.13 = (bf16[240,768]{1,0:T(8,128)(2,1)S(1)}, bf16[240,768]{1,0:T(8,128)(2,1)}, u32[]{:S(2)}) copy-start(bf16[240,768]{1,0:T(8,128)(2,1)} %copy-done.12) | copy-start | bytes 1105924
  139.5 11.3 %collective-permute-start.15 = (bf16[256,768]{1,0:T(8,128)(2,1)S(1)}, bf16[256,768]{1,0:T(8,128)(2,1)S(1)}, u32[]{:S(2)}, u32[]{:S(2)}) collective-permute-start(bf16[256,768]{1,0:T(8,128)(2,1)S(1)} %copy-done.6), channel_id=1, source_target_pairs={{0,8},{8,0},{1,9},{9,1},{2,10},{10,2},{3,11},{11,3},{4,12},{12,4},... | collective-permute-start | bytes 1179656 | tf_op jit(solution)/shard_map/ppermute | solution.py:758
  145.9 11.4 %copy-start.3 = (bf16[256,768]{1,0:T(8,128)(2,1)S(1)}, bf16[256,768]{1,0:T(8,128)(2,1)}, u32[]{:S(2)}) copy-start(bf16[256,768]{1,0:T(8,128)(2,1)} %shard_map.260.refs_0_) | copy-start | bytes 1179652
  145.9 11.4 %copy-start.4 = (bf16[128,768]{1,0:T(8,128)(2,1)S(1)}, bf16[128,768]{1,0:T(8,128)(2,1)}, u32[]{:S(2)}) copy-start(bf16[128,768]{1,0:T(8,128)(2,1)} %get-tuple-element.73.refs_13_.refs_6_) | copy-start | bytes 589828
  145.9 11.3 %copy-start.5 = (bf16[128,768]{1,0:T(8,128)(2,1)S(1)}, bf16[128,768]{1,0:T(8,128)(2,1)}, u32[]{:S(2)}) copy-start(bf16[128,768]{1,0:T(8,128)(2,1)} %get-tuple-element.72.refs_12_.refs_5_) | copy-start | bytes 589828
  145.9 11.3 %copy-start.7 = (bf16[256,768]{1,0:T(8,128)(2,1)S(1)}, bf16[256,768]{1,0:T(8,128)(2,1)}, u32[]{:S(2)}) copy-start(bf16[256,768]{1,0:T(8,128)(2,1)} %get-tuple-element.95.refs_2_) | copy-start | bytes 1179652
  145.9 11.3 %collective-permute-start.14 = (bf16[256,768]{1,0:T(8,128)(2,1)}, bf16[256,768]{1,0:T(8,128)(2,1)S(1)}, u32[]{:S(2)}, u32[]{:S(2)}) collective-permute-start(bf16[256,768]{1,0:T(8,128)(2,1)} %shard_map.260.refs_0_), channel_id=1, source_target_pairs={{0,8},{8,0},{1,9},{9,1},{2,10},{10,2},{3,11},{11,3},{4,12},{12,4},... | collective-permute-start | bytes 1179656 | tf_op jit(solution)/shard_map/ppermute | solution.py:758
  149.0 15.6 %copy-start.1 = (bf16[4,688,384]{2,1,0:T(8,128)(2,1)S(1)}, bf16[4,688,384]{2,1,0:T(8,128)(2,1)}, u32[]{:S(2)}) copy-start(bf16[4,688,384]{2,1,0:T(8,128)(2,1)} %get-tuple-element.94.refs_7_.refs_1_.refs_0_) | copy-start | bytes 6340612
  167.2 1.1 copy-start.24

commit v4 on v3

--- a/solution.py
+++ b/solution.py
@@ -686,7 +686,7 @@
         in_specs=[SM] + specs,
         out_specs=[VM] * 2,
         scratch_shapes=list(scratch),
-        compiler_params=params(54),
+        compiler_params=params(24),
         cost_estimate=pl.CostEstimate(flops=flops, bytes_accessed=4 * math.prod(block), transcendentals=0),
     )(flags, *operands)
 

time: 169 us -> 162 us (0.959)
  Pallas kernels: 63.4 us -> 58.2 us
    pallas_call x2, Pallas kernels: 10.3 us -> 5.16 us  [call_blocks(): pl.pallas_call(kernel, out_shape=outs, in_specs=[SM] + specs, out_specs=[...]
    unnamed x54 -> x74, local copies, waits for them, and re-layouts: 6.16 us -> 5.17 us
  transfers between devices with their start and end apart: 23 -> 23, of which waited for: 12 -> 12; matrix products, arithmetic and copies ran while one was open for 1% -> 1% of each run, Pallas kernels for 25% -> 26%
where the time goes in v4:
time: 162 us; the launch traced here: 161 us
  Pallas kernels  58.2 us (36%)
  waiting for transfers between devices  49.6 us (31%)
  starting transfers between devices  43.3 us (27%)
  local copies, waits for them, and re-layouts  5.7 us (4%)
  other arithmetic  2.85 us (2%)
    ppermute x10, starting transfers between devices, send(): lax.ppermute(value, 'dp', [(2 * a + c, 2 * b + c) for a, b in pairs for c...  24.3 us
    pallas_call x2, Pallas kernels, call_fb(): pl.pallas_call(functools.partial(fb_kernel, at), out_shape=outs, in_specs...  20.2 us
    ppermute x10, waiting for transfers between devices, send(): lax.ppermute(value, 'dp', [(2 * a + c, 2 * b + c) for a, b in pairs for c...  18.1 us
    pallas_call x1, Pallas kernels, call_b(): pl.pallas_call(functools.partial(b_kernel, micro), out_shape=outs, in_spe...  10.5 us
    ppermute x3, waiting for transfers between devices, swap(): return lax.ppermute(value, 'tensor', [(0, 1), (1, 0)])  9.73 us
    ppermute x4, starting transfers between devices, handed(): straight = lax.ppermute(value, 'section', [(source, target)])  8.87 us
    pallas_call x1, Pallas kernels, call_f(): pl.pallas_call(functools.partial(f_kernel, micro), out_shape=out, in_spec...  8.34 us
    ppermute x4, waiting for transfers between devices, handed(): straight = lax.ppermute(value, 'section', [(source, target)])  7.91 us
  transfers between devices with their start and end apart: 23, of which 12 were waited for; matrix products, arithmetic and copies ran while one was open for 1% of the time, Pallas kernels for 26%

profile of v4, /device:TPU:0, one launch (start us, length us, event | category | flops | bytes accessed | tf_op | source)
XLA Modules:
  0.0 161.0 jit_solution(14486399552096864725)
XLA Ops:
  0.7 0.6 pad_add_fusion.refs_0_.flag_ref
  1.3 8.3 %shard_map.254 = (bf16[128,768]{1,0:T(8,128)(2,1)}, bf16[128,768]{1,0:T(8,128)(2,1)}, f32[16,1536]{1,0:T(8,128)}) custom-call(s32[4]{0:T(128)} %pad_add_fusion.refs_0_.flag_ref, bf16[2,128,768]{2,1,0:T(8,128)(2,1)} %bitcast.61, f32[3,128,128]{2,1,0:T(8,128)} %constant.76.clone.refs_2_.refs_5_, bf16[3,768,384]{2,1,0:T(8,128)(2,1)} %bitcast.52, ...), custom_call_target="tpu_custom_call" | custom-call | flops 1811939328 | bytes 7077888 | tf_op jit(solution)/shard_map/pallas_call | solution.py:605
  9.6 4.9 %collective-permute-start.2 = (bf16[128,768]{1,0:T(8,128)(2,1)}, bf16[128,768]{1,0:T(8,128)(2,1)S(1)}, u32[]{:S(2)}, u32[]{:S(2)}) collective-permute-start(bf16[128,768]{1,0:T(8,128)(2,1)} %get-tuple-element.66), channel_id=1, source_target_pairs={{0,16},{1,17},{2,18},{3,19},{4,20},{5,21},{6,22},{7,23},{8,24},{9,... | collective-permute-start | bytes 589832 | tf_op jit(solution)/shard_map/ppermute | solution.py:752
  14.5 2.2 %collective-permute-start.3 = (bf16[128,768]{1,0:T(8,128)(2,1)}, bf16[128,768]{1,0:T(8,128)(2,1)S(1)}, u32[]{:S(2)}, u32[]{:S(2)}) collective-permute-start(bf16[128,768]{1,0:T(8,128)(2,1)} %get-tuple-element.66), channel_id=1, source_target_pairs={{0,24},{8,16},{1,25},{9,17},{2,26},{10,18},{3,27},{11,19},{4,28},{... | collective-permute-start | bytes 589832 | tf_op jit(solution)/shard_map/ppermute | solution.py:754
  16.7 1.3 collective-permute-start
  18.0 1.3 collective-permute-start.1
  19.3 0.7 collective-permute-done.2.refs_3_
  20.1 4.2 %collective-permute-done.3.refs_4_ = bf16[128,768]{1,0:T(8,128)(2,1)S(1)} collective-permute-done((bf16[128,768]{1,0:T(8,128)(2,1)}, bf16[128,768]{1,0:T(8,128)(2,1)S(1)}, u32[]{:S(2)}, u32[]{:S(2)}) %collective-permute-start.3) | collective-permute-done | bytes 196640 | tf_op jit(solution)/shard_map/ppermute | solution.py:754
  24.3 0.7 copy-done.34
  24.9 10.1 %shard_map.256 = (bf16[128,768]{1,0:T(8,128)(2,1)}, bf16[128,768]{1,0:T(8,128)(2,1)}, bf16[128,768]{1,0:T(8,128)(2,1)}, bf16[128,768]{1,0:T(8,128)(2,1)}, bf16[1...) custom-call(s32[4]{0:T(128)} %pad_add_fusion.refs_0_.flag_ref, ...), custom_call_target="tpu_custom_call" | custom-call | flops 1811939328 | bytes 7077888 | tf_op jit(solution)/shard_map/pallas_call | solution.py:628
  35.0 0.0 copy-start.2
  35.1 0.0 copy-start.22
  35.1 1.4 collective-permute-start.5
  36.5 1.5 collective-permute-start.7
  38.0 0.0 copy-start.31
  38.0 0.7 copy-done.31
  38.7 0.7 copy-done.32
  39.4 10.1 %shard_map.255 = (bf16[128,768]{1,0:T(8,128)(2,1)}, bf16[128,768]{1,0:T(8,128)(2,1)}, bf16[128,768]{1,0:T(8,128)(2,1)}, bf16[128,768]{1,0:T(8,128)(2,1)}, bf16[1...) custom-call(s32[4]{0:T(128)} %pad_add_fusion.refs_0_.flag_ref, ...), custom_call_target="tpu_custom_call" | custom-call | flops 1811939328 | bytes 7077888 | tf_op jit(solution)/shard_map/pallas_call | solution.py:628
  49.4 1.3 collective-permute-start.4
  50.7 1.3 collective-permute-start.6
  52.1 7.2 %collective-permute-done.4.refs_2_.refs_8_ = bf16[128,768]{1,0:T(8,128)(2,1)S(1)} collective-permute-done((bf16[128,768]{1,0:T(8,128)(2,1)}, bf16[128,768]{1,0:T(8,128)(2,1)S(1)}, u32[]{:S(2)}, u32[]{:S(2)}) %collective-permute-start.4) | collective-permute-done | bytes 196640 | tf_op jit(solution)/shard_map/ppermute | solution.py:752
  59.3 2.1 %collective-permute-done.6.refs_4_.refs_10_ = bf16[128,768]{1,0:T(8,128)(2,1)S(1)} collective-permute-done((bf16[128,768]{1,0:T(8,128)(2,1)}, bf16[128,768]{1,0:T(8,128)(2,1)S(1)}, u32[]{:S(2)}, u32[]{:S(2)}) %collective-permute-start.6) | collective-permute-done | bytes 196640 | tf_op jit(solution)/shard_map/ppermute | solution.py:754
  61.4 1.1 copy-done.7
  62.4 0.9 copy-done.21
  63.3 3.0 %shard_map.257 = (bf16[4,240,768]{2,1,0:T(8,128)(2,1)}, bf16[4,240,768]{2,1,0:T(8,128)(2,1)S(1)}) custom-call(s32[4]{0:T(128)S(1)} %copy-done.22, bf16[2,128,768]{2,1,0:T(8,128)(2,1)S(1)} %bitcast.41, bf16[128,768]{1,0:T(8,128)(2,1)S(1)} %collective-permute-done.4.refs_2_.refs_8_, bf16[128,768]{1,0:T(8,128)(2,1)S(1)} %collective-permute-done.5.refs_3_.refs_9_, ...), custom_call_target="tpu_custom_call" | custom-call | flops 754974720 | bytes 2949120 | tf_op jit(solution)/shard_map/pallas_call | solution.py:683
  66.3 0.1 collective-permute-start.8
  66.5 3.4 %collective-permute-done.8.refs_1_ = bf16[4,240,768]{2,1,0:T(8,128)(2,1)S(1)} collective-permute-done((bf16[4,240,768]{2,1,0:T(8,128)(2,1)}, bf16[4,240,768]{2,1,0:T(8,128)(2,1)S(1)}, u32[]{:S(2)}, u32[]{:S(2)}) %collective-permute-start.8) | collective-permute-done | bytes 1474592 | tf_op jit(solution)/shard_map/ppermute | solution.py:772
  69.9 1.3 fusion.4
  71.2 1.5 collective-permute-start.10
  72.8 2.4 %collective-permute-start.11 = (bf16[240,768]{1,0:T(8,128)(2,1)}, bf16[240,768]{1,0:T(8,128)(2,1)S(1)}, u32[]{:S(2)}, u32[]{:S(2)}) collective-permute-start(bf16[240,768]{1,0:T(8,128)(2,1)} %get-tuple-element.126.refs_27_), channel_id=1, source_target_pairs={{0,2},{1,3},{6,4},{7,5},{8,10},{9,11},{14,12},{15,13},{16,18},{17,... | collective-permute-start | bytes 1105928 | tf_op jit(solution)/shard_map/ppermute | solution.py:780
  75.2 0.7 collective-permute-start.12
  75.9 4.9 %collective-permute-start.13 = (bf16[240,768]{1,0:T(8,128)(2,1)}, bf16[240,768]{1,0:T(8,128)(2,1)S(1)}, u32[]{:S(2)}, u32[]{:S(2)}) collective-permute-start(bf16[240,768]{1,0:T(8,128)(2,1)} %get-tuple-element.127.refs_26_), channel_id=1, source_target_pairs={{0,4},{1,5},{6,2},{7,3},{8,12},{9,13},{14,10},{15,11},{16,20},{17,... | collective-permute-start | bytes 1105928 | tf_op jit(solution)/shard_map/ppermute | solution.py:780
  80.8 10.5 %shard_map.258 = (bf16[256,768]{1,0:T(8,128)(2,1)}, bf16[256,1536]{1,0:T(8,128)(2,1)}, bf16[256,1152]{1,0:T(8,128)(2,1)}, f32[16,384]{1,0:T(8,128)}, f32[8,384]{1,0:T(8,128)}, /*index=5*/bf16[256,768]{1,0:T(8,128)(2,1)}) custom-call(s32[4]{0:T(128)} %pad_add_fusion.refs_0_.flag_ref, bf16[2,128,768]{2,1,0:T(8,128)(2,1)} %bitcast.40, ...), custom_call_target="tpu_custom_call" | custom-call | flops 1811939328 | bytes 7077888 | tf_op jit(solution)/shard_map/pallas_call | solution.py:666
  91.3 0.0 copy-start.24
  91.3 0.0 copy-start.25
  91.3 1.5 collective-permute-start.9
  92.9 0.9 fusion.refs_9_
  93.8 1.5 collective-permute-done.9.refs_4_
  95.3 1.7 %collective-permute-done.13.refs_12_.refs_5_ = bf16[240,768]{1,0:T(8,128)(2,1)S(1)} collective-permute-done((bf16[240,768]{1,0:T(8,128)(2,1)}, bf16[240,768]{1,0:T(8,128)(2,1)S(1)}, u32[]{:S(2)}, u32[]{:S(2)}) %collective-permute-start.13) | collective-permute-done | bytes 368672 | tf_op jit(solution)/shard_map/ppermute | solution.py:780
  97.1 2.2 %shard_map.259 = (bf16[4,688,384]{2,1,0:T(8,128)(2,1)S(1)}, bf16[4,688,384]{2,1,0:T(8,128)(2,1)S(1)}) custom-call(s32[4]{0:T(128)S(1)} %copy-done.23, bf16[256,1536]{1,0:T(8,128)(2,1)S(1)} %copy-done.24, bf16[256,1152]{1,0:T(8,128)(2,1)S(1)} %copy-done.25, f32[16,384]{1,0:T(8,128)S(1)} %copy-done.30, f32[8,384]{1,0:T(8,128)S(1)} %collective-permute-done.9.refs_4_, ...), custom_call_target="tpu_custom_call" | custom-call | flops 1056964608 | bytes 4227072 | tf_op jit(solution)/shard_map/pallas_call | solution.py:683
  99.3 0.1 collective-permute-start.16
  99.4 4.2 %collective-permute-done.16.refs_2_.refs_1_ = bf16[4,688,384]{2,1,0:T(8,128)(2,1)S(1)} collective-permute-done((bf16[4,688,384]{2,1,0:T(8,128)(2,1)S(1)}, bf16[4,688,384]{2,1,0:T(8,128)(2,1)S(1)}, u32[]{:S(2)}, u32[]{:S(2)}) %collective-permute-start.16) | collective-permute-done | bytes 2113568 | tf_op jit(solution)/shard_map/ppermute | solution.py:772
  103.6 1.0 shard_map.261
  104.7 3.5 %collective-permute-start.17 = (bf16[688,384]{1,0:T(8,128)(2,1)S(1)}, bf16[688,384]{1,0:T(8,128)(2,1)S(1)}, u32[]{:S(2)}, u32[]{:S(2)}) collective-permute-start(bf16[688,384]{1,0:T(8,128)(2,1)S(1)} %get-tuple-element.98), channel_id=1, source_target_pairs={{0,2},{1,3},{2,0},{3,1},{4,6},{5,7},{6,4},{7,5},{8,10},{9,11},{10,... | collective-permute-start | bytes 1585160 | tf_op jit(solution)/shard_map/ppermute | solution.py:780
  108.2 0.8 collective-permute-start.18
  109.0 1.3 collective-permute-start.22
  110.3 10.2 %collective-permute-done.17.refs_7_.refs_3_.refs_2_ = bf16[688,384]{1,0:T(8,128)(2,1)S(1)} collective-permute-done((bf16[688,384]{1,0:T(8,128)(2,1)S(1)}, bf16[688,384]{1,0:T(8,128)(2,1)S(1)}, u32[]{:S(2)}, u32[]{:S(2)}) %collective-permute-start.17) | collective-permute-done | bytes 528416 | tf_op jit(solution)/shard_map/ppermute | solution.py:780
  120.5 2.5 %shard_map.263 = (bf16[688,384]{1,0:T(8,128)(2,1)}, bf16[688,384]{1,0:T(8,128)(2,1)}, bf16[688,384]{1,0:T(8,128)(2,1)}) custom-call(s32[4]{0:T(128)S(1)} %copy-done.23, bf16[4,688,384]{2,1,0:T(8,128)(2,1)S(1)} %get-tuple-element.94.refs_7_.refs_1_.refs_0_, bf16[4,688,384]{2,1,0:T(8,128)(2,1)S(1)} %collective-permute-done.16.refs_2_.refs_1_, ...), custom_call_target="tpu_custom_call" | custom-call | tf_op jit(solution)/shard_map/pallas_call | solution.py:696
  123.0 6.5 %collective-permute-start.19 = (bf16[688,384]{1,0:T(8,128)(2,1)}, bf16[688,384]{1,0:T(8,128)(2,1)S(1)}, u32[]{:S(2)}, u32[]{:S(2)}) collective-permute-start(bf16[688,384]{1,0:T(8,128)(2,1)} %get-tuple-element.102), channel_id=1, source_target_pairs={{0,2},{1,3},{6,4},{7,5},{8,10},{9,11},{14,12},{15,13},{16,18},{17,... | collective-permute-start | bytes 1585160 | tf_op jit(solution)/shard_map/ppermute | solution.py:780
  129.5 1.3 collective-permute-start.20
  130.9 1.3 collective-permute-start.21
  132.2 1.5 collective-permute-start.15
  133.7 4.8 %shard_map.260.refs_0_ = bf16[256,768]{1,0:T(8,128)(2,1)} custom-call(bf16[128,384]{1,0:T(8,128)(2,1)} %get-tuple-element.65.refs_8_.refs_0_, bf16[128,384]{1,0:T(8,128)(2,1)} %get-tuple-element.67.refs_9_.refs_1_, bf16[128,1536]{1,0:T(8,128)(2,1)} %get-tuple-element.68.refs_6_.refs_2_, bf16[128,1536]{1,0:T(8,128)(2,1)} %get-tuple-element.69.refs_7_.refs_3_, ...), custom_call_target="tpu_custom_call" | custom-call | flops 754974720 | bytes 2949120 | tf_op jit(solution)/shard_map/pallas_call | solution.py:734
  138.6 0.0 copy-start.3
  138.6 0.6 collective-permute-start.14
  139.2 2.5 %shard_map.265 = (f32[192,768]{1,0:T(8,128)}, f32[48,768]{1,0:T(8,128)}) custom-call(s32[4]{0:T(128)S(1)} %copy-done.23, bf16[4,240,768]{2,1,0:T(8,128)(2,1)S(1)} %get-tuple-element.84.refs_0_, bf16[4,240,768]{2,1,0:T(8,128)(2,1)S(1)} %collective-permute-done.8.refs_1_, bf16[240,768]{1,0:T(8,128)(2,1)S(1)} %collective-permute-done.10.refs_2_, ...), custom_call_target="tpu_custom_call" | custom-call | tf_op jit(solution)/shard_map/pallas_call | solution.py:708
  141.7 1.8 %collective-permute-done.15.refs_4_ = bf16[256,768]{1,0:T(8,128)(2,1)S(1)} collective-permute-done((bf16[256,768]{1,0:T(8,128)(2,1)S(1)}, bf16[256,768]{1,0:T(8,128)(2,1)S(1)}, u32[]{:S(2)}, u32[]{:S(2)}) %collective-permute-start.15) | collective-permute-done | bytes 393248 | tf_op jit(solution)/shard_map/ppermute | solution.py:758
  143.5 6.4 %collective-permute-done.14.refs_1_ = bf16[256,768]{1,0:T(8,128)(2,1)S(1)} collective-permute-done((bf16[256,768]{1,0:T(8,128)(2,1)}, bf16[256,768]{1,0:T(8,128)(2,1)S(1)}, u32[]{:S(2)}, u32[]{:S(2)}) %collective-permute-start.14) | collective-permute-done | bytes 393248 | tf_op jit(solution)/shard_map/ppermute | solution.py:758
  150.0 1.2 shard_map.262
  151.2 6.2 %collective-permute-done.21.refs_6_ = bf16[688,384]{1,0:T(8,128)(2,1)S(1)} collective-permute-done((bf16[688,384]{1,0:T(8,128)(2,1)}, bf16[688,384]{1,0:T(8,128)(2,1)S(1)}, u32[]{:S(2)}, u32[]{:S(2)}) %collective-permute-start.21) | collective-permute-done | bytes 528416 | tf_op jit(solution)/shard_map/ppermute | solution.py:780
  157.3 2.0 %shard_map.264 = (f32[96,1536]{1,0:T(8,128)}, f32[3,96,384]{2,1,0:T(8,128)}, f32[5,48]{1,0:T(8,128)S(1)}, f32[3,48]{1,0:T(4,128)S(1)}, f32[1,192]{1,0:T(1,128)}) custom-call(s32[4]{0:T(128)S(1)} %copy-done.23, bf16[4,688,384]{2,1,0:T(8,128)(2,1)S(1)} %copy-done.1, bf16[4,688,384]{2,1,0:T(8,128)(2,1)S(1)} %collective-permute-done.16.refs_2_.refs_1_, ...), custom_call_target="tpu_custom_call" | custom-call | tf_op jit(solution)/shard_map/pallas_call | solution.py:708
  159.4 0.5 fusion.5
  159.9 0.6 copy.31
  160.5 0.5 copy.33
  (72 shorter events, 0.2 us)
Async XLA Ops:
  9.6 10.5 %collective-permute-start.2 = (bf16[128,768]{1,0:T(8,128)(2,1)}, bf16[128,768]{1,0:T(8,128)(2,1)S(1)}, u32[]{:S(2)}, u32[]{:S(2)}) collective-permute-start(bf16[128,768]{1,0:T(8,128)(2,1)} %get-tuple-element.66), channel_id=1, source_target_pairs={{0,16},{1,17},{2,18},{3,19},{4,20},{5,21},{6,22},{7,23},{8,24},{9,... | collective-permute-start | bytes 589832 | tf_op jit(solution)/shard_map/ppermute | solution.py:752
  14.5 9.8 %collective-permute-start.3 = (bf16[128,768]{1,0:T(8,128)(2,1)}, bf16[128,768]{1,0:T(8,128)(2,1)S(1)}, u32[]{:S(2)}, u32[]{:S(2)}) collective-permute-start(bf16[128,768]{1,0:T(8,128)(2,1)} %get-tuple-element.66), channel_id=1, source_target_pairs={{0,24},{8,16},{1,25},{9,17},{2,26},{10,18},{3,27},{11,19},{4,28},{... | collective-permute-start | bytes 589832 | tf_op jit(solution)/shard_map/ppermute | solution.py:754
  16.7 21.3 %collective-permute-start = (bf16[128,768]{1,0:T(8,128)(2,1)}, bf16[128,768]{1,0:T(8,128)(2,1)S(1)}, u32[]{:S(2)}, u32[]{:S(2)}) collective-permute-start(bf16[128,768]{1,0:T(8,128)(2,1)} %get-tuple-element.63), channel_id=1, source_target_pairs={{0,16},{1,17},{2,18},{3,19},{4,20},{5,21},{6,22},{7,23},{8,24},{9,... | collective-permute-start | bytes 589832 | tf_op jit(solution)/shard_map/ppermute | solution.py:752
  18.0 20.0 %collective-permute-start.1 = (bf16[128,768]{1,0:T(8,128)(2,1)}, bf16[128,768]{1,0:T(8,128)(2,1)S(1)}, u32[]{:S(2)}, u32[]{:S(2)}) collective-permute-start(bf16[128,768]{1,0:T(8,128)(2,1)} %get-tuple-element.63), channel_id=1, source_target_pairs={{0,24},{8,16},{1,25},{9,17},{2,26},{10,18},{3,27},{11,19},{4,28},{... | collective-permute-start | bytes 589832 | tf_op jit(solution)/shard_map/ppermute | solution.py:754
  20.1 4.2 %copy-start.33 = (bf16[128,768]{1,0:T(8,128)(2,1)}, bf16[128,768]{1,0:T(8,128)(2,1)S(1)}, u32[]{:S(2)}) copy-start(bf16[128,768]{1,0:T(8,128)(2,1)S(1)} %collective-permute-done.2.refs_3_) | copy-start | bytes 589828
  24.3 0.7 copy-start.34
  35.0 26.3 %copy-start.2 = (bf16[2,1,128,768]{3,2,1,0:T(8,128)(2,1)S(1)}, bf16[2,1,128,768]{3,2,1,0:T(8,128)(2,1)}, u32[]{:S(2)}) copy-start(bf16[2,1,128,768]{3,2,1,0:T(8,128)(2,1)} %param.16) | copy-start | bytes 1179652
  35.0 26.3 %copy-start.6 = (bf16[128,1536]{1,0:T(8,128)(2,1)S(1)}, bf16[128,1536]{1,0:T(8,128)(2,1)}, u32[]{:S(2)}) copy-start(bf16[128,1536]{1,0:T(8,128)(2,1)} %get-tuple-element.69.refs_7_.refs_3_) | copy-start | bytes 1179652
  35.1 26.3 %copy-start.20 = (bf16[128,384]{1,0:T(8,128)(2,1)S(1)}, bf16[128,384]{1,0:T(8,128)(2,1)}, u32[]{:S(2)}) copy-start(bf16[128,384]{1,0:T(8,128)(2,1)} %get-tuple-element.67.refs_9_.refs_1_) | copy-start | bytes 294916
  35.1 26.3 %copy-start.22 = (s32[4]{0:T(128)S(1)}, s32[4]{0:T(128)}, u32[]{:S(2)}) copy-start(s32[4]{0:T(128)} %pad_add_fusion.refs_0_.flag_ref) | copy-start | bytes 52
  35.1 17.0 %collective-permute-start.5 = (bf16[128,768]{1,0:T(8,128)(2,1)}, bf16[128,768]{1,0:T(8,128)(2,1)S(1)}, u32[]{:S(2)}, u32[]{:S(2)}) collective-permute-start(bf16[128,768]{1,0:T(8,128)(2,1)} %get-tuple-element.71), channel_id=1, source_target_pairs={{16,0},{17,1},{18,2},{19,3},{20,4},{21,5},{22,6},{23,7},{24,8},{25... | collective-permute-start | bytes 589832 | tf_op jit(solution)/shard_map/ppermute | solution.py:752
  36.5 15.6 %collective-permute-start.7 = (bf16[128,768]{1,0:T(8,128)(2,1)}, bf16[128,768]{1,0:T(8,128)(2,1)S(1)}, u32[]{:S(2)}, u32[]{:S(2)}) collective-permute-start(bf16[128,768]{1,0:T(8,128)(2,1)} %get-tuple-element.71), channel_id=1, source_target_pairs={{16,8},{24,0},{17,9},{25,1},{18,10},{26,2},{19,11},{27,3},{20,12},... | collective-permute-start | bytes 589832 | tf_op jit(solution)/shard_map/ppermute | solution.py:754
  38.0 0.7 copy-start.31
  38.7 0.7 copy-start.32
  49.4 9.8 %collective-permute-start.4 = (bf16[128,768]{1,0:T(8,128)(2,1)}, bf16[128,768]{1,0:T(8,128)(2,1)S(1)}, u32[]{:S(2)}, u32[]{:S(2)}) collective-permute-start(bf16[128,768]{1,0:T(8,128)(2,1)} %get-tuple-element.70), channel_id=1, source_target_pairs={{16,0},{17,1},{18,2},{19,3},{20,4},{21,5},{22,6},{23,7},{24,8},{25... | collective-permute-start | bytes 589832 | tf_op jit(solution)/shard_map/ppermute | solution.py:752
  50.7 10.6 %collective-permute-start.6 = (bf16[128,768]{1,0:T(8,128)(2,1)}, bf16[128,768]{1,0:T(8,128)(2,1)S(1)}, u32[]{:S(2)}, u32[]{:S(2)}) collective-permute-start(bf16[128,768]{1,0:T(8,128)(2,1)} %get-tuple-element.70), channel_id=1, source_target_pairs={{16,8},{24,0},{17,9},{25,1},{18,10},{26,2},{19,11},{27,3},{20,12},... | collective-permute-start | bytes 589832 | tf_op jit(solution)/shard_map/ppermute | solution.py:754
  52.1 19.2 %copy-start.16 = (bf16[128,768]{1,0:T(8,128)(2,1)}, bf16[128,768]{1,0:T(8,128)(2,1)S(1)}, u32[]{:S(2)}) copy-start(bf16[128,768]{1,0:T(8,128)(2,1)S(1)} %collective-permute-done.5.refs_3_.refs_9_) | copy-start | bytes 589828
  52.1 14.2 %copy-start.17 = (bf16[128,768]{1,0:T(8,128)(2,1)}, bf16[128,768]{1,0:T(8,128)(2,1)S(1)}, u32[]{:S(2)}) copy-start(bf16[128,768]{1,0:T(8,128)(2,1)S(1)} %collective-permute-done.7.refs_5_.refs_11_) | copy-start | bytes 589828
  59.3 7.1 %copy-start.18 = (bf16[128,768]{1,0:T(8,128)(2,1)}, bf16[128,768]{1,0:T(8,128)(2,1)S(1)}, u32[]{:S(2)}) copy-start(bf16[128,768]{1,0:T(8,128)(2,1)S(1)} %collective-permute-done.4.refs_2_.refs_8_) | copy-start | bytes 589828
  61.4 5.0 %copy-start.19 = (bf16[128,768]{1,0:T(8,128)(2,1)}, bf16[128,768]{1,0:T(8,128)(2,1)S(1)}, u32[]{:S(2)}) copy-start(bf16[128,768]{1,0:T(8,128)(2,1)S(1)} %collective-permute-done.6.refs_4_.refs_10_) | copy-start | bytes 589828
  61.4 1.1 copy-start.7
  62.4 0.9 copy-start.21
  66.3 3.5 %collective-permute-start.8 = (bf16[4,240,768]{2,1,0:T(8,128)(2,1)}, bf16[4,240,768]{2,1,0:T(8,128)(2,1)S(1)}, u32[]{:S(2)}, u32[]{:S(2)}) collective-permute-start(bf16[4,240,768]{2,1,0:T(8,128)(2,1)} %get-tuple-element.85), channel_id=1, source_target_pairs={{0,1},{1,0},{2,3},{3,2},{4,5},{5,4},{6,7},{7,6},{8,9},{9,8},{10,11... | collective-permute-start | bytes 4423688 | tf_op jit(solution)/shard_map/ppermute | solution.py:772
  71.2 21.6 %collective-permute-start.10 = (bf16[240,768]{1,0:T(8,128)(2,1)}, bf16[240,768]{1,0:T(8,128)(2,1)S(1)}, u32[]{:S(2)}, u32[]{:S(2)}) collective-permute-start(bf16[240,768]{1,0:T(8,128)(2,1)} %get-tuple-element.129.refs_24_), channel_id=1, source_target_pairs={{0,2},{1,3},{2,0},{3,1},{4,6},{5,7},{6,4},{7,5},{8,10},{9,11},{10,... | collective-permute-start | bytes 1105928 | tf_op jit(solution)/shard_map/ppermute | solution.py:780
  72.8 22.5 %collective-permute-start.11 = (bf16[240,768]{1,0:T(8,128)(2,1)}, bf16[240,768]{1,0:T(8,128)(2,1)S(1)}, u32[]{:S(2)}, u32[]{:S(2)}) collective-permute-start(bf16[240,768]{1,0:T(8,128)(2,1)} %get-tuple-element.126.refs_27_), channel_id=1, source_target_pairs={{0,2},{1,3},{6,4},{7,5},{8,10},{9,11},{14,12},{15,13},{16,18},{17,... | collective-permute-start | bytes 1105928 | tf_op jit(solution)/shard_map/ppermute | solution.py:780
  75.2 20.1 %collective-permute-start.12 = (bf16[240,768]{1,0:T(8,128)(2,1)}, bf16[240,768]{1,0:T(8,128)(2,1)S(1)}, u32[]{:S(2)}, u32[]{:S(2)}) collective-permute-start(bf16[240,768]{1,0:T(8,128)(2,1)} %get-tuple-element.128.refs_25_), channel_id=1, source_target_pairs={{2,4},{3,5},{4,2},{5,3},{10,12},{11,13},{12,10},{13,11},{18,20},{1... | collective-permute-start | bytes 1105928 | tf_op jit(solution)/shard_map/ppermute | solution.py:780
  75.9 21.2 %collective-permute-start.13 = (bf16[240,768]{1,0:T(8,128)(2,1)}, bf16[240,768]{1,0:T(8,128)(2,1)S(1)}, u32[]{:S(2)}, u32[]{:S(2)}) collective-permute-start(bf16[240,768]{1,0:T(8,128)(2,1)} %get-tuple-element.127.refs_26_), channel_id=1, source_target_pairs={{0,4},{1,5},{6,2},{7,3},{8,12},{9,13},{14,10},{15,11},{16,20},{17,... | collective-permute-start | bytes 1105928 | tf_op jit(solution)/shard_map/ppermute | solution.py:780
  80.8 16.3 %copy-start.26 = (bf16[128,768]{1,0:T(8,128)(2,1)S(1)}, bf16[128,768]{1,0:T(8,128)(2,1)}, u32[]{:S(2)}) copy-start(bf16[128,768]{1,0:T(8,128)(2,1)} %get-tuple-element.91.refs_6_) | copy-start | bytes 589828
  80.8 16.3 %copy-start.27 = (bf16[128,768]{1,0:T(8,128)(2,1)S(1)}, bf16[128,768]{1,0:T(8,128)(2,1)}, u32[]{:S(2)}) copy-start(bf16[128,768]{1,0:T(8,128)(2,1)} %get-tuple-element.93.refs_8_) | copy-start | bytes 589828
  80.8 16.3 %copy-start.28 = (bf16[128,768]{1,0:T(8,128)(2,1)S(1)}, bf16[128,768]{1,0:T(8,128)(2,1)}, u32[]{:S(2)}) copy-start(bf16[128,768]{1,0:T(8,128)(2,1)} %get-tuple-element.90.refs_5_) | copy-start | bytes 589828
  80.8 16.3 %copy-start.29 = (bf16[128,768]{1,0:T(8,128)(2,1)S(1)}, bf16[128,768]{1,0:T(8,128)(2,1)}, u32[]{:S(2)}) copy-start(bf16[128,768]{1,0:T(8,128)(2,1)} %get-tuple-element.92.refs_7_) | copy-start | bytes 589828
  91.3 5.8 %copy-start.23 = (s32[4]{0:T(128)S(1)}, s32[4]{0:T(128)}, u32[]{:S(2)}) copy-start(s32[4]{0:T(128)} %pad_add_fusion.refs_0_.flag_ref) | copy-start | bytes 52
  91.3 5.8 %copy-start.24 = (bf16[256,1536]{1,0:T(8,128)(2,1)S(1)}, bf16[256,1536]{1,0:T(8,128)(2,1)}, u32[]{:S(2)}) copy-start(bf16[256,1536]{1,0:T(8,128)(2,1)} %get-tuple-element.86.refs_1_) | copy-start | bytes 2359300
  91.3 5.8 %copy-start.25 = (bf16[256,1152]{1,0:T(8,128)(2,1)S(1)}, bf16[256,1152]{1,0:T(8,128)(2,1)}, u32[]{:S(2)}) copy-start(bf16[256,1152]{1,0:T(8,128)(2,1)} %get-tuple-element.87.refs_2_) | copy-start | bytes 1769476
  91.3 5.8 %copy-start.30 = (f32[16,384]{1,0:T(8,128)S(1)}, f32[16,384]{1,0:T(8,128)}, u32[]{:S(2)}) copy-start(f32[16,384]{1,0:T(8,128)} %get-tuple-element.88.refs_3_) | copy-start | bytes 73732
  91.3 4.0 %collective-permute-start.9 = (f32[8,384]{1,0:T(8,128)}, f32[8,384]{1,0:T(8,128)S(1)}, u32[]{:S(2)}, u32[]{:S(2)}) collective-permute-start(f32[8,384]{1,0:T(8,128)} %get-tuple-element.89), channel_id=1, source_target_pairs={{0,8},{8,0},{1,9},{9,1},{2,10},{10,2},{3,11},{11,3},{4,12},{12,4},... | collective-permute-start | bytes 36872 | tf_op jit(solution)/shard_map/ppermute | solution.py:758
  95.3 4.0 %copy-start.10 = (bf16[240,768]{1,0:T(8,128)(2,1)}, bf16[240,768]{1,0:T(8,128)(2,1)S(1)}, u32[]{:S(2)}) copy-start(bf16[240,768]{1,0:T(8,128)(2,1)S(1)} %collective-permute-done.11.refs_10_.refs_3_) | copy-start | bytes 1105924
  95.3 4.0 %copy-start.12 = (bf16[240,768]{1,0:T(8,128)(2,1)}, bf16[240,768]{1,0:T(8,128)(2,1)S(1)}, u32[]{:S(2)}) copy-start(bf16[240,768]{1,0:T(8,128)(2,1)S(1)} %collective-permute-done.12.refs_11_.refs_4_) | copy-start | bytes 1105924
  97.0 2.3 %copy-start.14 = (bf16[240,768]{1,0:T(8,128)(2,1)}, bf16[240,768]{1,0:T(8,128)(2,1)S(1)}, u32[]{:S(2)}) copy-start(bf16[240,768]{1,0:T(8,128)(2,1)S(1)} %collective-permute-done.13.refs_12_.refs_5_) | copy-start | bytes 1105924
  99.3 21.2 %copy-start = (bf16[4,688,384]{2,1,0:T(8,128)(2,1)}, bf16[4,688,384]{2,1,0:T(8,128)(2,1)S(1)}, u32[]{:S(2)}) copy-start(bf16[4,688,384]{2,1,0:T(8,128)(2,1)S(1)} %get-tuple-element.94.refs_7_.refs_1_.refs_0_) | copy-start | bytes 6340612
  99.3 4.2 %collective-permute-start.16 = (bf16[4,688,384]{2,1,0:T(8,128)(2,1)S(1)}, bf16[4,688,384]{2,1,0:T(8,128)(2,1)S(1)}, u32[]{:S(2)}, u32[]{:S(2)}) collective-permute-start(bf16[4,688,384]{2,1,0:T(8,128)(2,1)S(1)} %get-tuple-element.97), channel_id=1, source_target_pairs={{0,1},{1,0},{2,3},{3,2},{4,5},{5,4},{6,7},{7,6},{8,9},{9,8},{10,11... | collective-permute-start | bytes 6340616 | tf_op jit(solution)/shard_map/ppermute | solution.py:772
  104.7 15.8 %collective-permute-start.17 = (bf16[688,384]{1,0:T(8,128)(2,1)S(1)}, bf16[688,384]{1,0:T(8,128)(2,1)S(1)}, u32[]{:S(2)}, u32[]{:S(2)}) collective-permute-start(bf16[688,384]{1,0:T(8,128)(2,1)S(1)} %get-tuple-element.98), channel_id=1, source_target_pairs={{0,2},{1,3},{2,0},{3,1},{4,6},{5,7},{6,4},{7,5},{8,10},{9,11},{10,... | collective-permute-start | bytes 1585160 | tf_op jit(solution)/shard_map/ppermute | solution.py:780
  108.2 24.0 %copy-start.8 = (bf16[256,768]{1,0:T(8,128)(2,1)S(1)}, bf16[256,768]{1,0:T(8,128)(2,1)}, u32[]{:S(2)}) copy-start(bf16[256,768]{1,0:T(8,128)(2,1)} %get-tuple-element.96.refs_3_) | copy-start | bytes 1179652
  108.2 12.3 %collective-permute-start.18 = (bf16[688,384]{1,0:T(8,128)(2,1)S(1)}, bf16[688,384]{1,0:T(8,128)(2,1)S(1)}, u32[]{:S(2)}, u32[]{:S(2)}) collective-permute-start(bf16[688,384]{1,0:T(8,128)(2,1)S(1)} %get-tuple-element.101), channel_id=1, source_target_pairs={{2,4},{3,5},{4,2},{5,3},{10,12},{11,13},{12,10},{13,11},{18,20},{1... | collective-permute-start | bytes 1585160 | tf_op jit(solution)/shard_map/ppermute | solution.py:780
  109.0 29.6 %collective-permute-start.22 = (bf16[240,768]{1,0:T(8,128)(2,1)}, bf16[240,768]{1,0:T(8,128)(2,1)}, u32[]{:S(2)}, u32[]{:S(2)}) collective-permute-start(bf16[240,768]{1,0:T(8,128)(2,1)} %fusion.refs_9_), channel_id=1, source_target_pairs={{2,6},{3,7},{4,0},{5,1},{10,14},{11,15},{12,8},{13,9},{18,22},{19,... | collective-permute-start | bytes 1105928 | tf_op jit(solution)/shard_map/ppermute | solution.py:780
  123.0 28.2 %collective-permute-start.19 = (bf16[688,384]{1,0:T(8,128)(2,1)}, bf16[688,384]{1,0:T(8,128)(2,1)S(1)}, u32[]{:S(2)}, u32[]{:S(2)}) collective-permute-start(bf16[688,384]{1,0:T(8,128)(2,1)} %get-tuple-element.102), channel_id=1, source_target_pairs={{0,2},{1,3},{6,4},{7,5},{8,10},{9,11},{14,12},{15,13},{16,18},{17,... | collective-permute-start | bytes 1585160 | tf_op jit(solution)/shard_map/ppermute | solution.py:780
  129.5 21.6 %collective-permute-start.20 = (bf16[688,384]{1,0:T(8,128)(2,1)}, bf16[688,384]{1,0:T(8,128)(2,1)S(1)}, u32[]{:S(2)}, u32[]{:S(2)}) collective-permute-start(bf16[688,384]{1,0:T(8,128)(2,1)} %get-tuple-element.103), channel_id=1, source_target_pairs={{0,4},{1,5},{6,2},{7,3},{8,12},{9,13},{14,10},{15,11},{16,20},{17,... | collective-permute-start | bytes 1585160 | tf_op jit(solution)/shard_map/ppermute | solution.py:780
  130.9 26.5 %collective-permute-start.21 = (bf16[688,384]{1,0:T(8,128)(2,1)}, bf16[688,384]{1,0:T(8,128)(2,1)S(1)}, u32[]{:S(2)}, u32[]{:S(2)}) collective-permute-start(bf16[688,384]{1,0:T(8,128)(2,1)} %get-tuple-element.104), channel_id=1, source_target_pairs={{2,6},{3,7},{4,0},{5,1},{10,14},{11,15},{12,8},{13,9},{18,22},{19,... | collective-permute-start | bytes 1585160 | tf_op jit(solution)/shard_map/ppermute | solution.py:780
  132.2 7.1 %copy-start.11 = (bf16[240,768]{1,0:T(8,128)(2,1)S(1)}, bf16[240,768]{1,0:T(8,128)(2,1)}, u32[]{:S(2)}) copy-start(bf16[240,768]{1,0:T(8,128)(2,1)} %copy-done.10) | copy-start | bytes 1105924
  132.2 7.1 %copy-start.13 = (bf16[240,768]{1,0:T(8,128)(2,1)S(1)}, bf16[240,768]{1,0:T(8,128)(2,1)}, u32[]{:S(2)}) copy-start(bf16[240,768]{1,0:T(8,128)(2,1)} %copy-done.12) | copy-start | bytes 1105924
  132.2 7.0 %copy-start.15 = (bf16[240,768]{1,0:T(8,128)(2,1)S(1)}, bf16[240,768]{1,0:T(8,128)(2,1)}, u32[]{:S(2)}) copy-start(bf16[240,768]{1,0:T(8,128)(2,1)} %copy-done.14) | copy-start | bytes 1105924
  132.2 11.3 %collective-permute-start.15 = (bf16[256,768]{1,0:T(8,128)(2,1)S(1)}, bf16[256,768]{1,0:T(8,128)(2,1)S(1)}, u32[]{:S(2)}, u32[]{:S(2)}) collective-permute-start(bf16[256,768]{1,0:T(8,128)(2,1)S(1)} %copy-done.8), channel_id=1, source_target_pairs={{0,8},{8,0},{1,9},{9,1},{2,10},{10,2},{3,11},{11,3},{4,12},{12,4},... | collective-permute-start | bytes 1179656 | tf_op jit(solution)/shard_map/ppermute | solution.py:758
  138.6 11.4 %copy-start.3 = (bf16[256,768]{1,0:T(8,128)(2,1)S(1)}, bf16[256,768]{1,0:T(8,128)(2,1)}, u32[]{:S(2)}) copy-start(bf16[256,768]{1,0:T(8,128)(2,1)} %shard_map.260.refs_0_) | copy-start | bytes 1179652
  138.6 11.4 %copy-start.4 = (bf16[128,768]{1,0:T(8,128)(2,1)S(1)}, bf16[128,768]{1,0:T(8,128)(2,1)}, u32[]{:S(2)}) copy-start(bf16[128,768]{1,0:T(8,128)(2,1)} %get-tuple-element.73.refs_13_.refs_6_) | copy-start | bytes 589828
  138.6 11.4 %copy-start.5 = (bf16[128,768]{1,0:T(8,128)(2,1)S(1)}, bf16[128,768]{1,0:T(8,128)(2,1)}, u32[]{:S(2)}) copy-start(bf16[128,768]{1,0:T(8,128)(2,1)} %get-tuple-element.72.refs_12_.refs_5_) | copy-start | bytes 589828
  138.6 11.4 %copy-start.9 = (bf16[256,768]{1,0:T(8,128)(2,1)S(1)}, bf16[256,768]{1,0:T(8,128)(2,1)}, u32[]{:S(2)}) copy-start(bf16[256,768]{1,0:T(8,128)(2,1)} %get-tuple-element.95.refs_2_) | copy-start | bytes 1179652
  138.6 11.3 %collective-permute-start.14 = (bf16[256,768]{1,0:T(8,128)(2,1)}, bf16[256,768]{1,0:T(8,128)(2,1)S(1)}, u32[]{:S(2)}, u32[]{:S(2)}) collective-permute-start(bf16[256,768]{1,0:T(8,128)(2,1)} %shard_map.260.refs_0_), channel_id=1, source_target_pairs={{0,8},{8,0},{1,9},{9,1},{2,10},{10,2},{3,11},{11,3},{4,12},{12,4},... | collective-permute-start | bytes 1179656 | tf_op jit(solution)/shard_map/ppermute | solution.py:758
  141.7 15.6 %copy-start.1 = (bf16[4,688,384]{2,1,0:T(8,128)(2,1)S(1)}, bf16[4,688,384]{2,1,0:T(8,128)(2,1)}, u32[]{:S(2)}) copy-start(bf16[4,688,384]{2,1,0:T(8,128)(2,1)} %copy-done) | copy-start | bytes 6340612
  159.9 1.1 copy-start.35

commit v5 on v4

--- a/solution.py
+++ b/solution.py
@@ -743,7 +743,7 @@
             pltpu.VMEM((total, hidden), BF),
             pltpu.SemaphoreType.DMA((8,)),
         ],
-        compiler_params=params(54),
+        compiler_params=params(24),
         cost_estimate=cost((ws[1], ws[3]), total, 1),
     )(*mixed, *active, pack, ws[1], ws[3], *after)
 

time: 162 us -> 160 us (0.988)
  Pallas kernels: 58.2 us -> 53.3 us
  waiting for transfers between devices: 49.6 us -> 53.9 us
    ppermute x3, waiting for transfers between devices: 9.73 us -> 14.3 us  [swap(): return lax.ppermute(value, 'tensor', [(0, 1), (1, 0)])]
    pallas_call x1, Pallas kernels: 4.81 us -> 1.46 us  [call_o(): pl.pallas_call(functools.partial(o_kernel, micro), out_shape=jax.ShapeDty...]
    unnamed x74 -> x70, local copies, waits for them, and re-layouts: 5.17 us -> 5.17 us
  transfers between devices with their start and end apart: 23 -> 23, of which waited for: 12 -> 12; matrix products, arithmetic and copies ran while one was open for 1% -> 0% of each run, Pallas kernels for 26% -> 23%
where the time goes in v5:
time: 160 us
  waiting for transfers between devices  53.9 us (34%)
  Pallas kernels  53.3 us (33%)
  starting transfers between devices  43.7 us (27%)
  local copies, waits for them, and re-layouts  5.69 us (4%)
  other arithmetic  2.11 us (1%)
    ppermute x10, starting transfers between devices, send(): lax.ppermute(value, 'dp', [(2 * a + c, 2 * b + c) for a, b in pairs for c...  24.6 us
    pallas_call x2, Pallas kernels, call_fb(): pl.pallas_call(functools.partial(fb_kernel, at), out_shape=outs, in_specs...  20.2 us
    ppermute x10, waiting for transfers between devices, send(): lax.ppermute(value, 'dp', [(2 * a + c, 2 * b + c) for a, b in pairs for c...  17.8 us
    ppermute x3, waiting for transfers between devices, swap(): return lax.ppermute(value, 'tensor', [(0, 1), (1, 0)])  14.3 us
    pallas_call x1, Pallas kernels, call_b(): pl.pallas_call(functools.partial(b_kernel, micro), out_shape=outs, in_spe...  10.4 us
    ppermute x4, starting transfers between devices, handed(): straight = lax.ppermute(value, 'section', [(source, target)])  8.87 us
    pallas_call x1, Pallas kernels, call_f(): pl.pallas_call(functools.partial(f_kernel, micro), out_shape=out, in_spec...  8.34 us
    ppermute x4, waiting for transfers between devices, handed(): straight = lax.ppermute(value, 'section', [(source, target)])  7.91 us
  transfers between devices with their start and end apart: 23, of which 12 were waited for; matrix products, arithmetic and copies ran while one was open for 0% of the time, Pallas kernels for 23%

profile of v5, /device:TPU:0, one launch (start us, length us, event | category | flops | bytes accessed | tf_op | source)
XLA Modules:
  0.0 159.9 jit_solution(2430469734578902507)
XLA Ops:
  0.7 0.6 pad_add_fusion.refs_0_.flag_ref
  1.3 8.3 %shard_map.254 = (bf16[128,768]{1,0:T(8,128)(2,1)}, bf16[128,768]{1,0:T(8,128)(2,1)}, f32[16,1536]{1,0:T(8,128)}) custom-call(s32[4]{0:T(128)} %pad_add_fusion.refs_0_.flag_ref, bf16[2,128,768]{2,1,0:T(8,128)(2,1)} %bitcast.61, f32[3,128,128]{2,1,0:T(8,128)} %constant.76.clone.refs_2_.refs_5_, bf16[3,768,384]{2,1,0:T(8,128)(2,1)} %bitcast.57, ...), custom_call_target="tpu_custom_call" | custom-call | flops 1811939328 | bytes 7077888 | tf_op jit(solution)/shard_map/pallas_call | solution.py:605
  9.6 4.9 %collective-permute-start.2 = (bf16[128,768]{1,0:T(8,128)(2,1)}, bf16[128,768]{1,0:T(8,128)(2,1)S(1)}, u32[]{:S(2)}, u32[]{:S(2)}) collective-permute-start(bf16[128,768]{1,0:T(8,128)(2,1)} %get-tuple-element.66), channel_id=1, source_target_pairs={{0,16},{1,17},{2,18},{3,19},{4,20},{5,21},{6,22},{7,23},{8,24},{9,... | collective-permute-start | bytes 589832 | tf_op jit(solution)/shard_map/ppermute | solution.py:752
  14.5 2.2 %collective-permute-start.3 = (bf16[128,768]{1,0:T(8,128)(2,1)}, bf16[128,768]{1,0:T(8,128)(2,1)S(1)}, u32[]{:S(2)}, u32[]{:S(2)}) collective-permute-start(bf16[128,768]{1,0:T(8,128)(2,1)} %get-tuple-element.66), channel_id=1, source_target_pairs={{0,24},{8,16},{1,25},{9,17},{2,26},{10,18},{3,27},{11,19},{4,28},{... | collective-permute-start | bytes 589832 | tf_op jit(solution)/shard_map/ppermute | solution.py:754
  16.7 1.3 collective-permute-start
  18.0 1.3 collective-permute-start.1
  19.3 0.7 collective-permute-done.2.refs_3_
  20.1 4.2 %collective-permute-done.3.refs_4_ = bf16[128,768]{1,0:T(8,128)(2,1)S(1)} collective-permute-done((bf16[128,768]{1,0:T(8,128)(2,1)}, bf16[128,768]{1,0:T(8,128)(2,1)S(1)}, u32[]{:S(2)}, u32[]{:S(2)}) %collective-permute-start.3) | collective-permute-done | bytes 196640 | tf_op jit(solution)/shard_map/ppermute | solution.py:754
  24.3 0.7 copy-done.32
  24.9 10.1 %shard_map.256 = (bf16[128,768]{1,0:T(8,128)(2,1)}, bf16[128,768]{1,0:T(8,128)(2,1)}, bf16[128,768]{1,0:T(8,128)(2,1)}, bf16[128,768]{1,0:T(8,128)(2,1)}, bf16[1...) custom-call(s32[4]{0:T(128)} %pad_add_fusion.refs_0_.flag_ref, ...), custom_call_target="tpu_custom_call" | custom-call | flops 1811939328 | bytes 7077888 | tf_op jit(solution)/shard_map/pallas_call | solution.py:628
  35.1 0.0 copy-start.2
  35.1 0.0 copy-start.6
  35.1 0.0 copy-start.20
  35.1 1.4 collective-permute-start.5
  36.5 1.5 collective-permute-start.7
  38.0 0.0 copy-start.29
  38.0 0.7 copy-done.29
  38.7 0.7 copy-done.30
  39.4 10.1 %shard_map.255 = (bf16[128,768]{1,0:T(8,128)(2,1)}, bf16[128,768]{1,0:T(8,128)(2,1)}, bf16[128,768]{1,0:T(8,128)(2,1)}, bf16[128,768]{1,0:T(8,128)(2,1)}, bf16[1...) custom-call(s32[4]{0:T(128)} %pad_add_fusion.refs_0_.flag_ref, ...), custom_call_target="tpu_custom_call" | custom-call | flops 1811939328 | bytes 7077888 | tf_op jit(solution)/shard_map/pallas_call | solution.py:628
  49.5 1.3 collective-permute-start.4
  50.8 1.3 collective-permute-start.6
  52.1 7.2 %collective-permute-done.4.refs_2_.refs_8_ = bf16[128,768]{1,0:T(8,128)(2,1)S(1)} collective-permute-done((bf16[128,768]{1,0:T(8,128)(2,1)}, bf16[128,768]{1,0:T(8,128)(2,1)S(1)}, u32[]{:S(2)}, u32[]{:S(2)}) %collective-permute-start.4) | collective-permute-done | bytes 196640 | tf_op jit(solution)/shard_map/ppermute | solution.py:752
  59.3 2.1 %collective-permute-done.6.refs_4_.refs_10_ = bf16[128,768]{1,0:T(8,128)(2,1)S(1)} collective-permute-done((bf16[128,768]{1,0:T(8,128)(2,1)}, bf16[128,768]{1,0:T(8,128)(2,1)S(1)}, u32[]{:S(2)}, u32[]{:S(2)}) %collective-permute-start.6) | collective-permute-done | bytes 196640 | tf_op jit(solution)/shard_map/ppermute | solution.py:754
  61.4 1.1 copy-done.8
  62.5 0.9 copy-done.18
  63.3 3.0 %shard_map.257 = (bf16[4,240,768]{2,1,0:T(8,128)(2,1)}, bf16[4,240,768]{2,1,0:T(8,128)(2,1)S(1)}) custom-call(s32[4]{0:T(128)S(1)} %copy-done.20, bf16[2,128,768]{2,1,0:T(8,128)(2,1)S(1)} %bitcast.51, bf16[128,768]{1,0:T(8,128)(2,1)S(1)} %collective-permute-done.4.refs_2_.refs_8_, bf16[128,768]{1,0:T(8,128)(2,1)S(1)} %collective-permute-done.5.refs_3_.refs_9_, ...), custom_call_target="tpu_custom_call" | custom-call | flops 754974720 | bytes 2949120 | tf_op jit(solution)/shard_map/pallas_call | solution.py:683
  66.3 0.1 collective-permute-start.8
  66.5 3.4 %collective-permute-done.8.refs_1_ = bf16[4,240,768]{2,1,0:T(8,128)(2,1)S(1)} collective-permute-done((bf16[4,240,768]{2,1,0:T(8,128)(2,1)}, bf16[4,240,768]{2,1,0:T(8,128)(2,1)S(1)}, u32[]{:S(2)}, u32[]{:S(2)}) %collective-permute-start.8) | collective-permute-done | bytes 1474592 | tf_op jit(solution)/shard_map/ppermute | solution.py:772
  69.9 1.4 fusion.4
  71.3 1.5 collective-permute-start.10
  72.8 2.4 %collective-permute-start.11 = (bf16[240,768]{1,0:T(8,128)(2,1)}, bf16[240,768]{1,0:T(8,128)(2,1)S(1)}, u32[]{:S(2)}, u32[]{:S(2)}) collective-permute-start(bf16[240,768]{1,0:T(8,128)(2,1)} %get-tuple-element.126.refs_27_), channel_id=1, source_target_pairs={{0,2},{1,3},{6,4},{7,5},{8,10},{9,11},{14,12},{15,13},{16,18},{17,... | collective-permute-start | bytes 1105928 | tf_op jit(solution)/shard_map/ppermute | solution.py:780
  75.2 0.7 collective-permute-start.12
  75.9 4.9 %collective-permute-start.13 = (bf16[240,768]{1,0:T(8,128)(2,1)}, bf16[240,768]{1,0:T(8,128)(2,1)S(1)}, u32[]{:S(2)}, u32[]{:S(2)}) collective-permute-start(bf16[240,768]{1,0:T(8,128)(2,1)} %get-tuple-element.127.refs_26_), channel_id=1, source_target_pairs={{0,4},{1,5},{6,2},{7,3},{8,12},{9,13},{14,10},{15,11},{16,20},{17,... | collective-permute-start | bytes 1105928 | tf_op jit(solution)/shard_map/ppermute | solution.py:780
  80.9 10.4 %shard_map.258 = (bf16[256,768]{1,0:T(8,128)(2,1)}, bf16[256,1536]{1,0:T(8,128)(2,1)}, bf16[256,1152]{1,0:T(8,128)(2,1)}, f32[16,384]{1,0:T(8,128)}, f32[8,384]{1,0:T(8,128)}, /*index=5*/bf16[256,768]{1,0:T(8,128)(2,1)}) custom-call(s32[4]{0:T(128)} %pad_add_fusion.refs_0_.flag_ref, bf16[2,128,768]{2,1,0:T(8,128)(2,1)} %bitcast.50, ...), custom_call_target="tpu_custom_call" | custom-call | flops 1811939328 | bytes 7077888 | tf_op jit(solution)/shard_map/pallas_call | solution.py:666
  91.3 0.0 copy-start.21
  91.3 1.5 collective-permute-start.9
  92.9 0.1 fusion.refs_9_
  93.0 2.3 %collective-permute-done.9.refs_4_ = f32[8,384]{1,0:T(8,128)S(1)} collective-permute-done((f32[8,384]{1,0:T(8,128)}, f32[8,384]{1,0:T(8,128)S(1)}, u32[]{:S(2)}, u32[]{:S(2)}) %collective-permute-start.9) | collective-permute-done | bytes 12320 | tf_op jit(solution)/shard_map/ppermute | solution.py:758
  95.3 1.8 %collective-permute-done.13.refs_12_.refs_5_ = bf16[240,768]{1,0:T(8,128)(2,1)S(1)} collective-permute-done((bf16[240,768]{1,0:T(8,128)(2,1)}, bf16[240,768]{1,0:T(8,128)(2,1)S(1)}, u32[]{:S(2)}, u32[]{:S(2)}) %collective-permute-start.13) | collective-permute-done | bytes 368672 | tf_op jit(solution)/shard_map/ppermute | solution.py:780
  97.1 2.2 %shard_map.259 = (bf16[4,688,384]{2,1,0:T(8,128)(2,1)S(1)}, bf16[4,688,384]{2,1,0:T(8,128)(2,1)S(1)}) custom-call(s32[4]{0:T(128)S(1)} %copy-done.21, bf16[256,1536]{1,0:T(8,128)(2,1)S(1)} %copy-done.22, bf16[256,1152]{1,0:T(8,128)(2,1)S(1)} %copy-done.23, f32[16,384]{1,0:T(8,128)S(1)} %copy-done.28, f32[8,384]{1,0:T(8,128)S(1)} %collective-permute-done.9.refs_4_, ...), custom_call_target="tpu_custom_call" | custom-call | flops 1056964608 | bytes 4227072 | tf_op jit(solution)/shard_map/pallas_call | solution.py:683
  99.3 0.1 collective-permute-start.16
  99.4 4.2 %collective-permute-done.16.refs_2_.refs_1_ = bf16[4,688,384]{2,1,0:T(8,128)(2,1)S(1)} collective-permute-done((bf16[4,688,384]{2,1,0:T(8,128)(2,1)S(1)}, bf16[4,688,384]{2,1,0:T(8,128)(2,1)S(1)}, u32[]{:S(2)}, u32[]{:S(2)}) %collective-permute-start.16) | collective-permute-done | bytes 2113568 | tf_op jit(solution)/shard_map/ppermute | solution.py:772
  103.6 1.0 shard_map.261
  104.6 3.5 %collective-permute-start.17 = (bf16[688,384]{1,0:T(8,128)(2,1)S(1)}, bf16[688,384]{1,0:T(8,128)(2,1)S(1)}, u32[]{:S(2)}, u32[]{:S(2)}) collective-permute-start(bf16[688,384]{1,0:T(8,128)(2,1)S(1)} %get-tuple-element.98), channel_id=1, source_target_pairs={{0,2},{1,3},{2,0},{3,1},{4,6},{5,7},{6,4},{7,5},{8,10},{9,11},{10,... | collective-permute-start | bytes 1585160 | tf_op jit(solution)/shard_map/ppermute | solution.py:780
  108.2 0.0 copy-start.9
  108.2 0.8 collective-permute-start.18
  109.0 1.4 collective-permute-start.22
  110.5 10.0 %collective-permute-done.17.refs_7_.refs_3_.refs_2_ = bf16[688,384]{1,0:T(8,128)(2,1)S(1)} collective-permute-done((bf16[688,384]{1,0:T(8,128)(2,1)S(1)}, bf16[688,384]{1,0:T(8,128)(2,1)S(1)}, u32[]{:S(2)}, u32[]{:S(2)}) %collective-permute-start.17) | collective-permute-done | bytes 528416 | tf_op jit(solution)/shard_map/ppermute | solution.py:780
  120.5 1.5 shard_map.263
  122.0 6.7 %collective-permute-start.19 = (bf16[688,384]{1,0:T(8,128)(2,1)S(1)}, bf16[688,384]{1,0:T(8,128)(2,1)S(1)}, u32[]{:S(2)}, u32[]{:S(2)}) collective-permute-start(bf16[688,384]{1,0:T(8,128)(2,1)S(1)} %get-tuple-element.102), channel_id=1, source_target_pairs={{0,2},{1,3},{6,4},{7,5},{8,10},{9,11},{14,12},{15,13},{16,18},{17,... | collective-permute-start | bytes 1585160 | tf_op jit(solution)/shard_map/ppermute | solution.py:780
  128.7 1.3 collective-permute-start.20
  130.0 1.3 collective-permute-start.21
  131.3 1.5 collective-permute-start.15
  132.9 1.5 shard_map.260.refs_0_
  134.4 0.6 collective-permute-start.14
  135.1 2.0 %shard_map.265 = (f32[192,768]{1,0:T(8,128)}, f32[48,768]{1,0:T(8,128)}) custom-call(s32[4]{0:T(128)S(1)} %copy-done.21, bf16[4,240,768]{2,1,0:T(8,128)(2,1)S(1)} %get-tuple-element.84.refs_0_, bf16[4,240,768]{2,1,0:T(8,128)(2,1)S(1)} %collective-permute-done.8.refs_1_, bf16[240,768]{1,0:T(8,128)(2,1)S(1)} %collective-permute-done.10.refs_2_, ...), custom_call_target="tpu_custom_call" | custom-call | tf_op jit(solution)/shard_map/pallas_call | solution.py:708
  137.1 6.4 %collective-permute-done.15.refs_4_ = bf16[256,768]{1,0:T(8,128)(2,1)S(1)} collective-permute-done((bf16[256,768]{1,0:T(8,128)(2,1)S(1)}, bf16[256,768]{1,0:T(8,128)(2,1)S(1)}, u32[]{:S(2)}, u32[]{:S(2)}) %collective-permute-start.15) | collective-permute-done | bytes 393248 | tf_op jit(solution)/shard_map/ppermute | solution.py:758
  143.5 5.6 %collective-permute-done.14.refs_1_ = bf16[256,768]{1,0:T(8,128)(2,1)S(1)} collective-permute-done((bf16[256,768]{1,0:T(8,128)(2,1)S(1)}, bf16[256,768]{1,0:T(8,128)(2,1)S(1)}, u32[]{:S(2)}, u32[]{:S(2)}) %collective-permute-start.14) | collective-permute-done | bytes 393248 | tf_op jit(solution)/shard_map/ppermute | solution.py:758
  149.1 1.2 shard_map.262
  150.3 6.0 %collective-permute-done.21.refs_6_ = bf16[688,384]{1,0:T(8,128)(2,1)S(1)} collective-permute-done((bf16[688,384]{1,0:T(8,128)(2,1)S(1)}, bf16[688,384]{1,0:T(8,128)(2,1)S(1)}, u32[]{:S(2)}, u32[]{:S(2)}) %collective-permute-start.21) | collective-permute-done | bytes 528416 | tf_op jit(solution)/shard_map/ppermute | solution.py:780
  156.3 2.0 %shard_map.264 = (f32[96,1536]{1,0:T(8,128)}, f32[3,96,384]{2,1,0:T(8,128)}, f32[5,48]{1,0:T(8,128)S(1)}, f32[3,48]{1,0:T(4,128)S(1)}, f32[1,192]{1,0:T(1,128)}) custom-call(s32[4]{0:T(128)S(1)} %copy-done.21, bf16[4,688,384]{2,1,0:T(8,128)(2,1)S(1)} %get-tuple-element.94.refs_7_.refs_1_.refs_0_, ...), custom_call_target="tpu_custom_call" | custom-call | tf_op jit(solution)/shard_map/pallas_call | solution.py:708
  158.3 0.5 fusion.5
  158.9 0.6 copy.31
  159.4 0.5 copy.33
  (68 shorter events, 0.2 us)
Async XLA Ops:
  9.6 10.5 %collective-permute-start.2 = (bf16[128,768]{1,0:T(8,128)(2,1)}, bf16[128,768]{1,0:T(8,128)(2,1)S(1)}, u32[]{:S(2)}, u32[]{:S(2)}) collective-permute-start(bf16[128,768]{1,0:T(8,128)(2,1)} %get-tuple-element.66), channel_id=1, source_target_pairs={{0,16},{1,17},{2,18},{3,19},{4,20},{5,21},{6,22},{7,23},{8,24},{9,... | collective-permute-start | bytes 589832 | tf_op jit(solution)/shard_map/ppermute | solution.py:752
  14.5 9.8 %collective-permute-start.3 = (bf16[128,768]{1,0:T(8,128)(2,1)}, bf16[128,768]{1,0:T(8,128)(2,1)S(1)}, u32[]{:S(2)}, u32[]{:S(2)}) collective-permute-start(bf16[128,768]{1,0:T(8,128)(2,1)} %get-tuple-element.66), channel_id=1, source_target_pairs={{0,24},{8,16},{1,25},{9,17},{2,26},{10,18},{3,27},{11,19},{4,28},{... | collective-permute-start | bytes 589832 | tf_op jit(solution)/shard_map/ppermute | solution.py:754
  16.7 21.3 %collective-permute-start = (bf16[128,768]{1,0:T(8,128)(2,1)}, bf16[128,768]{1,0:T(8,128)(2,1)S(1)}, u32[]{:S(2)}, u32[]{:S(2)}) collective-permute-start(bf16[128,768]{1,0:T(8,128)(2,1)} %get-tuple-element.63), channel_id=1, source_target_pairs={{0,16},{1,17},{2,18},{3,19},{4,20},{5,21},{6,22},{7,23},{8,24},{9,... | collective-permute-start | bytes 589832 | tf_op jit(solution)/shard_map/ppermute | solution.py:752
  18.0 20.0 %collective-permute-start.1 = (bf16[128,768]{1,0:T(8,128)(2,1)}, bf16[128,768]{1,0:T(8,128)(2,1)S(1)}, u32[]{:S(2)}, u32[]{:S(2)}) collective-permute-start(bf16[128,768]{1,0:T(8,128)(2,1)} %get-tuple-element.63), channel_id=1, source_target_pairs={{0,24},{8,16},{1,25},{9,17},{2,26},{10,18},{3,27},{11,19},{4,28},{... | collective-permute-start | bytes 589832 | tf_op jit(solution)/shard_map/ppermute | solution.py:754
  20.1 4.2 %copy-start.31 = (bf16[128,768]{1,0:T(8,128)(2,1)}, bf16[128,768]{1,0:T(8,128)(2,1)S(1)}, u32[]{:S(2)}) copy-start(bf16[128,768]{1,0:T(8,128)(2,1)S(1)} %collective-permute-done.2.refs_3_) | copy-start | bytes 589828
  24.3 0.7 copy-start.32
  35.1 26.3 %copy-start.2 = (bf16[2,1,128,768]{3,2,1,0:T(8,128)(2,1)S(1)}, bf16[2,1,128,768]{3,2,1,0:T(8,128)(2,1)}, u32[]{:S(2)}) copy-start(bf16[2,1,128,768]{3,2,1,0:T(8,128)(2,1)} %param.16) | copy-start | bytes 1179652
  35.1 26.3 %copy-start.6 = (bf16[128,1536]{1,0:T(8,128)(2,1)S(1)}, bf16[128,1536]{1,0:T(8,128)(2,1)}, u32[]{:S(2)}) copy-start(bf16[128,1536]{1,0:T(8,128)(2,1)} %get-tuple-element.69.refs_7_.refs_3_) | copy-start | bytes 1179652
  35.1 26.3 %copy-start.16 = (bf16[128,384]{1,0:T(8,128)(2,1)S(1)}, bf16[128,384]{1,0:T(8,128)(2,1)}, u32[]{:S(2)}) copy-start(bf16[128,384]{1,0:T(8,128)(2,1)} %get-tuple-element.67.refs_9_.refs_1_) | copy-start | bytes 294916
  35.1 26.3 %copy-start.20 = (s32[4]{0:T(128)S(1)}, s32[4]{0:T(128)}, u32[]{:S(2)}) copy-start(s32[4]{0:T(128)} %pad_add_fusion.refs_0_.flag_ref) | copy-start | bytes 52
  35.1 17.0 %collective-permute-start.5 = (bf16[128,768]{1,0:T(8,128)(2,1)}, bf16[128,768]{1,0:T(8,128)(2,1)S(1)}, u32[]{:S(2)}, u32[]{:S(2)}) collective-permute-start(bf16[128,768]{1,0:T(8,128)(2,1)} %get-tuple-element.71), channel_id=1, source_target_pairs={{16,0},{17,1},{18,2},{19,3},{20,4},{21,5},{22,6},{23,7},{24,8},{25... | collective-permute-start | bytes 589832 | tf_op jit(solution)/shard_map/ppermute | solution.py:752
  36.5 15.6 %collective-permute-start.7 = (bf16[128,768]{1,0:T(8,128)(2,1)}, bf16[128,768]{1,0:T(8,128)(2,1)S(1)}, u32[]{:S(2)}, u32[]{:S(2)}) collective-permute-start(bf16[128,768]{1,0:T(8,128)(2,1)} %get-tuple-element.71), channel_id=1, source_target_pairs={{16,8},{24,0},{17,9},{25,1},{18,10},{26,2},{19,11},{27,3},{20,12},... | collective-permute-start | bytes 589832 | tf_op jit(solution)/shard_map/ppermute | solution.py:754
  38.0 0.7 copy-start.29
  38.7 0.7 copy-start.30
  49.5 9.8 %collective-permute-start.4 = (bf16[128,768]{1,0:T(8,128)(2,1)}, bf16[128,768]{1,0:T(8,128)(2,1)S(1)}, u32[]{:S(2)}, u32[]{:S(2)}) collective-permute-start(bf16[128,768]{1,0:T(8,128)(2,1)} %get-tuple-element.70), channel_id=1, source_target_pairs={{16,0},{17,1},{18,2},{19,3},{20,4},{21,5},{22,6},{23,7},{24,8},{25... | collective-permute-start | bytes 589832 | tf_op jit(solution)/shard_map/ppermute | solution.py:752
  50.8 10.6 %collective-permute-start.6 = (bf16[128,768]{1,0:T(8,128)(2,1)}, bf16[128,768]{1,0:T(8,128)(2,1)S(1)}, u32[]{:S(2)}, u32[]{:S(2)}) collective-permute-start(bf16[128,768]{1,0:T(8,128)(2,1)} %get-tuple-element.70), channel_id=1, source_target_pairs={{16,8},{24,0},{17,9},{25,1},{18,10},{26,2},{19,11},{27,3},{20,12},... | collective-permute-start | bytes 589832 | tf_op jit(solution)/shard_map/ppermute | solution.py:754
  52.1 19.2 %copy-start.12 = (bf16[128,768]{1,0:T(8,128)(2,1)}, bf16[128,768]{1,0:T(8,128)(2,1)S(1)}, u32[]{:S(2)}) copy-start(bf16[128,768]{1,0:T(8,128)(2,1)S(1)} %collective-permute-done.5.refs_3_.refs_9_) | copy-start | bytes 589828
  52.1 14.2 %copy-start.13 = (bf16[128,768]{1,0:T(8,128)(2,1)}, bf16[128,768]{1,0:T(8,128)(2,1)S(1)}, u32[]{:S(2)}) copy-start(bf16[128,768]{1,0:T(8,128)(2,1)S(1)} %collective-permute-done.7.refs_5_.refs_11_) | copy-start | bytes 589828
  59.3 7.0 %copy-start.14 = (bf16[128,768]{1,0:T(8,128)(2,1)}, bf16[128,768]{1,0:T(8,128)(2,1)S(1)}, u32[]{:S(2)}) copy-start(bf16[128,768]{1,0:T(8,128)(2,1)S(1)} %collective-permute-done.4.refs_2_.refs_8_) | copy-start | bytes 589828
  61.4 5.0 %copy-start.15 = (bf16[128,768]{1,0:T(8,128)(2,1)}, bf16[128,768]{1,0:T(8,128)(2,1)S(1)}, u32[]{:S(2)}) copy-start(bf16[128,768]{1,0:T(8,128)(2,1)S(1)} %collective-permute-done.6.refs_4_.refs_10_) | copy-start | bytes 589828
  61.4 1.1 copy-start.8
  62.5 0.9 copy-start.18
  66.3 3.5 %collective-permute-start.8 = (bf16[4,240,768]{2,1,0:T(8,128)(2,1)}, bf16[4,240,768]{2,1,0:T(8,128)(2,1)S(1)}, u32[]{:S(2)}, u32[]{:S(2)}) collective-permute-start(bf16[4,240,768]{2,1,0:T(8,128)(2,1)} %get-tuple-element.85), channel_id=1, source_target_pairs={{0,1},{1,0},{2,3},{3,2},{4,5},{5,4},{6,7},{7,6},{8,9},{9,8},{10,11... | collective-permute-start | bytes 4423688 | tf_op jit(solution)/shard_map/ppermute | solution.py:772
  71.3 21.6 %collective-permute-start.10 = (bf16[240,768]{1,0:T(8,128)(2,1)}, bf16[240,768]{1,0:T(8,128)(2,1)S(1)}, u32[]{:S(2)}, u32[]{:S(2)}) collective-permute-start(bf16[240,768]{1,0:T(8,128)(2,1)} %get-tuple-element.129.refs_24_), channel_id=1, source_target_pairs={{0,2},{1,3},{2,0},{3,1},{4,6},{5,7},{6,4},{7,5},{8,10},{9,11},{10,... | collective-permute-start | bytes 1105928 | tf_op jit(solution)/shard_map/ppermute | solution.py:780
  72.8 22.5 %collective-permute-start.11 = (bf16[240,768]{1,0:T(8,128)(2,1)}, bf16[240,768]{1,0:T(8,128)(2,1)S(1)}, u32[]{:S(2)}, u32[]{:S(2)}) collective-permute-start(bf16[240,768]{1,0:T(8,128)(2,1)} %get-tuple-element.126.refs_27_), channel_id=1, source_target_pairs={{0,2},{1,3},{6,4},{7,5},{8,10},{9,11},{14,12},{15,13},{16,18},{17,... | collective-permute-start | bytes 1105928 | tf_op jit(solution)/shard_map/ppermute | solution.py:780
  75.2 20.1 %collective-permute-start.12 = (bf16[240,768]{1,0:T(8,128)(2,1)}, bf16[240,768]{1,0:T(8,128)(2,1)S(1)}, u32[]{:S(2)}, u32[]{:S(2)}) collective-permute-start(bf16[240,768]{1,0:T(8,128)(2,1)} %get-tuple-element.128.refs_25_), channel_id=1, source_target_pairs={{2,4},{3,5},{4,2},{5,3},{10,12},{11,13},{12,10},{13,11},{18,20},{1... | collective-permute-start | bytes 1105928 | tf_op jit(solution)/shard_map/ppermute | solution.py:780
  75.9 21.2 %collective-permute-start.13 = (bf16[240,768]{1,0:T(8,128)(2,1)}, bf16[240,768]{1,0:T(8,128)(2,1)S(1)}, u32[]{:S(2)}, u32[]{:S(2)}) collective-permute-start(bf16[240,768]{1,0:T(8,128)(2,1)} %get-tuple-element.127.refs_26_), channel_id=1, source_target_pairs={{0,4},{1,5},{6,2},{7,3},{8,12},{9,13},{14,10},{15,11},{16,20},{17,... | collective-permute-start | bytes 1105928 | tf_op jit(solution)/shard_map/ppermute | solution.py:780
  80.8 16.3 %copy-start.24 = (bf16[128,768]{1,0:T(8,128)(2,1)S(1)}, bf16[128,768]{1,0:T(8,128)(2,1)}, u32[]{:S(2)}) copy-start(bf16[128,768]{1,0:T(8,128)(2,1)} %get-tuple-element.91.refs_6_) | copy-start | bytes 589828
  80.8 16.3 %copy-start.25 = (bf16[128,768]{1,0:T(8,128)(2,1)S(1)}, bf16[128,768]{1,0:T(8,128)(2,1)}, u32[]{:S(2)}) copy-start(bf16[128,768]{1,0:T(8,128)(2,1)} %get-tuple-element.93.refs_8_) | copy-start | bytes 589828
  80.8 16.3 %copy-start.26 = (bf16[128,768]{1,0:T(8,128)(2,1)S(1)}, bf16[128,768]{1,0:T(8,128)(2,1)}, u32[]{:S(2)}) copy-start(bf16[128,768]{1,0:T(8,128)(2,1)} %get-tuple-element.90.refs_5_) | copy-start | bytes 589828
  80.8 16.3 %copy-start.27 = (bf16[128,768]{1,0:T(8,128)(2,1)S(1)}, bf16[128,768]{1,0:T(8,128)(2,1)}, u32[]{:S(2)}) copy-start(bf16[128,768]{1,0:T(8,128)(2,1)} %get-tuple-element.92.refs_7_) | copy-start | bytes 589828
  91.3 5.8 %copy-start.21 = (s32[4]{0:T(128)S(1)}, s32[4]{0:T(128)}, u32[]{:S(2)}) copy-start(s32[4]{0:T(128)} %pad_add_fusion.refs_0_.flag_ref) | copy-start | bytes 52
  91.3 5.8 %copy-start.22 = (bf16[256,1536]{1,0:T(8,128)(2,1)S(1)}, bf16[256,1536]{1,0:T(8,128)(2,1)}, u32[]{:S(2)}) copy-start(bf16[256,1536]{1,0:T(8,128)(2,1)} %get-tuple-element.86.refs_1_) | copy-start | bytes 2359300
  91.3 5.8 %copy-start.23 = (bf16[256,1152]{1,0:T(8,128)(2,1)S(1)}, bf16[256,1152]{1,0:T(8,128)(2,1)}, u32[]{:S(2)}) copy-start(bf16[256,1152]{1,0:T(8,128)(2,1)} %get-tuple-element.87.refs_2_) | copy-start | bytes 1769476
  91.3 5.8 %copy-start.28 = (f32[16,384]{1,0:T(8,128)S(1)}, f32[16,384]{1,0:T(8,128)}, u32[]{:S(2)}) copy-start(f32[16,384]{1,0:T(8,128)} %get-tuple-element.88.refs_3_) | copy-start | bytes 73732
  91.3 4.0 %collective-permute-start.9 = (f32[8,384]{1,0:T(8,128)}, f32[8,384]{1,0:T(8,128)S(1)}, u32[]{:S(2)}, u32[]{:S(2)}) collective-permute-start(f32[8,384]{1,0:T(8,128)} %get-tuple-element.89), channel_id=1, source_target_pairs={{0,8},{8,0},{1,9},{9,1},{2,10},{10,2},{3,11},{11,3},{4,12},{12,4},... | collective-permute-start | bytes 36872 | tf_op jit(solution)/shard_map/ppermute | solution.py:758
  99.3 4.2 %collective-permute-start.16 = (bf16[4,688,384]{2,1,0:T(8,128)(2,1)S(1)}, bf16[4,688,384]{2,1,0:T(8,128)(2,1)S(1)}, u32[]{:S(2)}, u32[]{:S(2)}) collective-permute-start(bf16[4,688,384]{2,1,0:T(8,128)(2,1)S(1)} %get-tuple-element.97), channel_id=1, source_target_pairs={{0,1},{1,0},{2,3},{3,2},{4,5},{5,4},{6,7},{7,6},{8,9},{9,8},{10,11... | collective-permute-start | bytes 6340616 | tf_op jit(solution)/shard_map/ppermute | solution.py:772
  104.6 15.8 %collective-permute-start.17 = (bf16[688,384]{1,0:T(8,128)(2,1)S(1)}, bf16[688,384]{1,0:T(8,128)(2,1)S(1)}, u32[]{:S(2)}, u32[]{:S(2)}) collective-permute-start(bf16[688,384]{1,0:T(8,128)(2,1)S(1)} %get-tuple-element.98), channel_id=1, source_target_pairs={{0,2},{1,3},{2,0},{3,1},{4,6},{5,7},{6,4},{7,5},{8,10},{9,11},{10,... | collective-permute-start | bytes 1585160 | tf_op jit(solution)/shard_map/ppermute | solution.py:780
  108.2 23.2 %copy-start.10 = (bf16[256,768]{1,0:T(8,128)(2,1)S(1)}, bf16[256,768]{1,0:T(8,128)(2,1)}, u32[]{:S(2)}) copy-start(bf16[256,768]{1,0:T(8,128)(2,1)} %get-tuple-element.96.refs_3_) | copy-start | bytes 1179652
  108.2 24.7 %copy-start = (bf16[1,1536,768]{2,1,0:T(8,128)(2,1)S(1)}, bf16[1,1536,768]{2,1,0:T(8,128)(2,1)}, u32[]{:S(2)}) copy-start(bf16[1,1536,768]{2,1,0:T(8,128)(2,1)} %param.27) | copy-start | bytes 7077892
  108.2 24.7 %copy-start.1 = (bf16[1,384,768]{2,1,0:T(8,128)(2,1)S(1)}, bf16[1,384,768]{2,1,0:T(8,128)(2,1)}, u32[]{:S(2)}) copy-start(bf16[1,384,768]{2,1,0:T(8,128)(2,1)} %param.23) | copy-start | bytes 1769476
  108.2 24.7 %copy-start.3 = (f32[16,1536]{1,0:T(8,128)S(1)}, f32[16,1536]{1,0:T(8,128)}, u32[]{:S(2)}) copy-start(f32[16,1536]{1,0:T(8,128)} %get-tuple-element.64.refs_6_.refs_3_.refs_4_) | copy-start | bytes 294916
  108.2 24.7 %copy-start.7 = (bf16[128,1536]{1,0:T(8,128)(2,1)S(1)}, bf16[128,1536]{1,0:T(8,128)(2,1)}, u32[]{:S(2)}) copy-start(bf16[128,1536]{1,0:T(8,128)(2,1)} %get-tuple-element.69.refs_7_.refs_3_) | copy-start | bytes 1179652
  108.2 24.7 %copy-start.9 = (bf16[128,1536]{1,0:T(8,128)(2,1)S(1)}, bf16[128,1536]{1,0:T(8,128)(2,1)}, u32[]{:S(2)}) copy-start(bf16[128,1536]{1,0:T(8,128)(2,1)} %get-tuple-element.68.refs_6_.refs_2_) | copy-start | bytes 1179652
  108.2 24.7 %copy-start.17 = (bf16[128,384]{1,0:T(8,128)(2,1)S(1)}, bf16[128,384]{1,0:T(8,128)(2,1)}, u32[]{:S(2)}) copy-start(bf16[128,384]{1,0:T(8,128)(2,1)} %get-tuple-element.67.refs_9_.refs_1_) | copy-start | bytes 294916
  108.2 24.7 %copy-start.19 = (bf16[128,384]{1,0:T(8,128)(2,1)S(1)}, bf16[128,384]{1,0:T(8,128)(2,1)}, u32[]{:S(2)}) copy-start(bf16[128,384]{1,0:T(8,128)(2,1)} %get-tuple-element.65.refs_8_.refs_0_) | copy-start | bytes 294916
  108.2 12.3 %collective-permute-start.18 = (bf16[688,384]{1,0:T(8,128)(2,1)S(1)}, bf16[688,384]{1,0:T(8,128)(2,1)S(1)}, u32[]{:S(2)}, u32[]{:S(2)}) collective-permute-start(bf16[688,384]{1,0:T(8,128)(2,1)S(1)} %get-tuple-element.101), channel_id=1, source_target_pairs={{2,4},{3,5},{4,2},{5,3},{10,12},{11,13},{12,10},{13,11},{18,20},{1... | collective-permute-start | bytes 1585160 | tf_op jit(solution)/shard_map/ppermute | solution.py:780
  109.0 25.4 %collective-permute-start.22 = (bf16[240,768]{1,0:T(8,128)(2,1)S(1)}, bf16[240,768]{1,0:T(8,128)(2,1)S(1)}, u32[]{:S(2)}, u32[]{:S(2)}) collective-permute-start(bf16[240,768]{1,0:T(8,128)(2,1)S(1)} %fusion.refs_9_), channel_id=1, source_target_pairs={{2,6},{3,7},{4,0},{5,1},{10,14},{11,15},{12,8},{13,9},{18,22},{19,... | collective-permute-start | bytes 1105928 | tf_op jit(solution)/shard_map/ppermute | solution.py:780
  122.0 28.3 %collective-permute-start.19 = (bf16[688,384]{1,0:T(8,128)(2,1)S(1)}, bf16[688,384]{1,0:T(8,128)(2,1)S(1)}, u32[]{:S(2)}, u32[]{:S(2)}) collective-permute-start(bf16[688,384]{1,0:T(8,128)(2,1)S(1)} %get-tuple-element.102), channel_id=1, source_target_pairs={{0,2},{1,3},{6,4},{7,5},{8,10},{9,11},{14,12},{15,13},{16,18},{17,... | collective-permute-start | bytes 1585160 | tf_op jit(solution)/shard_map/ppermute | solution.py:780
  128.7 21.6 %collective-permute-start.20 = (bf16[688,384]{1,0:T(8,128)(2,1)S(1)}, bf16[688,384]{1,0:T(8,128)(2,1)S(1)}, u32[]{:S(2)}, u32[]{:S(2)}) collective-permute-start(bf16[688,384]{1,0:T(8,128)(2,1)S(1)} %get-tuple-element.103), channel_id=1, source_target_pairs={{0,4},{1,5},{6,2},{7,3},{8,12},{9,13},{14,10},{15,11},{16,20},{17,... | collective-permute-start | bytes 1585160 | tf_op jit(solution)/shard_map/ppermute | solution.py:780
  130.0 26.3 %collective-permute-start.21 = (bf16[688,384]{1,0:T(8,128)(2,1)S(1)}, bf16[688,384]{1,0:T(8,128)(2,1)S(1)}, u32[]{:S(2)}, u32[]{:S(2)}) collective-permute-start(bf16[688,384]{1,0:T(8,128)(2,1)S(1)} %get-tuple-element.104), channel_id=1, source_target_pairs={{2,6},{3,7},{4,0},{5,1},{10,14},{11,15},{12,8},{13,9},{18,22},{19,... | collective-permute-start | bytes 1585160 | tf_op jit(solution)/shard_map/ppermute | solution.py:780
  131.3 12.1 %collective-permute-start.15 = (bf16[256,768]{1,0:T(8,128)(2,1)S(1)}, bf16[256,768]{1,0:T(8,128)(2,1)S(1)}, u32[]{:S(2)}, u32[]{:S(2)}) collective-permute-start(bf16[256,768]{1,0:T(8,128)(2,1)S(1)} %copy-done.10), channel_id=1, source_target_pairs={{0,8},{8,0},{1,9},{9,1},{2,10},{10,2},{3,11},{11,3},{4,12},{12,4},... | collective-permute-start | bytes 1179656 | tf_op jit(solution)/shard_map/ppermute | solution.py:758
  134.4 14.7 %copy-start.4 = (bf16[128,768]{1,0:T(8,128)(2,1)S(1)}, bf16[128,768]{1,0:T(8,128)(2,1)}, u32[]{:S(2)}) copy-start(bf16[128,768]{1,0:T(8,128)(2,1)} %get-tuple-element.73.refs_13_.refs_6_) | copy-start | bytes 589828
  134.4 14.7 %copy-start.5 = (bf16[128,768]{1,0:T(8,128)(2,1)S(1)}, bf16[128,768]{1,0:T(8,128)(2,1)}, u32[]{:S(2)}) copy-start(bf16[128,768]{1,0:T(8,128)(2,1)} %get-tuple-element.72.refs_12_.refs_5_) | copy-start | bytes 589828
  134.4 14.7 %copy-start.11 = (bf16[256,768]{1,0:T(8,128)(2,1)S(1)}, bf16[256,768]{1,0:T(8,128)(2,1)}, u32[]{:S(2)}) copy-start(bf16[256,768]{1,0:T(8,128)(2,1)} %get-tuple-element.95.refs_2_) | copy-start | bytes 1179652
  134.4 14.6 %collective-permute-start.14 = (bf16[256,768]{1,0:T(8,128)(2,1)S(1)}, bf16[256,768]{1,0:T(8,128)(2,1)S(1)}, u32[]{:S(2)}, u32[]{:S(2)}) collective-permute-start(bf16[256,768]{1,0:T(8,128)(2,1)S(1)} %shard_map.260.refs_0_), channel_id=1, source_target_pairs={{0,8},{8,0},{1,9},{9,1},{2,10},{10,2},{3,11},{11,3},{4,12},{12,4},... | collective-permute-start | bytes 1179656 | tf_op jit(solution)/shard_map/ppermute | solution.py:758
  158.9 1.1 copy-start.33
